TPU v7x, 128 devices: a whole 4x4x4 slice. The times are simulated.
128 devices in a mesh: pipe: 2 (over core), shard: 64 (over y, x, z).
Axes of the slice: x: 4, y: 4, z: 4, core: 2. Of those that a mesh axis runs over, the one named last changes fastest.
Arguments:
- latents: bfloat16 [2, 128, 256, 384], P(None, 'shard'), may hold values from -6 to 6
- conditions: bfloat16 [2, 128, 384], P(None, 'shard'), may hold values from -6 to 6
- cotangent: bfloat16 [2, 128, 256, 384], P(None, 'shard'), may hold values from -6 to 6
- w_qkv: bfloat16 [2, 384, 1152], P('pipe', 'shard'), may hold values from -0.3125 to 0.3125
- b_qv: bfloat16 [2, 768], P('pipe', 'shard'), may hold values from -3 to 3
- w_proj: bfloat16 [2, 384, 384], P('pipe', 'shard'), may hold values from -0.875 to 0.875
- b_proj: bfloat16 [2, 384], P('pipe', 'shard'), may hold values from -3 to 3
- w_fc1: bfloat16 [2, 384, 1536], P('pipe', 'shard'), may hold values from -0.3125 to 0.3125
- b_fc1: bfloat16 [2, 1536], P('pipe', 'shard'), may hold values from -3 to 3
- w_fc2: bfloat16 [2, 1536, 384], P('pipe', 'shard'), may hold values from -0.21875 to 0.21875
- b_fc2: bfloat16 [2, 384], P('pipe', 'shard'), may hold values from -3 to 3
- w_ada: bfloat16 [2, 384, 2304], P('pipe', 'shard'), may hold values from -0.4375 to 0.4375
- b_ada: bfloat16 [2, 2304], P('pipe', 'shard'), may hold values from -3 to 3
Outputs:
- section_outputs: bfloat16 [2, 2, 128, 256, 384], P('pipe', None, 'shard')
- input_grads: bfloat16 [2, 2, 128, 256, 384], P('pipe', None, 'shard')
- cond_grad: float32 [2, 128, 384], P(None, 'shard')
- grad_w_qkv: float32 [2, 384, 1152], P('pipe', 'shard')
- grad_b_qv: float32 [2, 768], P('pipe', 'shard')
- grad_w_proj: float32 [2, 384, 384], P('pipe', 'shard')
- grad_b_proj: float32 [2, 384], P('pipe', 'shard')
- grad_w_fc1: float32 [2, 384, 1536], P('pipe', 'shard')
- grad_b_fc1: float32 [2, 1536], P('pipe', 'shard')
- grad_w_fc2: float32 [2, 1536, 384], P('pipe', 'shard')
- grad_b_fc2: float32 [2, 384], P('pipe', 'shard')
- grad_w_ada: float32 [2, 384, 2304], P('pipe', 'shard')
- grad_b_ada: float32 [2, 2304], P('pipe', 'shard')
All inputs are finite; a program needn't handle non-finite values.
Results may differ from a plain program's by a relative error of at most 0.018.
The roundings to bfloat16 on the way count: a program that leaves them out, or rounds other values in their place, can miss the bound.
Values may be sent and summed in bfloat16 or wider, within the bound.
No kernel may reach another device: no remote copies, remote signals or barrier semaphores. Data moves between devices by JAX's collectives and lax.ppermute only.
A program may use at most 192 MiB of HBM per device.

v0:
```python
import jax
import jax.numpy as jnp
from jax import lax
from jax.sharding import PartitionSpec as P

HEADS = 6
HEAD = 64


EPSILON = 1e-06
FLOAT = jnp.float32
BRAIN = jnp.bfloat16


def split_up(x, dim, length):
    lengths = x.shape
    tiles = x.reshape(*lengths[:dim], length, lengths[dim] // length, *lengths[dim + 1 :])
    return jnp.moveaxis(tiles, dim, 0)


def sum_packed(arrays, axis, dims):
    length = lax.axis_size(axis)
    tiles = [split_up(a, dim, length) for a, dim in zip(arrays, dims)]
    lines = jnp.concatenate([b.reshape(length, -1) for b in tiles], axis=1)
    span = max(16, -(-lines.shape[1] // 1024) * 8)
    lines = jnp.pad(lines, ((0, 0), (0, span * 128 - lines.shape[1]))).reshape(-1, 128)
    line, at, finished = (lax.psum_scatter(lines, axis, tiled=True).reshape(-1), 0, [])
    for b in tiles:
        part = b[0]
        finished.append(line[at : at + part.size].reshape(part.shape))
        at += part.size
    return tuple(finished)


def joined_along(tiles, dim):
    lengths = list(tiles.shape[1:])
    lengths[dim] *= tiles.shape[0]
    return jnp.moveaxis(tiles, 0, dim).reshape(lengths)


def gather_packed(arrays, axis, dims):
    line = jnp.concatenate([a.reshape(-1) for a in arrays])
    lines, at, finished = (lax.all_gather(line, axis), 0, [])
    for a, dim in zip(arrays, dims):
        tiles = lines[:, at : at + a.size].reshape(-1, *a.shape)
        finished.append(joined_along(tiles, dim))
        at += a.size
    return tuple(finished)


def passed_along(x, axis, by):
    length = lax.axis_size(axis)
    pairs = [(i, i + by) for i in range(length) if 0 <= i + by < length]
    return lax.ppermute(x, axis, pairs)


def copy_for_each(x, axis):
    copies = jnp.broadcast_to(x, (lax.axis_size(axis), *x.shape))
    return lax.all_to_all(copies, axis, split_axis=0, concat_axis=0, tiled=True)


def taken_together(x, axis):
    return copy_for_each(x, axis).sum(axis=0)


def norm_rows(values):
    centre = values - jnp.mean(values, axis=-1, keepdims=True)
    spread = jnp.mean(centre * centre, axis=-1, keepdims=True)
    return centre * jax.lax.rsqrt(spread + EPSILON)


def gelu_tanh(values):
    return jax.nn.gelu(values, approximate=True)


def linear(inputs, weight):
    return jnp.einsum("lsd,de->lse", inputs, weight, preferred_element_type=FLOAT)


def weight_grad(inputs, gradients):
    return jnp.einsum("lsd,lse->de", inputs, gradients, preferred_element_type=FLOAT)


def back_linear(gradients, weight):
    return jnp.einsum("lse,de->lsd", gradients, weight, preferred_element_type=FLOAT)


def split_heads(qkv_all):
    latent_count, length, triple = qkv_all.shape
    return [
        portion.reshape(latent_count, length, HEADS, HEAD)
        for portion in jnp.split(qkv_all, 3, axis=-1)
    ]


def forward_block(section_input, conditions, weights):
    w_qkv, b_qv, w_proj, b_proj, w_fc1, b_fc1, w_fc2, b_fc2, w_ada, b_ada = weights
    latent_count, length, features = section_input.shape
    hidden_state = section_input.astype(FLOAT)
    cond_act = jax.nn.silu(conditions.astype(FLOAT)).astype(BRAIN)
    modulation = jnp.dot(cond_act, w_ada, preferred_element_type=FLOAT) + b_ada.astype(FLOAT)
    shift_one, scale_one, gate_one, shift_two, scale_two, gate_two = jnp.split(
        modulation[:, None, :], 6, axis=-1
    )
    attn_in = (norm_rows(hidden_state) * (1.0 + scale_one) + shift_one).astype(BRAIN)
    qkv_bias = jnp.concatenate(
        [b_qv[:features], jnp.zeros((features,), BRAIN), b_qv[features:]]
    ).astype(FLOAT)
    qkv_all = (linear(attn_in, w_qkv) + qkv_bias).astype(BRAIN)
    queries, keys_all, values_all = split_heads(qkv_all)
    scores = jnp.einsum(
        "lqhe,lkhe->lhqk", queries, keys_all, preferred_element_type=FLOAT
    ) * HEAD ** (-0.5)
    row_top = jnp.max(scores, axis=-1, keepdims=True)
    shifted = jnp.exp(scores - row_top)
    row_total = jnp.sum(shifted, axis=-1, keepdims=True)
    log_total = row_top + jnp.log(row_total)
    probabilities = (shifted / row_total).astype(BRAIN)
    attended = jnp.einsum(
        "lhqk,lkhe->lqhe", probabilities, values_all, preferred_element_type=FLOAT
    )
    attended = attended.reshape(latent_count, length, features).astype(BRAIN)
    branch_attn = linear(attended, w_proj) + b_proj.astype(FLOAT)
    middle = hidden_state + gate_one * branch_attn
    mlp_in = (norm_rows(middle) * (1.0 + scale_two) + shift_two).astype(BRAIN)
    pre_act = linear(mlp_in, w_fc1) + b_fc1.astype(FLOAT)
    activated = gelu_tanh(pre_act).astype(BRAIN)
    branch_mlp = linear(activated, w_fc2) + b_fc2.astype(FLOAT)
    emitted_rows = middle + gate_two * branch_mlp
    stored = (
        hidden_state,
        conditions,
        cond_act,
        modulation,
        attn_in,
        queries,
        keys_all,
        values_all,
        log_total,
        attended,
        branch_attn,
        middle,
        mlp_in,
        pre_act,
        activated,
        branch_mlp,
    )
    return (emitted_rows.astype(BRAIN), stored)


def backward_block(grad_out, stored, weights):
    w_qkv, b_qv, w_proj, b_proj, w_fc1, b_fc1, w_fc2, b_fc2, w_ada, b_ada = weights
    (
        hidden_state,
        conditions,
        cond_act,
        modulation,
        attn_in,
        queries,
        keys_all,
        values_all,
        log_total,
        attended,
        branch_attn,
        middle,
        mlp_in,
        pre_act,
        activated,
        branch_mlp,
    ) = stored
    latent_count, length, features = hidden_state.shape
    scale_factor = HEAD ** (-0.5)
    grad_final = grad_out.astype(FLOAT)
    shift_one, scale_one, gate_one, shift_two, scale_two, gate_two = jnp.split(
        modulation[:, None, :], 6, axis=-1
    )
    grad_mlp = (grad_final * gate_two).astype(BRAIN)
    grad_gate_two = jnp.sum(grad_final * branch_mlp, axis=1)
    grad_w_fc2 = weight_grad(activated, grad_mlp)
    grad_b_fc2 = jnp.sum(grad_mlp.astype(FLOAT), axis=(0, 1))
    grad_act = back_linear(grad_mlp, w_fc2)
    unused_gelu, gelu_pull = jax.vjp(gelu_tanh, pre_act)
    grad_pre = gelu_pull(grad_act)[0].astype(BRAIN)
    grad_w_fc1 = weight_grad(mlp_in, grad_pre)
    grad_b_fc1 = jnp.sum(grad_pre.astype(FLOAT), axis=(0, 1))
    grad_mlp_in = back_linear(grad_pre, w_fc1)
    normed_mid, norm_pull_mid = jax.vjp(norm_rows, middle)
    grad_scale_two = jnp.sum(grad_mlp_in * normed_mid, axis=1)
    grad_shift_two = jnp.sum(grad_mlp_in, axis=1)
    grad_middle = grad_final + norm_pull_mid(grad_mlp_in * (1.0 + scale_two))[0]
    grad_branch = (grad_middle * gate_one).astype(BRAIN)
    grad_gate_one = jnp.sum(grad_middle * branch_attn, axis=1)
    grad_w_proj = weight_grad(attended, grad_branch)
    grad_b_proj = jnp.sum(grad_branch.astype(FLOAT), axis=(0, 1))
    grad_att = (
        back_linear(grad_branch, w_proj).astype(BRAIN).reshape(latent_count, length, HEADS, HEAD)
    )
    scores = (
        jnp.einsum("lqhe,lkhe->lhqk", queries, keys_all, preferred_element_type=FLOAT)
        * scale_factor
    )
    prob_exact = jnp.exp(scores - log_total)
    grad_values = jnp.einsum(
        "lhqk,lqhe->lkhe", prob_exact.astype(BRAIN), grad_att, preferred_element_type=FLOAT
    )
    grad_probs = jnp.einsum("lqhe,lkhe->lhqk", grad_att, values_all, preferred_element_type=FLOAT)
    grad_scores = prob_exact * (
        grad_probs - jnp.sum(prob_exact * grad_probs, axis=-1, keepdims=True)
    )
    grad_scores = grad_scores.astype(BRAIN)
    grad_queries = (
        jnp.einsum("lhqk,lkhe->lqhe", grad_scores, keys_all, preferred_element_type=FLOAT)
        * scale_factor
    )
    grad_keys = (
        jnp.einsum("lhqk,lqhe->lkhe", grad_scores, queries, preferred_element_type=FLOAT)
        * scale_factor
    )
    grad_qkv = jnp.concatenate(
        [
            portion.reshape(latent_count, length, features)
            for portion in (grad_queries, grad_keys, grad_values)
        ],
        axis=-1,
    ).astype(BRAIN)
    grad_w_qkv = weight_grad(attn_in, grad_qkv)
    grad_qkv_total = jnp.sum(grad_qkv.astype(FLOAT), axis=(0, 1))
    grad_b_qv = jnp.concatenate([grad_qkv_total[:features], grad_qkv_total[2 * features :]])
    grad_attn_in = back_linear(grad_qkv, w_qkv)
    normed_in, norm_pull_in = jax.vjp(norm_rows, hidden_state)
    grad_scale_one = jnp.sum(grad_attn_in * normed_in, axis=1)
    grad_shift_one = jnp.sum(grad_attn_in, axis=1)
    grad_hidden = grad_middle + norm_pull_in(grad_attn_in * (1.0 + scale_one))[0]
    grad_mod = jnp.concatenate(
        [
            grad_shift_one,
            grad_scale_one,
            grad_gate_one,
            grad_shift_two,
            grad_scale_two,
            grad_gate_two,
        ],
        axis=-1,
    ).astype(BRAIN)
    grad_w_ada = jnp.dot(cond_act.T, grad_mod, preferred_element_type=FLOAT)
    grad_b_ada = jnp.sum(grad_mod.astype(FLOAT), axis=0)
    grad_cond_act = jnp.dot(grad_mod, w_ada.T, preferred_element_type=FLOAT)
    unused_silu, silu_pull = jax.vjp(jax.nn.silu, conditions.astype(FLOAT))
    grad_cond = silu_pull(grad_cond_act)[0]
    gradients = (
        grad_w_qkv,
        grad_b_qv,
        grad_w_proj,
        grad_b_proj,
        grad_w_fc1,
        grad_b_fc1,
        grad_w_fc2,
        grad_b_fc2,
        grad_w_ada,
        grad_b_ada,
    )
    return (grad_hidden.astype(BRAIN), grad_cond, gradients)


def reduce_end(gradients):
    return sum_packed(
        (
            gradients[0],
            gradients[1],
            gradients[2],
            gradients[3],
            gradients[4],
            gradients[5],
            gradients[6],
            gradients[7],
            gradients[8],
            gradients[9],
        ),
        "shard",
        (0, 0, 0, 0, 0, 0, 0, 0, 0, 0),
    )


def add_tuples(former, latter):
    return tuple((left + right for left, right in zip(former, latter)))


def shards(
    latents,
    conditions,
    cotangent,
    w_qkv,
    b_qv,
    w_proj,
    b_proj,
    w_fc1,
    b_fc1,
    w_fc2,
    b_fc2,
    w_ada,
    b_ada,
):
    is_first = lax.axis_index("pipe") == 0
    micro_count = latents.shape[0]
    weights = gather_packed(
        (
            w_qkv[0],
            b_qv[0],
            w_proj[0],
            b_proj[0],
            w_fc1[0],
            b_fc1[0],
            w_fc2[0],
            b_fc2[0],
            w_ada[0],
            b_ada[0],
        ),
        "shard",
        (0, 0, 0, 0, 0, 0, 0, 0, 0, 0),
    )
    incoming = jnp.zeros_like(latents[0])
    results = []
    records = []
    for section_turn in range(micro_count + 1):
        section_input = jnp.where(is_first, latents[min(section_turn, micro_count - 1)], incoming)
        cond_now = jnp.where(
            is_first,
            conditions[min(section_turn, micro_count - 1)],
            conditions[max(section_turn - 1, 0)],
        )
        result, stored = forward_block(section_input, cond_now, weights)
        results.append(result)
        records.append(stored)
        if section_turn < micro_count:
            incoming = passed_along(result, "pipe", 1)
    outgoing = jnp.zeros_like(latents[0])
    totals = None
    input_list = []
    cond_list = []
    for section_turn in range(micro_count + 1):
        record = jax.tree.map(
            lambda former, latter: jnp.where(is_first, former, latter),
            records[max(section_turn - 1, 0)],
            records[min(section_turn + 1, micro_count)],
        )
        grad_out = jnp.where(is_first, outgoing, cotangent[min(section_turn, micro_count - 1)])
        grad_in, grad_cond, gradients = backward_block(grad_out, record, weights)
        active = jnp.where(is_first, float(section_turn >= 1), float(section_turn < micro_count))
        gradients = tuple((active * member for member in gradients))
        totals = gradients if totals is None else add_tuples(totals, gradients)
        input_list.append(grad_in)
        cond_list.append(grad_cond)
        if section_turn < micro_count:
            outgoing = passed_along(grad_in, "pipe", -1)
    totals = reduce_end(totals)
    section_outputs = jnp.stack(
        [
            jnp.where(is_first, results[position], results[position + 1])
            for position in range(micro_count)
        ]
    )[None]
    input_grads = jnp.stack(
        [
            jnp.where(is_first, input_list[position + 1], input_list[position])
            for position in range(micro_count)
        ]
    )[None]
    cond_local = jnp.stack(
        [
            jnp.where(is_first, cond_list[position + 1], cond_list[position])
            for position in range(micro_count)
        ]
    )
    cond_grad = taken_together(cond_local, "pipe")
    return (section_outputs, input_grads, cond_grad) + tuple((member[None] for member in totals))


def solution(mesh):
    placed = (
        P(None, "shard", None, None),
        P(None, "shard", None),
        P(None, "shard", None, None),
        P("pipe", "shard", None),
        P("pipe", "shard"),
        P("pipe", "shard", None),
        P("pipe", "shard"),
        P("pipe", "shard", None),
        P("pipe", "shard"),
        P("pipe", "shard", None),
        P("pipe", "shard"),
        P("pipe", "shard", None),
        P("pipe", "shard"),
    )
    return jax.shard_map(
        shards,
        mesh=mesh,
        in_specs=placed,
        out_specs=(
            P("pipe", None, "shard", None, None),
            P("pipe", None, "shard", None, None),
            P(None, "shard", None),
            P("pipe", "shard", None),
            P("pipe", "shard"),
            P("pipe", "shard", None),
            P("pipe", "shard"),
            P("pipe", "shard", None),
            P("pipe", "shard"),
            P("pipe", "shard", None),
            P("pipe", "shard"),
            P("pipe", "shard", None),
            P("pipe", "shard"),
        ),
        check_vma=False,
    )
```

profile of v0, /device:TPU:1, one launch (start us, length us, event | category | flops | bytes accessed | tf_op | source)
XLA Modules:
  0.0 710.3 jit_solution(5774132255212726233)
XLA Ops:
  13.1 3.5 concatenate.69
  22.8 144.6 %all-reduce.6.cloned.1.call-done = bf16[2659584]{0:T(1024)(128)(2,1)} async-done(((bf16[2659584]{0:T(1024)(128)(2,1)}), bf16[2659584]{0:T(1024)(128)(2,1)}) %all-reduce.6.cloned.1.call-update) | async-done | bytes 5319184
  167.4 13.0 %reshape.575 = bf16[64,41556]{1,0:T(8,128)(2,1)} reshape(bf16[2659584]{0:T(1024)(128)(2,1)} %all-reduce.6.cloned.1.call-done) | data formatting | bytes 10638336 | tf_op jit(solution)/shard_map/all_gather | solution.py:43
  180.3 3.4 slice.190
  189.9 3.9 reshape_reshape.30
  253.2 3.5 convert_reduce_fusion.2
  274.5 7.0 fusion.51
  305.7 3.3 broadcast_select_fusion
  325.4 3.5 convert_reduce_fusion.1
  336.6 3.5 fusion.94
  373.7 7.9 %fusion.60 = f32[1536,384]{1,0:T(8,128)} fusion(f32[1536,384]{1,0:T(8,128)} %fusion.51, pred[]{:T(512)S(6)} %eq.3, bf16[2,256,384]{2,1,0:T(8,128)(2,1)} %copy-done.71, f32[2,384]{1,0:T(2,128)} %get-tuple-element.163, f32[2,256,1536]{2,1,0:T(8,128)} %copy-done.92, f32[2,256,1536]{2,1,0:T(8,128)} %copy-done.89), kind=kOutput, calls=%fused_computation.111 | convolution fusion | flops 620101632 | bytes 11406337 | tf_op jit(solution)/shard_map/lsd,lse->de/dot_general | solution.py:81
  387.7 3.5 convert_reduce_fusion
  394.7 3.9 convert_reduce_fusion.11
  425.8 3.8 fusion.53
  432.2 7.8 %fusion.50 = f32[1536,384]{1,0:T(8,128)} fusion(f32[1536,384]{1,0:T(8,128)} %fusion.60, pred[]{:T(512)S(6)} %eq.3, f32[]{:T(128)S(6)} %select_n.390, bf16[2,256,384]{2,1,0:T(8,128)(2,1)} %copy-done.108, f32[2,384]{1,0:T(2,128)S(1)} %copy-done.184, f32[2,256,1536]{2,1,0:T(8,128)} %copy-done.92, f32[2,256,1536]{2,1,0:T(8,128)} %copy-done.87), kind=kOutput, calls=%fused_computation.90 | convolution fusion | flops 620691456 | bytes 11406341 | tf_op jit(solution)/shard_map/lsd,lse->de/dot_general | solution.py:81
  449.1 4.7 reshape_reshape.39
  455.4 3.9 dynamic-update-slice.3
  460.9 11.5 %dynamic-update-slice.5 = f32[64,41556]{1,0:T(8,128)} dynamic-update-slice(f32[64,41556]{1,0:T(8,128)} %dynamic-update-slice.4, f32[64,9216]{1,0:T(8,128)S(1)} %reshape_reshape.37, s32[]{} %constant.110, s32[]{} %constant.114) | dynamic-update-slice | bytes 4718596
  474.0 12.1 %dynamic-update-slice.7 = f32[64,41556]{1,0:T(8,128)} dynamic-update-slice(f32[64,41556]{1,0:T(8,128)} %dynamic-update-slice.6, f32[64,9216]{1,0:T(8,128)} %reshape_reshape.38, s32[]{} %constant.110, s32[]{} %constant.116) | dynamic-update-slice | bytes 4718596
  487.6 12.1 %dynamic-update-slice.9 = f32[64,41556]{1,0:T(8,128)} dynamic-update-slice(f32[64,41556]{1,0:T(8,128)} %dynamic-update-slice.8, f32[64,13824]{1,0:T(8,128)} %reshape_reshape.39, s32[]{} %constant.110, s32[]{} %constant.118) | dynamic-update-slice | bytes 7077892
  501.2 8.9 %pad.4 = f32[64,41984]{1,0:T(8,128)} pad(f32[64,41556]{1,0:T(8,128)} %dynamic-update-slice.10, f32[]{:T(128)} %constant.74.clone.1), padding=0_0x0_428 | pad | bytes 21386244 | tf_op jit(solution)/shard_map/jit(_pad)/pad | solution.py:26
  510.0 10.6 %reshape.568 = f32[20992,128]{1,0:T(8,128)} reshape(f32[64,41984]{1,0:T(8,128)} %pad.4) | data formatting | bytes 21495808 | tf_op jit(solution)/shard_map/reshape | solution.py:26
  524.0 3.5 all_to_all.5
  532.6 163.3 %all-reduce.8.cloned.1.call-done = f32[20992,128]{1,0:T(8,128)} async-done(((f32[20992,128]{1,0:T(8,128)}), f32[20992,128]{1,0:T(8,128)}) %all-reduce.8.cloned.1.call-update) | async-done | bytes 10747920
  (809 shorter events, 244.7 us)
Async XLA Ops:
  7.2 160.2 %all-reduce.6.cloned.1.call-start = ((), (), s32[]{:S(2)}) async-start(), calls=%async_computation.1 | async-start | bytes 10641408
  21.7 674.2 %all-reduce.8.cloned.1.call-start = ((), (), s32[]{:S(2)}) async-start(), calls=%async_computation.2 | async-start | bytes 21495808
  21.9 178.0 %copy-start.197 = (f32[2,256]{1,0:T(2,128)}, f32[2,256]{1,0:T(2,128)S(1)}, u32[]{:S(2)}) copy-start(f32[2,256]{1,0:T(2,128)S(1)} %broadcast_multiply_fusion.11) | copy-start | bytes 6148
  196.5 13.9 %copy-start.153 = (f32[384]{0:T(512)}, f32[384]{0:T(512)S(1)}, u32[]{:S(2)}) copy-start(f32[384]{0:T(512)S(1)} %reshape.571) | copy-start | bytes 4612
  206.9 9.7 %copy-start.241 = (f32[384]{0:T(512)}, f32[384]{0:T(512)S(1)}, u32[]{:S(2)}) copy-start(f32[384]{0:T(512)S(1)} %reshape.573) | copy-start | bytes 4612
  215.3 8.8 %copy-start.224 = (f32[2,384]{1,0:T(2,128)}, f32[2,384]{1,0:T(2,128)S(1)}, u32[]{:S(2)}) copy-start(f32[2,384]{1,0:T(2,128)S(1)} %get-tuple-element.177) | copy-start | bytes 9220
  215.3 8.8 %copy-start.226 = (f32[2,384]{1,0:T(2,128)}, f32[2,384]{1,0:T(2,128)S(1)}, u32[]{:S(2)}) copy-start(f32[2,384]{1,0:T(2,128)S(1)} %get-tuple-element.178) | copy-start | bytes 9220
  218.8 4.2 collective-permute-start
  271.4 10.1 %copy-start.107 = (bf16[2,256,384]{2,1,0:T(8,128)(2,1)}, bf16[2,256,384]{2,1,0:T(8,128)(2,1)S(1)}, u32[]{:S(2)}) copy-start(bf16[2,256,384]{2,1,0:T(8,128)(2,1)S(1)} %get-tuple-element.112) | copy-start | bytes 1179652
  271.4 15.5 %collective-permute-start.1 = (bf16[2,256,384]{2,1,0:T(8,128)(2,1)S(1)}, bf16[2,256,384]{2,1,0:T(8,128)(2,1)}, u32[]{:S(2)}, u32[]{:S(2)}) collective-permute-start(bf16[2,256,384]{2,1,0:T(8,128)(2,1)S(1)} %get-tuple-element.112), channel_id=1, source_target_pairs={{0,64},{1,65},{2,66},{3,67},{4,68},{5,69},{6,70},{7,71},{8,72},{9,... | collective-permute-start | bytes 1179656 | tf_op jit(solution)/shard_map/ppermute | solution.py:54
  274.5 9.3 %copy-start.16 = (bf16[2,2,256,384]{3,2,1,0:T(8,128)(2,1)S(1)}, bf16[2,2,256,384]{3,2,1,0:T(8,128)(2,1)}, u32[]{:S(2)}) copy-start(bf16[2,2,256,384]{3,2,1,0:T(8,128)(2,1)} %param.13) | copy-start | bytes 2359300
  274.5 9.2 %copy-start.195 = (f32[2,256]{1,0:T(2,128)S(1)}, f32[2,256]{1,0:T(2,128)}, u32[]{:S(2)}) copy-start(f32[2,256]{1,0:T(2,128)} %copy-done.194) | copy-start | bytes 6148
  274.5 9.2 %copy-start.198 = (f32[2,256]{1,0:T(2,128)S(1)}, f32[2,256]{1,0:T(2,128)}, u32[]{:S(2)}) copy-start(f32[2,256]{1,0:T(2,128)} %copy-done.197) | copy-start | bytes 6148
  319.5 4.9 collective-permute-start.2
  360.7 24.9 %collective-permute-start.3 = (bf16[2,256,384]{2,1,0:T(8,128)(2,1)}, bf16[2,256,384]{2,1,0:T(8,128)(2,1)}, u32[]{:S(2)}, u32[]{:S(2)}) collective-permute-start(bf16[2,256,384]{2,1,0:T(8,128)(2,1)} %get-tuple-element.101), channel_id=1, source_target_pairs={{64,0},{65,1},{66,2},{67,3},{68,4},{69,5},{70,6},{71,7},{72,8},{73... | collective-permute-start | bytes 1179656 | tf_op jit(solution)/shard_map/ppermute | solution.py:54
  373.6 8.5 %copy-start.75 = (bf16[2,256,384]{2,1,0:T(8,128)(2,1)S(1)}, bf16[2,256,384]{2,1,0:T(8,128)(2,1)}, u32[]{:S(2)}) copy-start(bf16[2,256,384]{2,1,0:T(8,128)(2,1)} %copy-done.74) | copy-start | bytes 1179652
  373.6 8.5 %copy-start.135 = (bf16[2,6,64,256]{3,2,1,0:T(8,128)(2,1)S(1)}, bf16[2,6,64,256]{3,2,1,0:T(8,128)(2,1)}, u32[]{:S(2)}) copy-start(bf16[2,6,64,256]{3,2,1,0:T(8,128)(2,1)} %get-tuple-element.146) | copy-start | bytes 1179652
  373.6 9.7 %copy-start.51 = (f32[384,1536]{1,0:T(8,128)S(1)}, f32[384,1536]{1,0:T(8,128)}, u32[]{:S(2)}) copy-start(f32[384,1536]{1,0:T(8,128)} %convolution_bitcast_fusion.4) | copy-start | bytes 7077892
  373.6 9.7 %copy-start.57 = (bf16[2,256,384]{2,1,0:T(8,128)(2,1)S(1)}, bf16[2,256,384]{2,1,0:T(8,128)(2,1)}, u32[]{:S(2)}) copy-start(bf16[2,256,384]{2,1,0:T(8,128)(2,1)} %copy-done.56) | copy-start | bytes 1179652
  373.6 9.7 %copy-start.60 = (bf16[2,256,384]{2,1,0:T(8,128)(2,1)S(1)}, bf16[2,256,384]{2,1,0:T(8,128)(2,1)}, u32[]{:S(2)}) copy-start(bf16[2,256,384]{2,1,0:T(8,128)(2,1)} %copy-done.58) | copy-start | bytes 1179652
  373.6 9.7 %copy-start.103 = (bf16[2,256,1536]{2,1,0:T(8,128)(2,1)S(1)}, bf16[2,256,1536]{2,1,0:T(8,128)(2,1)}, u32[]{:S(2)}) copy-start(bf16[2,256,1536]{2,1,0:T(8,128)(2,1)} %copy-done.102) | copy-start | bytes 4718596
  417.5 8.1 %copy-start.208 = (f32[384]{0:T(512)S(1)}, f32[384]{0:T(512)}, u32[]{:S(2)}) copy-start(f32[384]{0:T(512)} %get-tuple-element.94) | copy-start | bytes 4612
  417.5 8.1 %copy-start.251 = (f32[384]{0:T(512)S(1)}, f32[384]{0:T(512)}, u32[]{:S(2)}) copy-start(f32[384]{0:T(512)} %get-tuple-element.130) | copy-start | bytes 4612
  417.5 8.3 %copy-start.13 = (f32[384,1536]{1,0:T(8,128)S(1)}, f32[384,1536]{1,0:T(8,128)}, u32[]{:S(2)}) copy-start(f32[384,1536]{1,0:T(8,128)} %fusion.55) | copy-start | bytes 7077892
  (251 other events, 822.0 us)
Sparse Core Ops, SparseCore 0:
  21.8 145.5 all-reduce.5
  520.8 175.0 all-reduce.7
where the time goes:
time: 722 us; the launch traced here: 710 us
  waiting for transfers between devices  308 us (43%)
  local copies, waits for them, and re-layouts  185 us (26%)
  matrix products  136 us (19%)
  other arithmetic  50.6 us (7%)
  between operations  19 us (3%)
  starting transfers between devices  7.83 us (1%)
    unnamed x4, waiting for transfers between devices  308 us
    unnamed x563, local copies, waits for them, and re-layouts  68.9 us
    dot_general x12, matrix products, weight_grad(): jnp.einsum('lsd,lse->de', inputs, gradients, preferred_element_type=FLOAT)  43.5 us
    dot_general x12, matrix products, back_linear(): jnp.einsum('lse,de->lsd', gradients, weight, preferred_element_type=FLOAT)  26.2 us
    dot_general x12, matrix products, linear(): jnp.einsum('lsd,de->lse', inputs, weight, preferred_element_type=FLOAT)  22.7 us
  transfers between devices with their start and end apart: 6, of which 3 were waited for; matrix products, arithmetic and copies ran while one was open for 7% of the time, Pallas kernels for 0%

commit v1 on v0

v1 whole, which is shorter than its diff:
```python
import functools

import jax
import jax.numpy as jnp
from jax import lax
from jax.experimental import pallas as pl
from jax.experimental.pallas import tpu as pltpu
from jax.sharding import PartitionSpec as P

F = jnp.float32
B = jnp.bfloat16
D = 384
HEADS = 6
HEAD = 64
FF = 1536
SEQ = 256
EPS = 1e-06
CHIPS = 64
ROWS = 512
EXP = 512

C_QKV, C_PROJ, C_FC1, C_ADA, C_FC2, C_END = 0, 1152, 1536, 3072, 5376, 6528
SPARE = 6
K0 = 0.7978845608028654
K1 = 0.044715

NN = (1, 0)
NT = (1, 1)
TN = (0, 0)


def dot(a, b, dims=NN):
    return lax.dot_general(a, b, (((dims[0],), (dims[1],)), ((), ())), preferred_element_type=F)


def selector():
    row = lax.broadcasted_iota(jnp.int32, (EXP, D), 0)
    col = lax.broadcasted_iota(jnp.int32, (EXP, D), 1)
    r = row & 7
    return ((col == (row >> 3) * 6 + r) & (r < 6)).astype(F).astype(B)


def row_kind(shape, dim, kind):
    return (lax.broadcasted_iota(jnp.int32, shape, dim) & 7) == kind


def stats(v):
    centre = v - jnp.mean(v, axis=-1, keepdims=True)
    inv = lax.rsqrt(jnp.mean(centre * centre, axis=-1, keepdims=True) + EPS)
    return centre * inv, inv


def norm_back(g, n, inv):
    mg = jnp.mean(g, axis=-1, keepdims=True)
    mgn = jnp.mean(g * n, axis=-1, keepdims=True)
    return inv * (g - mg - n * mgn)


def head_masks():
    lane = lax.broadcasted_iota(jnp.int32, (1, 128), 1)
    low = (lane < HEAD).astype(F)
    return low.astype(B), (1.0 - low).astype(B)


def unpack(g, sel, w):
    sel[...] = selector()

    def step(i, _):
        at = pl.multiple_of(i * 256, 256)
        w["main"][:, pl.ds(at, 256)] = dot(sel[...], g[:, pl.ds(at, 256)], TN).astype(B)
        return 0

    lax.fori_loop(0, C_ADA // 256, step, 0)
    pick = row_kind((8, EXP), 1, 6).astype(F).astype(B)
    w["bias"][...] = dot(pick, g[:, :C_ADA])
    pick7 = row_kind((8, EXP), 1, 7).astype(F).astype(B)
    w["bias2"][...] = dot(pick7, g[:, C_PROJ:C_FC1])

    def step2(i, _):
        at = pl.multiple_of(i * 128, 128)
        parts = [
            g[pl.ds(at, 128), C_FC2 + a * D : C_FC2 + (a + 1) * D].astype(F).reshape(16, 8, D)
            for a in range(3)
        ]
        whole = jnp.concatenate(parts, axis=1).reshape(D, D).astype(B)
        w["fc2"][pl.ds(pl.multiple_of(i * D, D), D), :] = whole
        return 0

    lax.fori_loop(0, 4, step2, 0)


def modulate(cond, g, sel, mod):
    c = cond[...]
    act = (c * jax.nn.sigmoid(c)).astype(B)
    wide = dot(act, sel[...], NT)
    wide = jnp.where(row_kind((8, EXP), 1, 6), 1.0, wide).astype(B)
    mod[...] = dot(wide, g[:, C_ADA:C_FC2])


def forward(x, w, mod, k, y):
    main, bias, fc2 = w["main"], w["bias"], w["fc2"]

    def ln_in(i, _):
        rows = pl.ds(pl.multiple_of(i * 128, 128), 128)
        lat = pl.ds(i // 2, 1)
        n, _ = stats(x[rows, :].astype(F))
        k["ain"][rows, :] = (n * (1.0 + mod[lat, D : 2 * D]) + mod[lat, :D]).astype(B)
        return 0

    lax.fori_loop(0, 4, ln_in, 0)

    for c in range(3):
        cs = slice(c * D, (c + 1) * D)
        k["qkv"][:, cs] = (dot(k["ain"][...], main[:, cs]) + bias[0:1, cs]).astype(B)

    low, high = head_masks()

    def attend(i, _):
        rows = pl.ds(pl.multiple_of((i // 3) * SEQ, SEQ), SEQ)
        at = (i % 3) * 128
        q = k["qkv"][rows, pl.ds(pl.multiple_of(at, 128), 128)]
        key = k["qkv"][rows, pl.ds(pl.multiple_of(D + at, 128), 128)]
        v = k["qkv"][rows, pl.ds(pl.multiple_of(2 * D + at, 128), 128)]
        total = None
        for h, m in enumerate((low, high)):
            s = dot(key, q * m, NT) * 0.125
            top = jnp.max(s, axis=0, keepdims=True)
            e = jnp.exp(s - top)
            t = jnp.sum(e, axis=0, keepdims=True)
            p = (e * (1.0 / t)).astype(B)
            k["lse"][i, h : h + 1, :] = top + jnp.log(t)
            part = dot(p, v * m, TN)
            total = part if total is None else total + part
        k["att"][rows, pl.ds(pl.multiple_of(at, 128), 128)] = total.astype(B)
        return 0

    lax.fori_loop(0, 6, attend, 0)

    def mid(i, _):
        rows = pl.ds(pl.multiple_of(i * 128, 128), 128)
        lat = pl.ds(i // 2, 1)
        o = dot(k["att"][rows, :], main[:, C_PROJ:C_FC1]) + bias[0:1, C_PROJ:C_FC1]
        x1 = x[rows, :].astype(F) + mod[lat, 2 * D : 3 * D] * o
        k["o"][rows, :] = o
        k["x1"][rows, :] = x1
        n, _ = stats(x1)
        k["min"][rows, :] = (n * (1.0 + mod[lat, 4 * D : 5 * D]) + mod[lat, 3 * D : 4 * D]).astype(B)
        return 0

    lax.fori_loop(0, 4, mid, 0)

    def mlp(i, _):
        at = pl.multiple_of(i * 256, 256)
        cs = pl.ds(at, 256)
        ws = pl.ds(pl.multiple_of(C_FC1 + at, 256), 256)
        z = dot(k["min"][...], main[:, ws]) + bias[0:1, ws]
        zz = z * z
        t = jnp.tanh(z * (K0 + K0 * K1 * zz))
        half = 0.5 + 0.5 * t
        k["act"][:, cs] = (z * half).astype(B)
        k["slope"][:, cs] = half + (0.5 * z) * (1.0 - t * t) * (K0 + 3.0 * K0 * K1 * zz)
        return 0

    lax.fori_loop(0, 6, mlp, 0)

    def out(i, _):
        rows = pl.ds(pl.multiple_of(i * 128, 128), 128)
        lat = pl.ds(i // 2, 1)
        f = dot(k["act"][rows, :], fc2[...]) + w["bias2"][0:1, :]
        k["f"][rows, :] = f
        y[rows, :] = (k["x1"][rows, :] + mod[lat, 5 * D : 6 * D] * f).astype(B)
        return 0

    lax.fori_loop(0, 4, out, 0)


def token_sum(v):
    return jnp.sum(v, axis=0, keepdims=True)


def spread(sel, v, ones):
    wide = dot(sel[...], v, NT)
    return jnp.where(row_kind((EXP, 1), 0, 6), 1.0, wide).astype(B) if ones else wide.astype(B)


def backward(grad, x, cond, g, sel, w, mod, k, t, dx, dc, put):
    main, fc2 = w["main"], w["fc2"]
    dmod = t["dmod"]
    dmod[...] = jnp.zeros_like(dmod)

    def add_mod(lat, piece, v):
        cs = slice(piece * D, (piece + 1) * D)
        dmod[lat, cs] = dmod[lat, cs] + v

    t["db2"][...] = jnp.zeros_like(t["db2"])

    def start(i, _):
        rows = pl.ds(pl.multiple_of(i * 128, 128), 128)
        lat = pl.ds(i // 2, 1)
        gr = grad[rows, :].astype(F)
        df = (gr * mod[lat, 5 * D : 6 * D]).astype(B)
        t["df"][rows, :] = df
        add_mod(lat, 5, token_sum(gr * k["f"][rows, :]))
        t["db2"][0:1, :] = t["db2"][0:1, :] + token_sum(df.astype(F))
        return 0

    lax.fori_loop(0, 4, start, 0)

    def dmlp(i, _):
        cs = pl.ds(pl.multiple_of(i * 256, 256), 256)
        da = dot(t["df"][...], fc2[cs, :], NT)
        t["dz"][:, cs] = (da * k["slope"][:, cs]).astype(B)
        return 0

    lax.fori_loop(0, 6, dmlp, 0)

    t["wide"][...] = spread(sel, k["min"][...], True)

    def dw1(i, _):
        at = pl.multiple_of(i * 256, 256)
        put(pl.ds(0, EXP), pl.ds(pl.multiple_of(C_FC1 + at, 256), 256), dot(t["wide"][...], t["dz"][:, pl.ds(at, 256)]).astype(B))
        return 0

    lax.fori_loop(0, 6, dw1, 0)

    for c in range(4):
        part = dot(k["act"][:, c * D : (c + 1) * D], t["df"][...], TN).reshape(16, 24, D)
        for a in range(3):
            put(
                slice(c * 128, (c + 1) * 128),
                slice(C_FC2 + a * D, C_FC2 + (a + 1) * D),
                part[:, 8 * a : 8 * a + 8, :].reshape(128, D).astype(B),
            )

    def dmid(i, _):
        rows = pl.ds(pl.multiple_of(i * 128, 128), 128)
        lat = pl.ds(i // 2, 1)
        dmin = dot(t["dz"][rows, :], main[:, C_FC1:C_ADA], NT)
        n, inv = stats(k["x1"][rows, :])
        add_mod(lat, 4, token_sum(dmin * n))
        add_mod(lat, 3, token_sum(dmin))
        d1 = grad[rows, :].astype(F) + norm_back(dmin * (1.0 + mod[lat, 4 * D : 5 * D]), n, inv)
        t["dx1"][rows, :] = d1
        do = (d1 * mod[lat, 2 * D : 3 * D]).astype(B)
        add_mod(lat, 2, token_sum(d1 * k["o"][rows, :]))
        t["df"][rows, :] = do
        t["datt"][rows, :] = dot(do, main[:, C_PROJ:C_FC1], NT).astype(B)
        return 0

    lax.fori_loop(0, 4, dmid, 0)

    t["wide"][...] = spread(sel, k["att"][...], True)
    dp = dot(t["wide"][...], t["df"][...])
    dp = jnp.where(row_kind((EXP, 1), 0, 7), t["db2"][0:1, :], dp)
    put(slice(0, EXP), slice(C_PROJ, C_FC1), dp.astype(B))

    low, high = head_masks()

    def dattend(i, _):
        rows = pl.ds(pl.multiple_of((i // 3) * SEQ, SEQ), SEQ)
        at = (i % 3) * 128
        qs = pl.ds(pl.multiple_of(at, 128), 128)
        ks = pl.ds(pl.multiple_of(D + at, 128), 128)
        vs = pl.ds(pl.multiple_of(2 * D + at, 128), 128)
        q = k["qkv"][rows, qs]
        key = k["qkv"][rows, ks]
        v = k["qkv"][rows, vs]
        da = t["datt"][rows, qs]
        dq = dk = dv = None
        for h, m in enumerate((low, high)):
            qm = q * m
            dam = da * m
            s = dot(key, qm, NT) * 0.125
            p = jnp.exp(s - k["lse"][i, h : h + 1, :])
            dp = dot(v, dam, NT)
            ds = (p * (dp - jnp.sum(p * dp, axis=0, keepdims=True))).astype(B)
            v1 = dot(p.astype(B), dam)
            k1 = dot(ds, qm)
            q1 = dot(ds, key * m, TN)
            dv = v1 if dv is None else dv + v1
            dk = k1 if dk is None else dk + k1
            dq = q1 if dq is None else dq + q1
        t["dqkv"][rows, qs] = (dq * 0.125).astype(B)
        t["dqkv"][rows, ks] = (dk * 0.125).astype(B)
        t["dqkv"][rows, vs] = dv.astype(B)
        return 0

    lax.fori_loop(0, 6, dattend, 0)

    t["wide"][...] = spread(sel, k["ain"][...], True)

    def dwq(i, _):
        cs = pl.ds(pl.multiple_of(i * 384, 128), 384)
        put(pl.ds(0, EXP), cs, dot(t["wide"][...], t["dqkv"][:, cs]).astype(B))
        return 0

    lax.fori_loop(0, 3, dwq, 0)

    def dlast(i, _):
        rows = pl.ds(pl.multiple_of(i * 128, 128), 128)
        lat = pl.ds(i // 2, 1)
        dain = dot(t["dqkv"][rows, :], main[:, C_QKV:C_PROJ], NT)
        n, inv = stats(x[rows, :].astype(F))
        add_mod(lat, 1, token_sum(dain * n))
        add_mod(lat, 0, token_sum(dain))
        back = norm_back(dain * (1.0 + mod[lat, D : 2 * D]), n, inv)
        dx[rows, :] = (t["dx1"][rows, :] + back).astype(B)
        return 0

    lax.fori_loop(0, 4, dlast, 0)

    dm = dmod[...].astype(B)
    c = cond[...]
    sig = jax.nn.sigmoid(c)
    act = (c * sig).astype(B)
    live = lax.broadcasted_iota(jnp.int32, (8, 1), 0) < 2
    dm = jnp.where(live, dm.astype(F), 0.0)
    wide = dot(sel[...], act, NT)
    wide = jnp.where(row_kind((EXP, 1), 0, 6), 1.0, wide).astype(B)
    for i in range(3):
        at = i * 768
        put(slice(0, EXP), slice(C_ADA + at, C_ADA + at + 768), dot(wide, dm[:, at : at + 768].astype(B)).astype(B))
    dwide = dot(dm.astype(B), g[:, C_ADA:C_FC2], NT)
    dact = lax.dot_general(
        dwide, sel[...].astype(F), (((1,), (0,)), ((), ())), precision=lax.Precision.HIGHEST, preferred_element_type=F
    )
    dc[...] = dact * (sig * (1.0 + c * (1.0 - sig)))


KEEP = (
    ("ain", (ROWS, D), B),
    ("qkv", (ROWS, 3 * D), B),
    ("lse", (6, 8, SEQ), F),
    ("att", (ROWS, D), B),
    ("o", (ROWS, D), F),
    ("x1", (ROWS, D), F),
    ("min", (ROWS, D), B),
    ("slope", (ROWS, FF), F),
    ("act", (ROWS, FF), B),
    ("f", (ROWS, D), F),
)
WEIGHTS = (("main", (D, C_ADA), B), ("bias", (8, C_ADA), F), ("bias2", (8, D), F), ("fc2", (FF, D), B))
TEMPS = (
    ("dmod", (8, 6 * D), F),
    ("db2", (8, D), F),
    ("df", (ROWS, D), B),
    ("dz", (ROWS, FF), B),
    ("wide", (EXP, ROWS), B),
    ("dx1", (ROWS, D), F),
    ("datt", (ROWS, D), B),
    ("dqkv", (ROWS, 3 * D), B),
)
SEL = (("sel", (EXP, D), B),)
MOD = (("mod", (8, 6 * D), F),)


def buffers(table):
    return [pltpu.VMEM(shape, dtype) for _, shape, dtype in table]


def shapes(table):
    return [jax.ShapeDtypeStruct(shape, dtype) for _, shape, dtype in table]


def named(table, refs):
    return {name: ref for (name, _, _), ref in zip(table, refs)}


def fetch(pick, first, second, into, sem, cols=None):
    def go(ref):
        src = ref if cols is None else ref.at[:, cols[0] : cols[1]]
        copy = pltpu.make_async_copy(src, into, sem)
        copy.start()
        copy.wait()

    @pl.when(pick)
    def _():
        go(first)

    @pl.when(jnp.logical_not(pick))
    def _():
        go(second)


def front_kernel(core, own, other, x, cond, *refs):
    n_keep, n_w = len(KEEP), len(WEIGHTS)
    y = refs[0]
    k = named(KEEP, refs[1 : 1 + n_keep])
    w = named(WEIGHTS, refs[1 + n_keep : 1 + n_keep + n_w])
    mod, g, sel, sem = refs[1 + n_keep + n_w :]
    fetch(core[0] == 0, own, other, g, sem)
    unpack(g, sel, w)
    modulate(cond, g, sel, mod)
    forward(x, w, mod, k, y)


def turn_kernel(core, own, other, x, cond, grad, y, dx, dc, pack, *refs):
    n_keep, n_w, n_t = len(KEEP), len(WEIGHTS), len(TEMPS)
    k = named(KEEP, refs[:n_keep])
    w = named(WEIGHTS, refs[n_keep : n_keep + n_w])
    t = named(TEMPS, refs[n_keep + n_w : n_keep + n_w + n_t])
    mod, g, sel, sem = refs[n_keep + n_w + n_t :]
    fetch(core[0] == 1, own, other, g, sem)
    unpack(g, sel, w)
    modulate(cond, g, sel, mod)
    forward(x, w, mod, k, y)

    def put(rows, cols, value):
        pack[rows, cols] = value

    backward(grad, x, cond, g, sel, w, mod, k, t, dx, dc, put)


def back_kernel(core, own, other, x, cond, grad, *refs):
    n_keep, n_w, n_t = len(KEEP), len(WEIGHTS), len(TEMPS)
    k = named(KEEP, refs[:n_keep])
    w = named(WEIGHTS, refs[n_keep : n_keep + n_w])
    mod, dx, dc, pack = refs[n_keep + n_w : n_keep + n_w + 4]
    refs = refs[n_keep + n_w + 4 :]
    t = named(TEMPS, refs[:n_t])
    g, sel, sem = refs[n_t:]
    sel[...] = selector()
    fetch(core[0] == 0, own, other, g.at[:, C_ADA:C_FC2], sem, (C_ADA, C_FC2))

    def put(rows, cols, value):
        pack[rows, cols] = value

    backward(grad, x, cond, g, sel, w, mod, k, t, dx, dc, put)


VM = pl.BlockSpec(memory_space=pltpu.VMEM)
ANY = pl.BlockSpec(memory_space=pl.ANY)
SM = pl.BlockSpec(memory_space=pltpu.SMEM)
PARAMS = pltpu.CompilerParams(vmem_limit_bytes=60 * 1024 * 1024)
G_BUF = pltpu.VMEM((EXP, C_END), B)
SEL_BUF = pltpu.VMEM((EXP, D), B)
SEM = pltpu.SemaphoreType.DMA
ROWS_OUT = jax.ShapeDtypeStruct((ROWS, D), B)
COND_OUT = jax.ShapeDtypeStruct((8, D), F)
PACK_OUT = jax.ShapeDtypeStruct((EXP, C_END), B)


def front(core, own, other, x, cond):
    outs = [ROWS_OUT] + shapes(KEEP) + shapes(WEIGHTS) + shapes(MOD)
    return pl.pallas_call(
        front_kernel,
        out_shape=outs,
        in_specs=[SM, ANY, ANY, VM, VM],
        out_specs=[VM] * len(outs),
        scratch_shapes=[G_BUF, SEL_BUF, SEM],
        compiler_params=PARAMS,
        name="front",
    )(core, own, other, x, cond)


def turn(core, own, other, x, cond, grad):
    return pl.pallas_call(
        turn_kernel,
        out_shape=[ROWS_OUT, ROWS_OUT, COND_OUT, PACK_OUT],
        in_specs=[SM, ANY, ANY, VM, VM, VM],
        out_specs=[VM] * 4,
        scratch_shapes=buffers(KEEP) + buffers(WEIGHTS) + buffers(TEMPS) + buffers(MOD) + [G_BUF, SEL_BUF, SEM],
        compiler_params=PARAMS,
        name="turn",
    )(core, own, other, x, cond, grad)


def back(core, own, other, x, cond, grad, kept):
    return pl.pallas_call(
        back_kernel,
        out_shape=[ROWS_OUT, COND_OUT, PACK_OUT],
        in_specs=[SM, ANY, ANY, VM, VM, VM] + [VM] * len(kept),
        out_specs=[VM] * 3,
        scratch_shapes=buffers(TEMPS) + [G_BUF, SEL_BUF, SEM],
        compiler_params=PARAMS,
        name="back",
    )(core, own, other, x, cond, grad, *kept)


def line_up(j, w_qkv, b_qv, w_proj, b_proj, w_fc1, b_fc1, w_fc2, b_fc2, w_ada, b_ada):
    main = jnp.concatenate([w_qkv, w_proj, w_fc1, w_ada], axis=1)
    line = jnp.zeros((C_FC2,), B)
    at_qv = jnp.where(j < 32, 12 * j, 12 * j + D)
    line = lax.dynamic_update_slice(line, b_qv, (at_qv,))
    line = lax.dynamic_update_slice(line, b_proj, (C_PROJ + 6 * j,))
    line = lax.dynamic_update_slice(line, b_fc1, (C_FC1 + 24 * j,))
    line = lax.dynamic_update_slice(line, b_ada, (C_ADA + 36 * j,))
    spare = lax.dynamic_update_slice(jnp.zeros((C_FC2,), B), b_fc2, (C_PROJ + 6 * j,))
    top = jnp.concatenate([main, line[None], spare[None]], axis=0)
    return jnp.concatenate([top, w_fc2[:8], w_fc2[8:16], w_fc2[16:]], axis=1)


def swap(x):
    return lax.ppermute(x, "pipe", [(0, 1), (1, 0)])


def to_all(block):
    copies = jnp.broadcast_to(block[None], (CHIPS, *block.shape))
    return lax.all_to_all(copies, "shard", 0, 0, tiled=True).reshape(EXP, block.shape[1])


def shards(latents, conditions, cotangent, w_qkv, b_qv, w_proj, b_proj, w_fc1, b_fc1, w_fc2, b_fc2, w_ada, b_ada):
    p = lax.axis_index("pipe")
    j = lax.axis_index("shard")
    first = p == 0
    core = p.reshape(1).astype(jnp.int32)
    own = to_all(line_up(j, w_qkv[0], b_qv[0], w_proj[0], b_proj[0], w_fc1[0], b_fc1[0], w_fc2[0], b_fc2[0], w_ada[0], b_ada[0]))
    other = swap(own)
    x = lax.dynamic_index_in_dim(latents, p, 0, keepdims=False).reshape(ROWS, D)
    cot = lax.dynamic_index_in_dim(cotangent, p, 0, keepdims=False).reshape(ROWS, D)
    cond = lax.dynamic_index_in_dim(conditions, p, 0, keepdims=False).astype(F)
    cond = jnp.concatenate([cond, jnp.zeros((6, D), F)], axis=0)

    h, *kept = front(core, own, other, x, cond)
    y, dx1, dc1, pack1 = turn(core, own, other, h, cond, cot)
    dx0, dc0, pack0 = back(core, own, other, x, cond, dx1, kept)

    def pair(for_first, for_second):
        keep = jnp.where(first, for_first, for_second)
        came = swap(jnp.where(first, for_second, for_first))
        both = jnp.where(first, jnp.stack([keep, came]), jnp.stack([came, keep]))
        return both.reshape(1, 2, 2, SEQ, D)

    section_outputs = pair(h, y)
    input_grads = pair(dx0, dx1)
    dc = (dc0 + dc1)[:2]
    dc_other = swap(dc)
    cond_grad = jnp.where(first, jnp.stack([dc, dc_other]), jnp.stack([dc_other, dc]))

    mine = jnp.where(first, pack0, pack1)
    came = swap(jnp.where(first, pack1, pack0))
    total = (mine.astype(F) + came.astype(F)).astype(B).reshape(CHIPS, 8, C_END)
    parts = lax.all_to_all(total, "shard", 0, 0, tiled=True)
    done = jnp.sum(parts.astype(F), axis=0)

    rows = done[:6]
    at_qv = jnp.where(j < 32, 12 * j, 12 * j + D)
    line = done[6]
    outs = (
        rows[:, C_QKV:C_PROJ],
        lax.dynamic_slice(line, (at_qv,), (12,)),
        rows[:, C_PROJ:C_FC1],
        lax.dynamic_slice(line, (C_PROJ + 6 * j,), (6,)),
        rows[:, C_FC1:C_ADA],
        lax.dynamic_slice(line, (C_FC1 + 24 * j,), (24,)),
        done[:, C_FC2:].reshape(8, 3, D).transpose(1, 0, 2).reshape(24, D),
        lax.dynamic_slice(done[7], (C_PROJ + 6 * j,), (6,)),
        rows[:, C_ADA:C_FC2],
        lax.dynamic_slice(line, (C_ADA + 36 * j,), (36,)),
    )
    return (section_outputs, input_grads, cond_grad) + tuple(o[None] for o in outs)


def solution(mesh):
    rows = P(None, "shard", None, None)
    wide = P("pipe", "shard", None)
    thin = P("pipe", "shard")
    both = P("pipe", None, "shard", None, None)
    pairs = (wide, thin) * 5
    return jax.shard_map(
        shards,
        mesh=mesh,
        in_specs=(rows, P(None, "shard", None), rows) + pairs,
        out_specs=(both, both, P(None, "shard", None)) + pairs,
        check_vma=False,
    )
```

time: 722 us -> 350 us (0.48); the launches traced: 710 us -> 349 us
  waiting for transfers between devices: 308 us -> 116 us
  local copies, waits for them, and re-layouts: 185 us -> 12.3 us
  matrix products: 136 us -> 0 us
  Pallas kernels: 0 us -> 97 us
  blocking collectives: 3.51 us -> 90.7 us
  other arithmetic: 50.6 us -> 23.3 us
  between operations: 19 us -> 0.87 us
    unnamed x4 -> x0, waiting for transfers between devices: 308 us -> none
    dot_general x66 -> x0, matrix products: 136 us -> none  [the longest x12 43.5 us: weight_grad(): jnp.einsum('lsd,lse->de', inputs, gradients, preferred_element_type=FLOAT)]
    pallas_call x0 -> x3, Pallas kernels: none -> 97 us  [the longest x1 42.5 us: turn(): pl.pallas_call(turn_kernel, out_shape=[ROWS_OUT, ROWS_OUT, COND_OUT, PACK...]
    all_to_all x0 -> x1, waiting for transfers between devices: none -> 95.1 us  [shards(): parts = lax.all_to_all(total, 'shard', 0, 0, tiled=True)]
    all_to_all x1, blocking collectives: 3.51 us -> 90.7 us  [to_all(): lax.all_to_all(copies, 'shard', 0, 0, tiled=True)]
    unnamed x563 -> x16, local copies, waits for them, and re-layouts: 68.9 us -> 0.05 us
    another operation x19 -> x0, local copies, waits for them, and re-layouts: 31.2 us -> none  [the longest x5 13.9 us: sum_packed(): lines = jnp.concatenate([b.reshape(length, -1) for b in tiles], axis=1)]
    reduce_sum x33 -> x1, other arithmetic: 26.3 us -> 3.89 us  [shards(): done = jnp.sum(parts.astype(F), axis=0)]
  transfers between devices with their start and end apart: 6 -> 6, of which waited for: 3 -> 4; matrix products, arithmetic and copies ran while one was open for 7% -> 1% of each run, Pallas kernels for 0% -> 0%
where the time goes in v1:
time: 350 us; the launch traced here: 349 us
  waiting for transfers between devices  116 us (33%)
  Pallas kernels  97 us (28%)
  blocking collectives  90.7 us (26%)
  other arithmetic  23.3 us (7%)
  local copies, waits for them, and re-layouts  12.3 us (4%)
  starting transfers between devices  9 us (3%)
    all_to_all x1, waiting for transfers between devices, shards(): parts = lax.all_to_all(total, 'shard', 0, 0, tiled=True)  95.1 us
    all_to_all x1, blocking collectives, to_all(): lax.all_to_all(copies, 'shard', 0, 0, tiled=True)  90.7 us
    pallas_call x1, Pallas kernels, turn(): pl.pallas_call(turn_kernel, out_shape=[ROWS_OUT, ROWS_OUT, COND_OUT, PACK...  42.5 us
    pallas_call x1, Pallas kernels, back(): pl.pallas_call(back_kernel, out_shape=[ROWS_OUT, COND_OUT, PACK_OUT], in_...  29.4 us
    pallas_call x1, Pallas kernels, front(): pl.pallas_call(front_kernel, out_shape=outs, in_specs=[SM, ANY, ANY, VM,...  25.1 us
    ppermute x5, waiting for transfers between devices, swap(): return lax.ppermute(x, 'pipe', [(0, 1), (1, 0)])  20.7 us
    reshape x1, other arithmetic, shards(): total = (mine.astype(F) + came.astype(F)).astype(B).reshape(CHIPS, 8, C_END)  8.03 us
  transfers between devices with their start and end apart: 6, of which 4 were waited for; matrix products, arithmetic and copies ran while one was open for 1% of the time, Pallas kernels for 0%

profile of v1, /device:TPU:1, one launch (start us, length us, event | category | flops | bytes accessed | tf_op | source)
XLA Modules:
  0.0 348.9 jit_solution(9573175976854643933)
XLA Ops:
  0.7 0.7 slice_bitcast_fusion.2
  1.4 0.8 dynamic_update_slice.24
  2.2 0.8 dynamic_update_slice.20
  3.0 0.8 dynamic_update_slice.21
  3.8 0.8 dynamic_update_slice.22
  4.6 0.8 dynamic_update_slice.23
  5.4 0.9 pad_maximum_fusion
  6.7 90.7 %all_to_all.10 = bf16[64,8,6528]{2,1,0:T(8,128)(2,1)} all-to-all(bf16[64,8,6528]{2,1,0:T(8,128)(2,1)S(1)} %broadcast_in_dim.13), channel_id=1, replica_groups=mesh['pipe'=2,'shard'=64] {'shard'}, dimensions={0} | all-to-all | bytes 13369344 | tf_op jit(solution)/shard_map/all_to_all | solution.py:499
  97.4 2.0 collective-permute-start
  100.1 1.0 constant_dynamic-slice_fusion.5
  101.1 9.1 %collective-permute-done.other = bf16[512,6528]{1,0:T(8,128)(2,1)} collective-permute-done((bf16[512,6528]{1,0:T(8,128)(2,1)}, bf16[512,6528]{1,0:T(8,128)(2,1)}, u32[]{:S(2)}, u32[]{:S(2)}) %collective-permute-start) | collective-permute-done | bytes 6684704 | tf_op jit(solution)/shard_map/ppermute | solution.py:494
  110.1 25.1 %front.1 = (bf16[512,384]{1,0:T(8,128)(2,1)}, bf16[512,384]{1,0:T(8,128)(2,1)}, bf16[512,1152]{1,0:T(8,128)(2,1)}, f32[6,8,256]{2,1,0:T(8,128)}, bf16[512,384]{1...) custom-call(s32[1]{0:T(128)} %bitcast.core, ...), custom_call_target="tpu_custom_call" | custom-call | tf_op jit(solution)/shard_map/front/pallas_call | solution.py:445
  135.2 42.5 %turn.1 = (bf16[512,384]{1,0:T(8,128)(2,1)}, bf16[512,384]{1,0:T(8,128)(2,1)}, f32[8,384]{1,0:T(8,128)}, bf16[512,6528]{1,0:T(8,128)(2,1)}) custom-call(s32[1]{0:T(128)} %bitcast.core, bf16[512,6528]{1,0:T(8,128)(2,1)} %bitcast.8.own, bf16[512,6528]{1,0:T(8,128)(2,1)} %collective-permute-done.other, bf16[512,384]{1,0:T(8,128)(2,1)} %get-tuple-element.36.x, ...), custom_call_target="tpu_custom_call" | custom-call | tf_op jit(solution)/shard_map/turn/pallas_call | solution.py:457
  177.7 29.4 %back.1 = (bf16[512,384]{1,0:T(8,128)(2,1)}, f32[8,384]{1,0:T(8,128)}, bf16[512,6528]{1,0:T(8,128)(2,1)}) custom-call(s32[1]{0:T(128)} %bitcast.core, bf16[512,6528]{1,0:T(8,128)(2,1)} %bitcast.8.own, bf16[512,6528]{1,0:T(8,128)(2,1)} %collective-permute-done.other, bf16[512,384]{1,0:T(8,128)(2,1)} %bitcast.30, f32[8,384]{1,0:T(8,128)} %pad_convert_fusion.cond, ...), custom_call_target="tpu_custom_call" | custom-call | tf_op jit(solution)/shard_map/back/pallas_call | solution.py:469
  207.1 6.4 %broadcast_select_fusion = bf16[512,6528]{1,0:T(8,128)(2,1)} fusion(bf16[512,6528]{1,0:T(8,128)(2,1)} %get-tuple-element.58, bf16[512,6528]{1,0:T(8,128)(2,1)} %get-tuple-element.57, pred[]{:T(512)S(6)} %eq.3), kind=kLoop, calls=%fused_computation.3 | loop fusion | flops 3342336 | bytes 20054016 | tf_op jit(solution)/shard_map/jit(_where)/select_n | solution.py:531
  213.8 10.7 %collective-permute-done.4 = bf16[512,6528]{1,0:T(8,128)(2,1)S(1)} collective-permute-done((bf16[512,6528]{1,0:T(8,128)(2,1)}, bf16[512,6528]{1,0:T(8,128)(2,1)S(1)}, u32[]{:S(2)}, u32[]{:S(2)}) %collective-permute-start.4) | collective-permute-done | bytes 6684704 | tf_op jit(solution)/shard_map/ppermute | solution.py:494
  224.5 8.0 %fusion = bf16[64,8,6528]{2,1,0:T(8,128)(2,1)} fusion(bf16[512,6528]{1,0:T(8,128)(2,1)S(1)} %collective-permute-done.4, bf16[512,6528]{1,0:T(8,128)(2,1)} %get-tuple-element.57, bf16[512,6528]{1,0:T(8,128)(2,1)} %get-tuple-element.58, pred[]{:T(512)S(6)} %eq.3), kind=kLoop, calls=%fused_computation.2 | loop fusion | flops 16711680 | bytes 26738688 | tf_op jit(solution)/shard_map/reshape | solution.py:532
  232.5 5.9 %all-to-all-start.1 = ((bf16[64,8,6528]{2,1,0:T(8,128)(2,1)}), bf16[64,8,6528]{2,1,0:T(8,128)(2,1)}, u32[]{:S(2)}, u32[]{:S(2)}) async-start(bf16[64,8,6528]{2,1,0:T(8,128)(2,1)} %fusion), calls=%async_computation.1 | async-start | bytes 13369344 | tf_op jit(solution)/shard_map/all_to_all | solution.py:533
  239.3 0.7 slice_add_fusion
  240.3 0.9 collective-permute-done.3
  241.8 1.0 maximum_select_fusion.1
  242.8 1.0 maximum_select_fusion
  243.8 95.1 %all-to-all-done.1 = bf16[64,8,6528]{2,1,0:T(8,128)(2,1)} async-done(((bf16[64,8,6528]{2,1,0:T(8,128)(2,1)}), bf16[64,8,6528]{2,1,0:T(8,128)(2,1)}, u32[]{:S(2)}, u32[]{:S(2)}) %all-to-all-start.1) | async-done | bytes 6684704 | tf_op jit(solution)/shard_map/all_to_all | solution.py:533
  338.9 3.9 %convert_reduce_fusion = f32[8,6528]{1,0:T(8,128)S(1)} fusion(bf16[64,8,6528]{2,1,0:T(8,128)(2,1)} %all-to-all-done.1), kind=kLoop, calls=%fused_computation | loop fusion | flops 6632448 | bytes 6893568 | tf_op jit(solution)/shard_map/reduce_sum | solution.py:534
  (45 shorter events, 9.2 us)
Async XLA Ops:
  0.6 98.8 %copy-start = (bf16[2,2,384]{2,1,0:T(2,128)(2,1)S(1)}, bf16[2,2,384]{2,1,0:T(2,128)(2,1)}, u32[]{:S(2)}) copy-start(bf16[2,2,384]{2,1,0:T(2,128)(2,1)} %param.14) | copy-start | bytes 9220
  6.7 93.3 %copy-start.6 = (bf16[2,2,256,384]{3,2,1,0:T(8,128)(2,1)S(1)}, bf16[2,2,256,384]{3,2,1,0:T(8,128)(2,1)}, u32[]{:S(2)}) copy-start(bf16[2,2,256,384]{3,2,1,0:T(8,128)(2,1)} %param.15) | copy-start | bytes 2359300
  6.7 93.3 %copy-start.7 = (bf16[2,2,256,384]{3,2,1,0:T(8,128)(2,1)S(1)}, bf16[2,2,256,384]{3,2,1,0:T(8,128)(2,1)}, u32[]{:S(2)}) copy-start(bf16[2,2,256,384]{3,2,1,0:T(8,128)(2,1)} %param.13) | copy-start | bytes 2359300
  97.4 12.7 %collective-permute-start = (bf16[512,6528]{1,0:T(8,128)(2,1)}, bf16[512,6528]{1,0:T(8,128)(2,1)}, u32[]{:S(2)}, u32[]{:S(2)}) collective-permute-start(bf16[512,6528]{1,0:T(8,128)(2,1)} %bitcast.8.own), channel_id=1, source_target_pairs={{0,64},{64,0},{1,65},{65,1},{2,66},{66,2},{3,67},{67,3},{4,68},{68... | collective-permute-start | bytes 20054024 | tf_op jit(solution)/shard_map/ppermute | solution.py:494
  213.6 10.9 %collective-permute-start.4 = (bf16[512,6528]{1,0:T(8,128)(2,1)}, bf16[512,6528]{1,0:T(8,128)(2,1)S(1)}, u32[]{:S(2)}, u32[]{:S(2)}) collective-permute-start(bf16[512,6528]{1,0:T(8,128)(2,1)} %broadcast_select_fusion), channel_id=1, source_target_pairs={{0,64},{64,0},{1,65},{65,1},{2,66},{66,2},{3,67},{67,3},{4,68},{68... | collective-permute-start | bytes 20054024 | tf_op jit(solution)/shard_map/ppermute | solution.py:494
  232.5 5.9 %copy-start.3 = (bf16[512,384]{1,0:T(8,128)(2,1)S(1)}, bf16[512,384]{1,0:T(8,128)(2,1)}, u32[]{:S(2)}) copy-start(bf16[512,384]{1,0:T(8,128)(2,1)} %get-tuple-element.38.grad) | copy-start | bytes 1179652
  232.5 5.9 %copy-start.5 = (bf16[512,384]{1,0:T(8,128)(2,1)S(1)}, bf16[512,384]{1,0:T(8,128)(2,1)}, u32[]{:S(2)}) copy-start(bf16[512,384]{1,0:T(8,128)(2,1)} %get-tuple-element.54) | copy-start | bytes 1179652
  232.5 6.3 %copy-start.2 = (bf16[512,384]{1,0:T(8,128)(2,1)S(1)}, bf16[512,384]{1,0:T(8,128)(2,1)}, u32[]{:S(2)}) copy-start(bf16[512,384]{1,0:T(8,128)(2,1)} %get-tuple-element.36.x) | copy-start | bytes 1179652
  232.5 6.3 %copy-start.4 = (bf16[512,384]{1,0:T(8,128)(2,1)S(1)}, bf16[512,384]{1,0:T(8,128)(2,1)}, u32[]{:S(2)}) copy-start(bf16[512,384]{1,0:T(8,128)(2,1)} %get-tuple-element.37) | copy-start | bytes 1179652
  232.5 106.4 %all-to-all-start.1 = ((bf16[64,8,6528]{2,1,0:T(8,128)(2,1)}), bf16[64,8,6528]{2,1,0:T(8,128)(2,1)}, u32[]{:S(2)}, u32[]{:S(2)}) async-start(bf16[64,8,6528]{2,1,0:T(8,128)(2,1)} %fusion), calls=%async_computation.1 | async-start | bytes 13369344 | tf_op jit(solution)/shard_map/all_to_all | solution.py:533
  238.4 110.5 %copy-start.1 = (bf16[2,2,384]{2,1,0:T(2,128)(2,1)S(1)}, bf16[2,2,384]{2,1,0:T(2,128)(2,1)}, u32[]{:S(2)}) copy-start(bf16[2,2,384]{2,1,0:T(2,128)(2,1)} %param.14) | copy-start | bytes 9220
  238.5 3.3 collective-permute-start.2
  238.9 3.9 %collective-permute-start.1 = (bf16[512,384]{1,0:T(8,128)(2,1)S(1)}, bf16[512,384]{1,0:T(8,128)(2,1)S(1)}, u32[]{:S(2)}, u32[]{:S(2)}) collective-permute-start(bf16[512,384]{1,0:T(8,128)(2,1)S(1)} %get-tuple-element.62), channel_id=1, source_target_pairs={{0,64},{64,0},{1,65},{65,1},{2,66},{66,2},{3,67},{67,3},{4,68},{68... | collective-permute-start | bytes 1179656 | tf_op jit(solution)/shard_map/ppermute | solution.py:494
  240.0 1.2 collective-permute-start.3

commit v2 on v1

--- a/solution.py
+++ b/solution.py
@@ -20,6 +20,7 @@
 EXP = 512
 
 C_QKV, C_PROJ, C_FC1, C_ADA, C_FC2, C_END = 0, 1152, 1536, 3072, 5376, 6528
+HALF = 3328
 SPARE = 6
 K0 = 0.7978845608028654
 K1 = 0.044715
@@ -218,7 +219,7 @@
 
     def dw1(i, _):
         at = pl.multiple_of(i * 256, 256)
-        put(pl.ds(0, EXP), pl.ds(pl.multiple_of(C_FC1 + at, 256), 256), dot(t["wide"][...], t["dz"][:, pl.ds(at, 256)]).astype(B))
+        put(0, pl.ds(0, EXP), pl.ds(pl.multiple_of(C_FC1 + at, 256), 256), dot(t["wide"][...], t["dz"][:, pl.ds(at, 256)]).astype(B))
         return 0
 
     lax.fori_loop(0, 6, dw1, 0)
@@ -227,8 +228,9 @@
         part = dot(k["act"][:, c * D : (c + 1) * D], t["df"][...], TN).reshape(16, 24, D)
         for a in range(3):
             put(
+                1,
                 slice(c * 128, (c + 1) * 128),
-                slice(C_FC2 + a * D, C_FC2 + (a + 1) * D),
+                slice(C_FC2 - HALF + a * D, C_FC2 - HALF + (a + 1) * D),
                 part[:, 8 * a : 8 * a + 8, :].reshape(128, D).astype(B),
             )
 
@@ -252,7 +254,7 @@
     t["wide"][...] = spread(sel, k["att"][...], True)
     dp = dot(t["wide"][...], t["df"][...])
     dp = jnp.where(row_kind((EXP, 1), 0, 7), t["db2"][0:1, :], dp)
-    put(slice(0, EXP), slice(C_PROJ, C_FC1), dp.astype(B))
+    put(0, slice(0, EXP), slice(C_PROJ, C_FC1), dp.astype(B))
 
     low, high = head_masks()
 
@@ -291,7 +293,7 @@
 
     def dwq(i, _):
         cs = pl.ds(pl.multiple_of(i * 384, 128), 384)
-        put(pl.ds(0, EXP), cs, dot(t["wide"][...], t["dqkv"][:, cs]).astype(B))
+        put(0, pl.ds(0, EXP), cs, dot(t["wide"][...], t["dqkv"][:, cs]).astype(B))
         return 0
 
     lax.fori_loop(0, 3, dwq, 0)
@@ -317,9 +319,11 @@
     dm = jnp.where(live, dm.astype(F), 0.0)
     wide = dot(sel[...], act, NT)
     wide = jnp.where(row_kind((EXP, 1), 0, 6), 1.0, wide).astype(B)
-    for i in range(3):
-        at = i * 768
-        put(slice(0, EXP), slice(C_ADA + at, C_ADA + at + 768), dot(wide, dm[:, at : at + 768].astype(B)).astype(B))
+    for i in range(9):
+        at = i * 256
+        to = C_ADA + at if i == 0 else C_ADA + at - HALF
+        put(int(i > 0), slice(0, EXP), slice(to, to + 256), dot(wide, dm[:, at : at + 256].astype(B)).astype(B))
+    put(1, slice(0, EXP), slice(C_END - HALF, HALF), jnp.zeros((EXP, 2 * HALF - C_END), B))
     dwide = dot(dm.astype(B), g[:, C_ADA:C_FC2], NT)
     dact = lax.dot_general(
         dwide, sel[...].astype(F), (((1,), (0,)), ((), ())), precision=lax.Precision.HIGHEST, preferred_element_type=F
@@ -366,20 +370,46 @@
     return {name: ref for (name, _, _), ref in zip(table, refs)}
 
 
-def fetch(pick, first, second, into, sem, cols=None):
-    def go(ref):
-        src = ref if cols is None else ref.at[:, cols[0] : cols[1]]
-        copy = pltpu.make_async_copy(src, into, sem)
+def fetch(core, own, other, g, sems, ada_only=False):
+    def go(low, high):
+        if ada_only:
+            copies = [
+                pltpu.make_async_copy(low.at[:, C_ADA:HALF], g.at[:, C_ADA:HALF], sems.at[0]),
+                pltpu.make_async_copy(high.at[:, : C_FC2 - HALF], g.at[:, HALF:C_FC2], sems.at[1]),
+            ]
+        else:
+            copies = [
+                pltpu.make_async_copy(low, g.at[:, :HALF], sems.at[0]),
+                pltpu.make_async_copy(high.at[:, : C_END - HALF], g.at[:, HALF:], sems.at[1]),
+            ]
+        for copy in copies:
+            copy.start()
+        for copy in copies:
+            copy.wait()
+
+    @pl.when(core == 0)
+    def _():
+        go(own, other)
+
+    @pl.when(core != 0)
+    def _():
+        go(other, own)
+
+
+def pack_out(pack, keep, send, sems):
+    copies = [pltpu.make_async_copy(pack.at[i], ref, sems.at[i]) for i, ref in enumerate((keep, send))]
+    for copy in copies:
         copy.start()
+    for copy in copies:
         copy.wait()
 
-    @pl.when(pick)
-    def _():
-        go(first)
-
-    @pl.when(jnp.logical_not(pick))
-    def _():
-        go(second)
+
+def putter(core, pack):
+    def put(half, rows, cols, value):
+        slot = core if half == 0 else 1 - core
+        pack[slot, rows, cols] = value
+
+    return put
 
 
 def front_kernel(core, own, other, x, cond, *refs):
@@ -387,45 +417,39 @@
     y = refs[0]
     k = named(KEEP, refs[1 : 1 + n_keep])
     w = named(WEIGHTS, refs[1 + n_keep : 1 + n_keep + n_w])
-    mod, g, sel, sem = refs[1 + n_keep + n_w :]
-    fetch(core[0] == 0, own, other, g, sem)
+    mod, g, sel, sems = refs[1 + n_keep + n_w :]
+    fetch(core[0], own, other, g, sems)
     unpack(g, sel, w)
     modulate(cond, g, sel, mod)
     forward(x, w, mod, k, y)
 
 
-def turn_kernel(core, own, other, x, cond, grad, y, dx, dc, pack, *refs):
+def turn_kernel(core, own, other, x, cond, grad, y, dx, dc, keep, send, *refs):
     n_keep, n_w, n_t = len(KEEP), len(WEIGHTS), len(TEMPS)
     k = named(KEEP, refs[:n_keep])
     w = named(WEIGHTS, refs[n_keep : n_keep + n_w])
     t = named(TEMPS, refs[n_keep + n_w : n_keep + n_w + n_t])
-    mod, g, sel, sem = refs[n_keep + n_w + n_t :]
-    fetch(core[0] == 1, own, other, g, sem)
+    mod, g, sel, pack, sems = refs[n_keep + n_w + n_t :]
+    fetch(core[0], own, other, g, sems)
     unpack(g, sel, w)
     modulate(cond, g, sel, mod)
     forward(x, w, mod, k, y)
-
-    def put(rows, cols, value):
-        pack[rows, cols] = value
-
-    backward(grad, x, cond, g, sel, w, mod, k, t, dx, dc, put)
+    backward(grad, x, cond, g, sel, w, mod, k, t, dx, dc, putter(core[0], pack))
+    pack_out(pack, keep, send, sems)
 
 
 def back_kernel(core, own, other, x, cond, grad, *refs):
     n_keep, n_w, n_t = len(KEEP), len(WEIGHTS), len(TEMPS)
     k = named(KEEP, refs[:n_keep])
     w = named(WEIGHTS, refs[n_keep : n_keep + n_w])
-    mod, dx, dc, pack = refs[n_keep + n_w : n_keep + n_w + 4]
-    refs = refs[n_keep + n_w + 4 :]
+    mod, dx, dc, keep, send = refs[n_keep + n_w : n_keep + n_w + 5]
+    refs = refs[n_keep + n_w + 5 :]
     t = named(TEMPS, refs[:n_t])
-    g, sel, sem = refs[n_t:]
+    g, sel, pack, sems = refs[n_t:]
     sel[...] = selector()
-    fetch(core[0] == 0, own, other, g.at[:, C_ADA:C_FC2], sem, (C_ADA, C_FC2))
-
-    def put(rows, cols, value):
-        pack[rows, cols] = value
-
-    backward(grad, x, cond, g, sel, w, mod, k, t, dx, dc, put)
+    fetch(core[0], own, other, g, sems, ada_only=True)
+    backward(grad, x, cond, g, sel, w, mod, k, t, dx, dc, putter(core[0], pack))
+    pack_out(pack, keep, send, sems)
 
 
 VM = pl.BlockSpec(memory_space=pltpu.VMEM)
@@ -434,10 +458,15 @@
 PARAMS = pltpu.CompilerParams(vmem_limit_bytes=60 * 1024 * 1024)
 G_BUF = pltpu.VMEM((EXP, C_END), B)
 SEL_BUF = pltpu.VMEM((EXP, D), B)
-SEM = pltpu.SemaphoreType.DMA
+SEMS = pltpu.SemaphoreType.DMA((2,))
 ROWS_OUT = jax.ShapeDtypeStruct((ROWS, D), B)
 COND_OUT = jax.ShapeDtypeStruct((8, D), F)
-PACK_OUT = jax.ShapeDtypeStruct((EXP, C_END), B)
+HALF_OUT = jax.ShapeDtypeStruct((EXP, HALF), B)
+PACK_BUF = pltpu.VMEM((2, EXP, HALF), B)
+
+
+def cost(units):
+    return pl.CostEstimate(flops=units * 2_000_000_000, bytes_accessed=units * 10_000_000, transcendentals=units * 2_000_000)
 
 
 def front(core, own, other, x, cond):
@@ -447,8 +476,9 @@
         out_shape=outs,
         in_specs=[SM, ANY, ANY, VM, VM],
         out_specs=[VM] * len(outs),
-        scratch_shapes=[G_BUF, SEL_BUF, SEM],
+        scratch_shapes=[G_BUF, SEL_BUF, SEMS],
         compiler_params=PARAMS,
+        cost_estimate=cost(1),
         name="front",
     )(core, own, other, x, cond)
 
@@ -456,11 +486,12 @@
 def turn(core, own, other, x, cond, grad):
     return pl.pallas_call(
         turn_kernel,
-        out_shape=[ROWS_OUT, ROWS_OUT, COND_OUT, PACK_OUT],
+        out_shape=[ROWS_OUT, ROWS_OUT, COND_OUT, HALF_OUT, HALF_OUT],
         in_specs=[SM, ANY, ANY, VM, VM, VM],
-        out_specs=[VM] * 4,
-        scratch_shapes=buffers(KEEP) + buffers(WEIGHTS) + buffers(TEMPS) + buffers(MOD) + [G_BUF, SEL_BUF, SEM],
+        out_specs=[VM] * 3 + [ANY] * 2,
+        scratch_shapes=buffers(KEEP) + buffers(WEIGHTS) + buffers(TEMPS) + buffers(MOD) + [G_BUF, SEL_BUF, PACK_BUF, SEMS],
         compiler_params=PARAMS,
+        cost_estimate=cost(3),
         name="turn",
     )(core, own, other, x, cond, grad)
 
@@ -468,11 +499,12 @@
 def back(core, own, other, x, cond, grad, kept):
     return pl.pallas_call(
         back_kernel,
-        out_shape=[ROWS_OUT, COND_OUT, PACK_OUT],
+        out_shape=[ROWS_OUT, COND_OUT, HALF_OUT, HALF_OUT],
         in_specs=[SM, ANY, ANY, VM, VM, VM] + [VM] * len(kept),
-        out_specs=[VM] * 3,
-        scratch_shapes=buffers(TEMPS) + [G_BUF, SEL_BUF, SEM],
+        out_specs=[VM] * 2 + [ANY] * 2,
+        scratch_shapes=buffers(TEMPS) + [G_BUF, SEL_BUF, PACK_BUF, SEMS],
         compiler_params=PARAMS,
+        cost_estimate=cost(2),
         name="back",
     )(core, own, other, x, cond, grad, *kept)
 
@@ -487,7 +519,7 @@
     line = lax.dynamic_update_slice(line, b_ada, (C_ADA + 36 * j,))
     spare = lax.dynamic_update_slice(jnp.zeros((C_FC2,), B), b_fc2, (C_PROJ + 6 * j,))
     top = jnp.concatenate([main, line[None], spare[None]], axis=0)
-    return jnp.concatenate([top, w_fc2[:8], w_fc2[8:16], w_fc2[16:]], axis=1)
+    return jnp.concatenate([top, w_fc2[:8], w_fc2[8:16], w_fc2[16:], jnp.zeros((8, 2 * HALF - C_END), B)], axis=1)
 
 
 def swap(x):
@@ -497,6 +529,10 @@
 def to_all(block):
     copies = jnp.broadcast_to(block[None], (CHIPS, *block.shape))
     return lax.all_to_all(copies, "shard", 0, 0, tiled=True).reshape(EXP, block.shape[1])
+
+
+def scatter(block):
+    return lax.all_to_all(block.reshape(CHIPS, 8, HALF), "shard", 0, 0, tiled=True)
 
 
 def shards(latents, conditions, cotangent, w_qkv, b_qv, w_proj, b_proj, w_fc1, b_fc1, w_fc2, b_fc2, w_ada, b_ada):
@@ -504,16 +540,26 @@
     j = lax.axis_index("shard")
     first = p == 0
     core = p.reshape(1).astype(jnp.int32)
-    own = to_all(line_up(j, w_qkv[0], b_qv[0], w_proj[0], b_proj[0], w_fc1[0], b_fc1[0], w_fc2[0], b_fc2[0], w_ada[0], b_ada[0]))
-    other = swap(own)
+    block = line_up(j, w_qkv[0], b_qv[0], w_proj[0], b_proj[0], w_fc1[0], b_fc1[0], w_fc2[0], b_fc2[0], w_ada[0], b_ada[0])
+    low, high = block[:, :HALF], block[:, HALF:]
+    mine = jnp.where(first, low, high)
+    came = swap(jnp.where(first, high, low))
+    own0 = to_all(jnp.where(first, mine, came))
+    own1 = lax.all_gather(jnp.where(first, came, mine), "shard", tiled=True)
+    other0 = swap(own0)
     x = lax.dynamic_index_in_dim(latents, p, 0, keepdims=False).reshape(ROWS, D)
     cot = lax.dynamic_index_in_dim(cotangent, p, 0, keepdims=False).reshape(ROWS, D)
     cond = lax.dynamic_index_in_dim(conditions, p, 0, keepdims=False).astype(F)
     cond = jnp.concatenate([cond, jnp.zeros((6, D), F)], axis=0)
 
-    h, *kept = front(core, own, other, x, cond)
-    y, dx1, dc1, pack1 = turn(core, own, other, h, cond, cot)
-    dx0, dc0, pack0 = back(core, own, other, x, cond, dx1, kept)
+    h, *kept = front(core, own0, other0, x, cond)
+    h, own1 = lax.optimization_barrier((h, own1))
+    other1 = swap(own1)
+    y, dx1, dc1, keep1, send1 = turn(core, own1, other1, h, cond, cot)
+    parts1 = scatter(keep1 + swap(send1))
+    dx0, dc0, keep0, send0 = back(core, own0, other0, x, cond, dx1, kept)
+    parts1, send0 = lax.optimization_barrier((parts1, send0))
+    parts0 = scatter(keep0 + swap(send0))
 
     def pair(for_first, for_second):
         keep = jnp.where(first, for_first, for_second)
@@ -527,11 +573,11 @@
     dc_other = swap(dc)
     cond_grad = jnp.where(first, jnp.stack([dc, dc_other]), jnp.stack([dc_other, dc]))
 
-    mine = jnp.where(first, pack0, pack1)
-    came = swap(jnp.where(first, pack1, pack0))
-    total = (mine.astype(F) + came.astype(F)).astype(B).reshape(CHIPS, 8, C_END)
-    parts = lax.all_to_all(total, "shard", 0, 0, tiled=True)
-    done = jnp.sum(parts.astype(F), axis=0)
+    sum0 = jnp.sum(parts0.astype(F), axis=0)
+    sum1 = jnp.sum(parts1.astype(F), axis=0)
+    kept_half = jnp.where(first, sum0, sum1)
+    came_half = swap(jnp.where(first, sum1, sum0))
+    done = jnp.concatenate([jnp.where(first, kept_half, came_half), jnp.where(first, came_half, kept_half)], axis=1)[:, :C_END]
 
     rows = done[:6]
     at_qv = jnp.where(j < 32, 12 * j, 12 * j + D)

time: 350 us -> 316 us (0.903)
  blocking collectives: 90.7 us -> 0 us
  starting transfers between devices: 9 us -> 38 us
  between operations: 0.87 us -> 14.3 us
  waiting for transfers between devices: 116 us -> 129 us
    all_to_all x1 -> x0, blocking collectives: 90.7 us -> none  [to_all(): lax.all_to_all(copies, 'shard', 0, 0, tiled=True)]
    all_to_all x1 -> x3, starting transfers between devices: 5.85 us -> 26.7 us  [the longest x2 14.6 us: scatter(): lax.all_to_all(block.reshape(CHIPS, 8, HALF), 'shard', 0, 0, tiled=True)]
    all_gather x0 -> x1, waiting for transfers between devices: none -> 15.6 us  [shards(): own1 = lax.all_gather(jnp.where(first, came, mine), 'shard', tiled=True)]
    ppermute x5 -> x9, starting transfers between devices: 3.15 us -> 11.3 us  [swap(): return lax.ppermute(x, 'pipe', [(0, 1), (1, 0)])]
    select_n x1 -> x4, other arithmetic: 6.43 us -> 1.51 us  [the longest x1 0.83 us: shards(): came = swap(jnp.where(first, high, low))]
    all_to_all x1 -> x3, waiting for transfers between devices: 95.1 us -> 90.3 us  [the longest x2 48.4 us: scatter(): lax.all_to_all(block.reshape(CHIPS, 8, HALF), 'shard', 0, 0, tiled=True)]
    unnamed x16 -> x19, local copies, waits for them, and re-layouts: 0.05 us -> 4.71 us
    ppermute x5 -> x9, waiting for transfers between devices: 20.7 us -> 22.4 us  [swap(): return lax.ppermute(x, 'pipe', [(0, 1), (1, 0)])]
  transfers between devices with their start and end apart: 6 -> 13, of which waited for: 4 -> 9; matrix products, arithmetic and copies ran while one was open for 1% -> 4% of each run, Pallas kernels for 0% -> 17%
where the time goes in v2:
time: 316 us; the launch traced here: 315 us
  waiting for transfers between devices  129 us (41%)
  Pallas kernels  97.9 us (31%)
  starting transfers between devices  38 us (12%)
  other arithmetic  22.5 us (7%)
  between operations  14.3 us (5%)
  local copies, waits for them, and re-layouts  12.9 us (4%)
    all_to_all x2, waiting for transfers between devices, scatter(): lax.all_to_all(block.reshape(CHIPS, 8, HALF), 'shard', 0, 0, tiled=True)  48.4 us
    pallas_call x1, Pallas kernels, turn(): pl.pallas_call(turn_kernel, out_shape=[ROWS_OUT, ROWS_OUT, COND_OUT, HALF...  43.3 us
    all_to_all x1, waiting for transfers between devices, to_all(): lax.all_to_all(copies, 'shard', 0, 0, tiled=True)  41.9 us
    pallas_call x1, Pallas kernels, back(): pl.pallas_call(back_kernel, out_shape=[ROWS_OUT, COND_OUT, HALF_OUT, HALF...  29.4 us
    pallas_call x1, Pallas kernels, front(): pl.pallas_call(front_kernel, out_shape=outs, in_specs=[SM, ANY, ANY, VM,...  25.2 us
    ppermute x9, waiting for transfers between devices, swap(): return lax.ppermute(x, 'pipe', [(0, 1), (1, 0)])  22.4 us
    all_gather x1, waiting for transfers between devices, shards(): own1 = lax.all_gather(jnp.where(first, came, mine), 'shard', tiled=True)  15.6 us
    all_to_all x2, starting transfers between devices, scatter(): lax.all_to_all(block.reshape(CHIPS, 8, HALF), 'shard', 0, 0, tiled=True)  14.6 us
  transfers between devices with their start and end apart: 13, of which 9 were waited for; matrix products, arithmetic and copies ran while one was open for 4% of the time, Pallas kernels for 17%

profile of v2, /device:TPU:1, one launch (start us, length us, event | category | flops | bytes accessed | tf_op | source)
XLA Modules:
  0.0 314.7 jit_solution(15320299345812500756)
XLA Ops:
  15.0 1.5 collective-permute-start
  18.1 2.0 broadcast_in_dim.16
  20.0 12.0 %all-to-all-start = ((bf16[64,8,3328]{2,1,0:T(8,128)(2,1)}), bf16[64,8,3328]{2,1,0:T(8,128)(2,1)}, u32[]{:S(2)}, u32[]{:S(2)}) async-start(bf16[64,8,3328]{2,1,0:T(8,128)(2,1)} %broadcast_in_dim.16), calls=%async_computation | async-start | bytes 6815744 | tf_op jit(solution)/shard_map/all_to_all | solution.py:531
  32.8 41.9 %all-to-all-done = bf16[64,8,3328]{2,1,0:T(8,128)(2,1)} async-done(((bf16[64,8,3328]{2,1,0:T(8,128)(2,1)}), bf16[64,8,3328]{2,1,0:T(8,128)(2,1)}, u32[]{:S(2)}, u32[]{:S(2)}) %all-to-all-start) | async-done | bytes 3407904 | tf_op jit(solution)/shard_map/all_to_all | solution.py:531
  74.7 2.2 collective-permute-start.1
  78.3 4.6 %collective-permute-done.1.other = bf16[512,3328]{1,0:T(8,128)(2,1)} collective-permute-done((bf16[512,3328]{1,0:T(8,128)(2,1)}, bf16[512,3328]{1,0:T(8,128)(2,1)}, u32[]{:S(2)}, u32[]{:S(2)}) %collective-permute-start.1) | collective-permute-done | bytes 3407904 | tf_op jit(solution)/shard_map/ppermute | solution.py:526
  82.9 25.2 %front.1 = (bf16[512,384]{1,0:T(8,128)(2,1)}, bf16[512,384]{1,0:T(8,128)(2,1)}, bf16[512,1152]{1,0:T(8,128)(2,1)}, f32[6,8,256]{2,1,0:T(8,128)}, bf16[512,384]{1...) custom-call(s32[1]{0:T(128)} %bitcast.core, ...), custom_call_target="tpu_custom_call" | custom-call | flops 2000000000 | bytes 10000000 | tf_op jit(solution)/shard_map/front/pallas_call | solution.py:474
  108.1 15.6 %all-gather.2.cloned.1.call-done.own = bf16[512,3328]{1,0:T(8,128)(2,1)} async-done(((bf16[8,3328]{1,0:T(8,128)(2,1)}), bf16[512,3328]{1,0:T(8,128)(2,1)}) %all-gather.2.cloned.1.call-update) | async-done | bytes 3407888 | tf_op jit(solution)/shard_map/all_gather | solution.py:548
  123.8 1.5 collective-permute-start.2
  126.0 5.2 %collective-permute-done.2.other = bf16[512,3328]{1,0:T(8,128)(2,1)} collective-permute-done((bf16[512,3328]{1,0:T(8,128)(2,1)}, bf16[512,3328]{1,0:T(8,128)(2,1)}, u32[]{:S(2)}, u32[]{:S(2)}) %collective-permute-start.2) | collective-permute-done | bytes 3407904 | tf_op jit(solution)/shard_map/ppermute | solution.py:526
  131.2 43.3 %turn.1 = (bf16[512,384]{1,0:T(8,128)(2,1)}, bf16[512,384]{1,0:T(8,128)(2,1)}, f32[8,384]{1,0:T(8,128)}, bf16[512,3328]{1,0:T(8,128)(2,1)}, bf16[512,3328]{1,0:T(8,128)(2,1)}) custom-call(s32[1]{0:T(128)} %bitcast.core, bf16[512,3328]{1,0:T(8,128)(2,1)} %all-gather.2.cloned.1.call-done.own, bf16[512,3328]{1,0:T(8,128)(2,1)} %collective-permute-done.2.other, ...), custom_call_target="tpu_custom_call" | custom-call | flops 6000000000 | bytes 30000000 | tf_op jit(solution)/shard_map/turn/pallas_call | solution.py:487
  175.0 5.9 %collective-permute-done.6 = bf16[512,3328]{1,0:T(8,128)(2,1)S(1)} collective-permute-done((bf16[512,3328]{1,0:T(8,128)(2,1)}, bf16[512,3328]{1,0:T(8,128)(2,1)S(1)}, u32[]{:S(2)}, u32[]{:S(2)}) %collective-permute-start.6) | collective-permute-done | bytes 3407904 | tf_op jit(solution)/shard_map/ppermute | solution.py:526
  180.8 4.1 %add_bitcast_fusion.1 = bf16[64,8,3328]{2,1,0:T(8,128)(2,1)} fusion(bf16[512,3328]{1,0:T(8,128)(2,1)} %get-tuple-element.66, bf16[512,3328]{1,0:T(8,128)(2,1)S(1)} %collective-permute-done.6), kind=kLoop, calls=%fused_computation.3 | loop fusion | flops 1703936 | bytes 10223616 | tf_op jit(solution)/shard_map/reshape | solution.py:535
  185.0 6.5 %all-to-all-start.1 = ((bf16[64,8,3328]{2,1,0:T(8,128)(2,1)}), bf16[64,8,3328]{2,1,0:T(8,128)(2,1)S(1)}, u32[]{:S(2)}, u32[]{:S(2)}) async-start(bf16[64,8,3328]{2,1,0:T(8,128)(2,1)} %add_bitcast_fusion.1), calls=%async_computation.1 | async-start | bytes 6815744 | tf_op jit(solution)/shard_map/all_to_all | solution.py:535
  191.5 29.4 %back.1 = (bf16[512,384]{1,0:T(8,128)(2,1)}, f32[8,384]{1,0:T(8,128)}, bf16[512,3328]{1,0:T(8,128)(2,1)}, bf16[512,3328]{1,0:T(8,128)(2,1)}) custom-call(s32[1]{0:T(128)} %bitcast.core, bf16[512,3328]{1,0:T(8,128)(2,1)} %bitcast.8.own, bf16[512,3328]{1,0:T(8,128)(2,1)} %collective-permute-done.1.other, bf16[512,384]{1,0:T(8,128)(2,1)} %bitcast.42, ...), custom_call_target="tpu_custom_call" | custom-call | flops 4000000000 | bytes 20000000 | tf_op jit(solution)/shard_map/back/pallas_call | solution.py:500
  220.9 12.8 %all-to-all-done.1 = bf16[64,8,3328]{2,1,0:T(8,128)(2,1)S(1)} async-done(((bf16[64,8,3328]{2,1,0:T(8,128)(2,1)}), bf16[64,8,3328]{2,1,0:T(8,128)(2,1)S(1)}, u32[]{:S(2)}, u32[]{:S(2)}) %all-to-all-start.1) | async-done | bytes 3407904 | tf_op jit(solution)/shard_map/all_to_all | solution.py:535
  233.7 2.1 collective-permute-start.7
  235.9 5.9 %collective-permute-done.7 = bf16[512,3328]{1,0:T(8,128)(2,1)S(1)} collective-permute-done((bf16[512,3328]{1,0:T(8,128)(2,1)}, bf16[512,3328]{1,0:T(8,128)(2,1)S(1)}, u32[]{:S(2)}, u32[]{:S(2)}) %collective-permute-start.7) | collective-permute-done | bytes 3407904 | tf_op jit(solution)/shard_map/ppermute | solution.py:526
  241.7 4.2 %add_bitcast_fusion = bf16[64,8,3328]{2,1,0:T(8,128)(2,1)} fusion(bf16[512,3328]{1,0:T(8,128)(2,1)} %get-tuple-element.65, bf16[512,3328]{1,0:T(8,128)(2,1)S(1)} %collective-permute-done.7), kind=kLoop, calls=%fused_computation.2 | loop fusion | flops 1703936 | bytes 10223616 | tf_op jit(solution)/shard_map/reshape | solution.py:535
  245.9 8.1 %all-to-all-start.2 = ((bf16[64,8,3328]{2,1,0:T(8,128)(2,1)}), bf16[64,8,3328]{2,1,0:T(8,128)(2,1)}, u32[]{:S(2)}, u32[]{:S(2)}) async-start(bf16[64,8,3328]{2,1,0:T(8,128)(2,1)} %add_bitcast_fusion), calls=%async_computation.2 | async-start | bytes 6815744 | tf_op jit(solution)/shard_map/all_to_all | solution.py:535
  254.1 1.3 broadcast_select_fusion.1
  260.8 35.6 %all-to-all-done.2 = bf16[64,8,3328]{2,1,0:T(8,128)(2,1)} async-done(((bf16[64,8,3328]{2,1,0:T(8,128)(2,1)}), bf16[64,8,3328]{2,1,0:T(8,128)(2,1)}, u32[]{:S(2)}, u32[]{:S(2)}) %all-to-all-start.2) | async-done | bytes 3407904 | tf_op jit(solution)/shard_map/all_to_all | solution.py:535
  296.4 2.5 convert_reduce_fusion.1
  298.8 2.2 collective-permute-start.8
  (64 shorter events, 24.8 us)
Async XLA Ops:
  7.2 70.3 %copy-start = (bf16[2,2,256,384]{3,2,1,0:T(8,128)(2,1)S(1)}, bf16[2,2,256,384]{3,2,1,0:T(8,128)(2,1)}, u32[]{:S(2)}) copy-start(bf16[2,2,256,384]{3,2,1,0:T(8,128)(2,1)} %param.13) | copy-start | bytes 2359300
  15.0 2.4 collective-permute-start
  20.0 56.8 %copy-start.5 = (bf16[2,2,384]{2,1,0:T(2,128)(2,1)S(1)}, bf16[2,2,384]{2,1,0:T(2,128)(2,1)}, u32[]{:S(2)}) copy-start(bf16[2,2,384]{2,1,0:T(2,128)(2,1)} %param.14) | copy-start | bytes 9220
  20.0 54.7 %all-to-all-start = ((bf16[64,8,3328]{2,1,0:T(8,128)(2,1)}), bf16[64,8,3328]{2,1,0:T(8,128)(2,1)}, u32[]{:S(2)}, u32[]{:S(2)}) async-start(bf16[64,8,3328]{2,1,0:T(8,128)(2,1)} %broadcast_in_dim.16), calls=%async_computation | async-start | bytes 6815744 | tf_op jit(solution)/shard_map/all_to_all | solution.py:531
  32.1 91.7 %all-gather.2.cloned.1.call-start = ((), (), s32[]{:S(2)}) async-start(), calls=%async_computation.3 | async-start | bytes 3461120 | tf_op jit(solution)/shard_map/all_gather | solution.py:548
  74.7 8.2 %collective-permute-start.1 = (bf16[512,3328]{1,0:T(8,128)(2,1)}, bf16[512,3328]{1,0:T(8,128)(2,1)}, u32[]{:S(2)}, u32[]{:S(2)}) collective-permute-start(bf16[512,3328]{1,0:T(8,128)(2,1)} %bitcast.8.own), channel_id=1, source_target_pairs={{0,64},{64,0},{1,65},{65,1},{2,66},{66,2},{3,67},{67,3},{4,68},{68... | collective-permute-start | bytes 10223624 | tf_op jit(solution)/shard_map/ppermute | solution.py:526
  82.9 42.4 %copy-start.4 = (bf16[2,2,256,384]{3,2,1,0:T(8,128)(2,1)S(1)}, bf16[2,2,256,384]{3,2,1,0:T(8,128)(2,1)}, u32[]{:S(2)}) copy-start(bf16[2,2,256,384]{3,2,1,0:T(8,128)(2,1)} %param.15) | copy-start | bytes 2359300
  123.8 7.5 %collective-permute-start.2 = (bf16[512,3328]{1,0:T(8,128)(2,1)}, bf16[512,3328]{1,0:T(8,128)(2,1)}, u32[]{:S(2)}, u32[]{:S(2)}) collective-permute-start(bf16[512,3328]{1,0:T(8,128)(2,1)} %all-gather.2.cloned.1.call-done.own), channel_id=1, source_target_pairs={{0,64},{64,0},{1,65},{65,1},{2,66},{66,2},{3,67},{67,3},{4,68},{68... | collective-permute-start | bytes 10223624 | tf_op jit(solution)/shard_map/ppermute | solution.py:526
  174.5 6.3 %collective-permute-start.6 = (bf16[512,3328]{1,0:T(8,128)(2,1)}, bf16[512,3328]{1,0:T(8,128)(2,1)S(1)}, u32[]{:S(2)}, u32[]{:S(2)}) collective-permute-start(bf16[512,3328]{1,0:T(8,128)(2,1)} %get-tuple-element.67), channel_id=1, source_target_pairs={{0,64},{64,0},{1,65},{65,1},{2,66},{66,2},{3,67},{67,3},{4,68},{68... | collective-permute-start | bytes 10223624 | tf_op jit(solution)/shard_map/ppermute | solution.py:526
  185.0 48.7 %all-to-all-start.1 = ((bf16[64,8,3328]{2,1,0:T(8,128)(2,1)}), bf16[64,8,3328]{2,1,0:T(8,128)(2,1)S(1)}, u32[]{:S(2)}, u32[]{:S(2)}) async-start(bf16[64,8,3328]{2,1,0:T(8,128)(2,1)} %add_bitcast_fusion.1), calls=%async_computation.1 | async-start | bytes 6815744 | tf_op jit(solution)/shard_map/all_to_all | solution.py:535
  233.7 12.2 %copy-start.2 = (bf16[64,8,3328]{2,1,0:T(8,128)(2,1)}, bf16[64,8,3328]{2,1,0:T(8,128)(2,1)S(1)}, u32[]{:S(2)}) copy-start(bf16[64,8,3328]{2,1,0:T(8,128)(2,1)S(1)} %all-to-all-done.1) | copy-start | bytes 10223620
  233.7 8.0 %collective-permute-start.7 = (bf16[512,3328]{1,0:T(8,128)(2,1)}, bf16[512,3328]{1,0:T(8,128)(2,1)S(1)}, u32[]{:S(2)}, u32[]{:S(2)}) collective-permute-start(bf16[512,3328]{1,0:T(8,128)(2,1)} %get-tuple-element.69), channel_id=1, source_target_pairs={{0,64},{64,0},{1,65},{65,1},{2,66},{66,2},{3,67},{67,3},{4,68},{68... | collective-permute-start | bytes 10223624 | tf_op jit(solution)/shard_map/ppermute | solution.py:526
  245.9 50.4 %all-to-all-start.2 = ((bf16[64,8,3328]{2,1,0:T(8,128)(2,1)}), bf16[64,8,3328]{2,1,0:T(8,128)(2,1)}, u32[]{:S(2)}, u32[]{:S(2)}) async-start(bf16[64,8,3328]{2,1,0:T(8,128)(2,1)} %add_bitcast_fusion), calls=%async_computation.2 | async-start | bytes 6815744 | tf_op jit(solution)/shard_map/all_to_all | solution.py:535
  254.1 6.2 %copy-start.3 = (bf16[64,8,3328]{2,1,0:T(8,128)(2,1)S(1)}, bf16[64,8,3328]{2,1,0:T(8,128)(2,1)}, u32[]{:S(2)}) copy-start(bf16[64,8,3328]{2,1,0:T(8,128)(2,1)} %copy-done.2) | copy-start | bytes 10223620
  255.4 3.9 %collective-permute-start.4 = (bf16[512,384]{1,0:T(8,128)(2,1)S(1)}, bf16[512,384]{1,0:T(8,128)(2,1)S(1)}, u32[]{:S(2)}, u32[]{:S(2)}) collective-permute-start(bf16[512,384]{1,0:T(8,128)(2,1)S(1)} %get-tuple-element.87), channel_id=1, source_target_pairs={{0,64},{64,0},{1,65},{65,1},{2,66},{66,2},{3,67},{67,3},{4,68},{68... | collective-permute-start | bytes 1179656 | tf_op jit(solution)/shard_map/ppermute | solution.py:526
  256.9 1.8 collective-permute-start.5
  258.1 43.0 %collective-permute-start.3 = (bf16[512,384]{1,0:T(8,128)(2,1)S(1)}, bf16[512,384]{1,0:T(8,128)(2,1)S(1)}, u32[]{:S(2)}, u32[]{:S(2)}) collective-permute-start(bf16[512,384]{1,0:T(8,128)(2,1)S(1)} %get-tuple-element.89), channel_id=1, source_target_pairs={{0,64},{64,0},{1,65},{65,1},{2,66},{66,2},{3,67},{67,3},{4,68},{68... | collective-permute-start | bytes 1179656 | tf_op jit(solution)/shard_map/ppermute | solution.py:526
  260.3 47.5 %copy-start.1 = (bf16[2,2,256,384]{3,2,1,0:T(8,128)(2,1)S(1)}, bf16[2,2,256,384]{3,2,1,0:T(8,128)(2,1)}, u32[]{:S(2)}) copy-start(bf16[2,2,256,384]{3,2,1,0:T(8,128)(2,1)} %param.13) | copy-start | bytes 2359300
  298.8 3.3 %collective-permute-start.8 = (f32[8,3328]{1,0:T(8,128)S(1)}, f32[8,3328]{1,0:T(8,128)S(1)}, u32[]{:S(2)}, u32[]{:S(2)}) collective-permute-start(f32[8,3328]{1,0:T(8,128)S(1)} %broadcast_select_fusion.6), channel_id=1, source_target_pairs={{0,64},{64,0},{1,65},{65,1},{2,66},{66,2},{3,67},{67,3},{4,68},{68... | collective-permute-start | bytes 319496 | tf_op jit(solution)/shard_map/ppermute | solution.py:526
Sparse Core Ops, SparseCore 0:
  36.4 87.3 all-gather.1

commit v3 on v2

v3 whole, which is shorter than its diff:
```python
import functools

import jax
import jax.numpy as jnp
from jax import lax
from jax.experimental import pallas as pl
from jax.experimental.pallas import tpu as pltpu
from jax.sharding import PartitionSpec as P

F = jnp.float32
B = jnp.bfloat16
D = 384
HEADS = 6
HEAD = 64
FF = 1536
SEQ = 256
EPS = 1e-06
CHIPS = 64
ROWS = 512
EXP = 512

C_QKV, C_PROJ, C_FC1, C_MAIN = 0, 1152, 1536, 3072
QUARTER = 768

G_FC2, G_ADA, G_BIAS, G_END = 2304, 3456, 5248, 5376
G_HALF = 2688
BIASES = ((0, 12), (12, 6), (18, 24), (42, 6), (48, 36))

P_HALF = 2560
P_DB0 = 2304
P_MOD, P_DB1, P_COND = 1152, 2304, 2432
SHIFTS = (0, 6, 4, 2)

K0 = 0.7978845608028654
K1 = 0.044715

NN = (1, 0)
NT = (1, 1)
TN = (0, 0)


def dot(a, b, dims=NN):
    return lax.dot_general(a, b, (((dims[0],), (dims[1],)), ((), ())), preferred_element_type=F)


def targets(shape, dim, shift):
    at = lax.broadcasted_iota(jnp.int32, shape, dim)
    r = ((at & 7) + (8 - shift)) & 7
    return jnp.where(r < 6, (at >> 3) * 6 + r, -1)


def build_selectors(sel, selt):
    col = lax.broadcasted_iota(jnp.int32, (1, D), 1)
    row = lax.broadcasted_iota(jnp.int32, (D, 1), 0)
    for i, shift in enumerate(SHIFTS):
        sel[i] = (targets((EXP, 1), 0, shift) == col).astype(F).astype(B)
        selt[i] = (row == targets((1, EXP), 1, shift)).astype(F).astype(B)


def group_of(n, width):
    return jnp.floor((n.astype(F) + 0.5) * (1.0 / width)).astype(jnp.int32)


def natural_bias(gb, lane, width):
    n = CHIPS * width
    at = lax.broadcasted_iota(jnp.int32, (1, n), 1)
    owner = group_of(at, width)
    spot = at - owner * width + lane
    pick = (lax.broadcasted_iota(jnp.int32, (128, 1), 0) == spot).astype(F).astype(B)
    wide = dot(gb, pick)
    return jnp.sum(jnp.where(lax.broadcasted_iota(jnp.int32, (CHIPS, 1), 0) == owner, wide, 0.0), axis=0, keepdims=True)


def tile_row(shape, dim):
    return lax.broadcasted_iota(jnp.int32, shape, dim) & 7


def stats(v):
    centre = v - jnp.mean(v, axis=-1, keepdims=True)
    inv = lax.rsqrt(jnp.mean(centre * centre, axis=-1, keepdims=True) + EPS)
    return centre * inv, inv


def norm_back(g, n, inv):
    mg = jnp.mean(g, axis=-1, keepdims=True)
    mgn = jnp.mean(g * n, axis=-1, keepdims=True)
    return inv * (g - mg - n * mgn)


def head_masks():
    lane = lax.broadcasted_iota(jnp.int32, (1, 128), 1)
    low = (lane < HEAD).astype(F)
    return low.astype(B), (1.0 - low).astype(B)


def unpack(g, selt, w):
    r8 = tile_row((EXP, 1), 0)

    def piece(a, c):
        return g[:, a * QUARTER + c : a * QUARTER + c + 384]

    def merge(edge, a, c):
        return jnp.where(r8 >= edge, piece(a, c).astype(F), piece(a + 1, c).astype(F)).astype(B)

    for c in (0, 384):
        w["main"][:, c : c + 384] = dot(selt[0], piece(0, c)).astype(B)
        w["main"][:, QUARTER + c : QUARTER + c + 384] = dot(selt[1], merge(6, 0, c)).astype(B)
        w["main"][:, 2 * QUARTER + c : 2 * QUARTER + c + 384] = dot(selt[2], merge(4, 1, c)).astype(B)
        w["main"][:, 3 * QUARTER + c : 3 * QUARTER + c + 384] = dot(selt[3], piece(2, c)).astype(B)

    lead = (lax.broadcasted_iota(jnp.int32, (CHIPS, EXP), 0) * 8 == lax.broadcasted_iota(jnp.int32, (CHIPS, EXP), 1)).astype(F).astype(B)
    gb = dot(lead, g[:, G_BIAS:G_END]).astype(B)
    qv, proj, fc1, fc2, ada = (natural_bias(gb, lane, width) for lane, width in BIASES)
    w["bias"][:, :D] = qv[:, :D]
    w["bias"][:, D : 2 * D] = jnp.zeros((1, D), F)
    w["bias"][:, 2 * D : C_PROJ] = qv[:, D:]
    w["bias"][:, C_PROJ:C_FC1] = proj
    w["bias"][:, C_FC1:C_MAIN] = fc1
    w["bias2"][...] = fc2

    def step2(i, _):
        at = pl.multiple_of(i * 128, 128)
        parts = [g[pl.ds(at, 128), G_FC2 + a * D : G_FC2 + (a + 1) * D].astype(F).reshape(16, 8, D) for a in range(3)]
        whole = jnp.concatenate(parts, axis=1).reshape(D, D).astype(B)
        w["fc2"][pl.ds(pl.multiple_of(i * D, D), D), :] = whole
        return 0

    lax.fori_loop(0, 4, step2, 0)
    return ada


def ada_groups():
    return [(i % 4, (6 * i) // 8, SHIFTS[i % 4] in (6, 4)) for i in range(9)]


def modulate(cond, g, selt, ada, mod):
    c = cond[...]
    act = (c * jax.nn.sigmoid(c)).astype(B)
    r8 = tile_row((1, EXP), 1)
    wides = [dot(act, selt[i]) for i in range(4)]
    for n, (i, a, more) in enumerate(ada_groups()):
        at = G_ADA + a * 256
        first = jnp.where(r8 >= SHIFTS[i], wides[i], 0.0).astype(B)
        part = dot(first, g[:, at : at + 256])
        if more:
            part = part + dot(jnp.where(r8 < SHIFTS[i], wides[i], 0.0).astype(B), g[:, at + 256 : at + 512])
        mod[:, n * 256 : (n + 1) * 256] = part + ada[:, n * 256 : (n + 1) * 256]


def cond_back(dm, g, g_at, selt):
    r8 = tile_row((1, EXP), 1)
    sums = [jnp.zeros((8, EXP), F)] * 4
    for n, (i, a, more) in enumerate(ada_groups()):
        at = g_at + a * 256
        piece = dm[:, n * 256 : (n + 1) * 256]
        sums[i] = sums[i] + jnp.where(r8 >= SHIFTS[i], dot(piece, g[:, at : at + 256], NT), 0.0)
        if more:
            sums[i] = sums[i] + jnp.where(r8 < SHIFTS[i], dot(piece, g[:, at + 256 : at + 512], NT), 0.0)
    total = jnp.zeros((8, D), F)
    for i in range(4):
        rest = sums[i]
        for _ in range(3):
            level = rest.astype(B)
            rest = rest - level.astype(F)
            total = total + dot(level, selt[i], NT)
    return total


def forward(x, w, mod, k, y):
    main, bias, fc2 = w["main"], w["bias"], w["fc2"]

    def ln_in(i, _):
        rows = pl.ds(pl.multiple_of(i * 128, 128), 128)
        lat = pl.ds(i // 2, 1)
        n, _ = stats(x[rows, :].astype(F))
        k["ain"][rows, :] = (n * (1.0 + mod[lat, D : 2 * D]) + mod[lat, :D]).astype(B)
        return 0

    lax.fori_loop(0, 4, ln_in, 0)

    for c in range(3):
        cs = slice(c * D, (c + 1) * D)
        k["qkv"][:, cs] = (dot(k["ain"][...], main[:, cs]) + bias[:, cs]).astype(B)

    low, high = head_masks()

    def attend(i, _):
        rows = pl.ds(pl.multiple_of((i // 3) * SEQ, SEQ), SEQ)
        at = (i % 3) * 128
        q = k["qkv"][rows, pl.ds(pl.multiple_of(at, 128), 128)]
        key = k["qkv"][rows, pl.ds(pl.multiple_of(D + at, 128), 128)]
        v = k["qkv"][rows, pl.ds(pl.multiple_of(2 * D + at, 128), 128)]
        total = None
        for h, m in enumerate((low, high)):
            s = dot(key, q * m, NT) * 0.125
            top = jnp.max(s, axis=0, keepdims=True)
            e = jnp.exp(s - top)
            t = jnp.sum(e, axis=0, keepdims=True)
            p = (e * (1.0 / t)).astype(B)
            k["lse"][i, h : h + 1, :] = top + jnp.log(t)
            part = dot(p, v * m, TN)
            total = part if total is None else total + part
        k["att"][rows, pl.ds(pl.multiple_of(at, 128), 128)] = total.astype(B)
        return 0

    lax.fori_loop(0, 6, attend, 0)

    def mid(i, _):
        rows = pl.ds(pl.multiple_of(i * 128, 128), 128)
        lat = pl.ds(i // 2, 1)
        o = dot(k["att"][rows, :], main[:, C_PROJ:C_FC1]) + bias[:, C_PROJ:C_FC1]
        x1 = x[rows, :].astype(F) + mod[lat, 2 * D : 3 * D] * o
        k["o"][rows, :] = o
        k["x1"][rows, :] = x1
        n, _ = stats(x1)
        k["min"][rows, :] = (n * (1.0 + mod[lat, 4 * D : 5 * D]) + mod[lat, 3 * D : 4 * D]).astype(B)
        return 0

    lax.fori_loop(0, 4, mid, 0)

    def mlp(i, _):
        at = pl.multiple_of(i * 256, 256)
        cs = pl.ds(at, 256)
        ws = pl.ds(pl.multiple_of(C_FC1 + at, 256), 256)
        z = dot(k["min"][...], main[:, ws]) + bias[:, ws]
        zz = z * z
        t = jnp.tanh(z * (K0 + K0 * K1 * zz))
        half = 0.5 + 0.5 * t
        k["act"][:, cs] = (z * half).astype(B)
        k["slope"][:, cs] = half + (0.5 * z) * (1.0 - t * t) * (K0 + 3.0 * K0 * K1 * zz)
        return 0

    lax.fori_loop(0, 6, mlp, 0)

    def out(i, _):
        rows = pl.ds(pl.multiple_of(i * 128, 128), 128)
        lat = pl.ds(i // 2, 1)
        f = dot(k["act"][rows, :], fc2[...]) + w["bias2"][...]
        k["f"][rows, :] = f
        y[rows, :] = (k["x1"][rows, :] + mod[lat, 5 * D : 6 * D] * f).astype(B)
        return 0

    lax.fori_loop(0, 4, out, 0)


def token_sum(v):
    return jnp.sum(v, axis=0, keepdims=True)


def spread(sel, i, v):
    return dot(sel[i], v, NT).astype(B)


def backward(core, grad, x, cond, g, g_at, sel, selt, w, mod, k, t, dx, dc, put):
    main, fc2 = w["main"], w["fc2"]
    dmod = t["dmod"]
    dmod[...] = jnp.zeros_like(dmod)

    def add_mod(lat, piece, v):
        cs = slice(piece * D, (piece + 1) * D)
        dmod[lat, cs] = dmod[lat, cs] + v

    t["db"][...] = jnp.zeros_like(t["db"])
    r8 = tile_row((EXP, 1), 0)

    def add_db(at, v):
        t["db"][:, at : at + v.shape[1]] = t["db"][:, at : at + v.shape[1]] + v


    def start(i, _):
        rows = pl.ds(pl.multiple_of(i * 128, 128), 128)
        lat = pl.ds(i // 2, 1)
        gr = grad[rows, :].astype(F)
        df = (gr * mod[lat, 5 * D : 6 * D]).astype(B)
        t["df"][rows, :] = df
        add_mod(lat, 5, token_sum(gr * k["f"][rows, :]))
        add_db(2688, token_sum(df.astype(F)))
        return 0

    lax.fori_loop(0, 4, start, 0)

    def dmlp(i, _):
        cs = pl.ds(pl.multiple_of(i * 256, 256), 256)
        da = dot(t["df"][...], fc2[cs, :], NT)
        dz = (da * k["slope"][:, cs]).astype(B)
        t["dz"][:, cs] = dz
        ds = pl.ds(pl.multiple_of(1152 + i * 256, 128), 256)
        t["db"][:, ds] = token_sum(dz.astype(F))
        return 0

    lax.fori_loop(0, 6, dmlp, 0)

    t["wide2"][...] = spread(sel, 2, k["min"][...])
    t["wide"][...] = spread(sel, 3, k["min"][...])
    for c in range(0, QUARTER, 256):
        d2 = dot(t["wide2"][...], t["dz"][:, c : c + 256])
        d3 = dot(t["wide"][...], t["dz"][:, QUARTER + c : QUARTER + c + 256])
        put(0, slice(0, EXP), slice(2 * QUARTER + c, 2 * QUARTER + c + 256), jnp.where(r8 < 2, d2, d3).astype(B))
        t["part"][:, c : c + 256] = d2

    for c in range(4):
        part = dot(k["act"][:, c * D : (c + 1) * D], t["df"][...], TN).reshape(16, 24, D)
        for a in range(3):
            put(
                1,
                slice(c * 128, (c + 1) * 128),
                slice(a * D, (a + 1) * D),
                part[:, 8 * a : 8 * a + 8, :].reshape(128, D).astype(B),
            )

    def dmid(i, _):
        rows = pl.ds(pl.multiple_of(i * 128, 128), 128)
        lat = pl.ds(i // 2, 1)
        dmin = dot(t["dz"][rows, :], main[:, C_FC1:C_MAIN], NT)
        n, inv = stats(k["x1"][rows, :])
        add_mod(lat, 4, token_sum(dmin * n))
        add_mod(lat, 3, token_sum(dmin))
        d1 = grad[rows, :].astype(F) + norm_back(dmin * (1.0 + mod[lat, 4 * D : 5 * D]), n, inv)
        t["dx1"][rows, :] = d1
        do = (d1 * mod[lat, 2 * D : 3 * D]).astype(B)
        add_mod(lat, 2, token_sum(d1 * k["o"][rows, :]))
        t["df"][rows, :] = do
        add_db(768, token_sum(do.astype(F)))
        t["datt"][rows, :] = dot(do, main[:, C_PROJ:C_FC1], NT).astype(B)
        return 0

    lax.fori_loop(0, 4, dmid, 0)

    t["wide2"][...] = spread(sel, 1, k["att"][...])
    d1 = dot(t["wide2"][...], t["df"][...])
    put(0, slice(0, EXP), slice(QUARTER + 384, 2 * QUARTER), jnp.where(r8 < 4, d1, t["part"][:, 384:]).astype(B))
    t["part2"][...] = d1

    low, high = head_masks()

    def dattend(i, _):
        rows = pl.ds(pl.multiple_of((i // 3) * SEQ, SEQ), SEQ)
        at = (i % 3) * 128
        qs = pl.ds(pl.multiple_of(at, 128), 128)
        ks = pl.ds(pl.multiple_of(D + at, 128), 128)
        vs = pl.ds(pl.multiple_of(2 * D + at, 128), 128)
        q = k["qkv"][rows, qs]
        key = k["qkv"][rows, ks]
        v = k["qkv"][rows, vs]
        da = t["datt"][rows, qs]
        dq = dk = dv = None
        for h, m in enumerate((low, high)):
            qm = q * m
            dam = da * m
            s = dot(key, qm, NT) * 0.125
            p = jnp.exp(s - k["lse"][i, h : h + 1, :])
            dp = dot(v, dam, NT)
            ds = (p * (dp - jnp.sum(p * dp, axis=0, keepdims=True))).astype(B)
            v1 = dot(p.astype(B), dam)
            k1 = dot(ds, qm)
            q1 = dot(ds, key * m, TN)
            dv = v1 if dv is None else dv + v1
            dk = k1 if dk is None else dk + k1
            dq = q1 if dq is None else dq + q1
        t["dqkv"][rows, qs] = (dq * 0.125).astype(B)
        t["dqkv"][rows, ks] = (dk * 0.125).astype(B)
        t["dqkv"][rows, vs] = dv.astype(B)
        return 0

    lax.fori_loop(0, 6, dattend, 0)

    t["wide"][...] = spread(sel, 0, k["ain"][...])
    t["wide2"][...] = spread(sel, 1, k["ain"][...])
    d1 = dot(t["wide2"][...], t["dqkv"][:, QUARTER:])
    d0 = dot(t["wide"][...], t["dqkv"][:, :384])
    put(0, slice(0, EXP), slice(0, 384), jnp.where(r8 < 6, d0, d1).astype(B))
    put(0, slice(0, EXP), slice(QUARTER, QUARTER + 384), jnp.where(r8 < 4, d1, t["part"][:, :384]).astype(B))
    d0 = dot(t["wide"][...], t["dqkv"][:, 384:QUARTER])
    put(0, slice(0, EXP), slice(384, QUARTER), jnp.where(r8 < 6, d0, t["part2"][...]).astype(B))

    def bias_sums(i, _):
        rows = pl.ds(pl.multiple_of(i * 128, 128), 128)
        add_db(0, token_sum(t["dqkv"][rows, :D].astype(F)))
        add_db(D, token_sum(t["dqkv"][rows, 2 * D :].astype(F)))
        return 0

    lax.fori_loop(0, 4, bias_sums, 0)

    def dlast(i, _):
        rows = pl.ds(pl.multiple_of(i * 128, 128), 128)
        lat = pl.ds(i // 2, 1)
        dain = dot(t["dqkv"][rows, :], main[:, C_QKV:C_PROJ], NT)
        n, inv = stats(x[rows, :].astype(F))
        add_mod(lat, 1, token_sum(dain * n))
        add_mod(lat, 0, token_sum(dain))
        back = norm_back(dain * (1.0 + mod[lat, D : 2 * D]), n, inv)
        dx[rows, :] = (t["dx1"][rows, :] + back).astype(B)
        return 0

    lax.fori_loop(0, 4, dlast, 0)

    c = cond[...]
    sig = jax.nn.sigmoid(c)
    act = c * sig
    dm = dmod[...].astype(B).astype(F)
    dc[...] = cond_back(dm.astype(B), g, g_at, selt) * (sig * (1.0 + c * (1.0 - sig)))

    mine = 2 * core
    block = pltpu.roll(dm[:, :1152], mine, 0) + pltpu.roll(dm[:, 1152:], mine + 4, 0)
    for q in range(4):
        rows = slice(q * 128, (q + 1) * 128)
        put(1, rows, slice(P_MOD, P_DB1), jnp.broadcast_to(block[None], (16, 8, 1152)).reshape(128, 1152).astype(B))

    db = t["db"]
    for half, at, first in ((0, P_DB0, 0), (0, P_DB0 + 128, 8), (1, P_DB1, 16)):
        rows = jnp.concatenate([db[:, (first + i) * 128 : (first + i + 1) * 128] for i in range(8)], axis=0)
        put(half, slice(0, EXP), slice(at, at + 128), jnp.broadcast_to(rows[None], (CHIPS, 8, 128)).reshape(EXP, 128).astype(B))

    act = act.astype(B).astype(F)
    both = pltpu.roll(act, mine, 0) + pltpu.roll(act, mine + 4, 0)
    both = jnp.broadcast_to(both[None], (CHIPS, 8, D)).reshape(EXP, D)
    feature = lax.broadcasted_iota(jnp.int32, (1, D), 1)
    device = lax.broadcasted_iota(jnp.int32, (EXP, 1), 0) >> 3
    both = jnp.where(group_of(feature, 6) == device, both, 0.0).astype(B)
    feature = lax.broadcasted_iota(jnp.int32, (D, 1), 0)
    lane = lax.broadcasted_iota(jnp.int32, (1, 128), 1)
    pick = ((feature - 6 * group_of(feature, 6)) == (lane & 7)) & (lane < 16)
    found = dot(both, pick.astype(F).astype(B))
    put(1, slice(0, EXP), slice(P_COND, P_HALF), jnp.where((r8 >> 2) == (lane >> 3), found, 0.0).astype(B))


KEEP = (
    ("ain", (ROWS, D), B),
    ("qkv", (ROWS, 3 * D), B),
    ("lse", (6, 8, SEQ), F),
    ("att", (ROWS, D), B),
    ("o", (ROWS, D), F),
    ("x1", (ROWS, D), F),
    ("min", (ROWS, D), B),
    ("slope", (ROWS, FF), F),
    ("act", (ROWS, FF), B),
    ("f", (ROWS, D), F),
)
WEIGHTS = (("main", (D, C_MAIN), B), ("bias", (1, C_MAIN), F), ("bias2", (1, D), F), ("fc2", (FF, D), B))
TEMPS = (
    ("dmod", (8, 6 * D), F),
    ("db", (1, 3072), F),
    ("part", (EXP, QUARTER), F),
    ("part2", (EXP, D), F),
    ("wide2", (EXP, ROWS), B),
    ("df", (ROWS, D), B),
    ("dz", (ROWS, FF), B),
    ("wide", (EXP, ROWS), B),
    ("dx1", (ROWS, D), F),
    ("datt", (ROWS, D), B),
    ("dqkv", (ROWS, 3 * D), B),
)
MOD = (("mod", (8, 6 * D), F),)


def buffers(table):
    return [pltpu.VMEM(shape, dtype) for _, shape, dtype in table]


def shapes(table):
    return [jax.ShapeDtypeStruct(shape, dtype) for _, shape, dtype in table]


def named(table, refs):
    return {name: ref for (name, _, _), ref in zip(table, refs)}


def fetch_halves(core, own, other, g, sems):
    def go(low, high):
        copies = [
            pltpu.make_async_copy(low, g.at[:, :G_HALF], sems.at[0]),
            pltpu.make_async_copy(high, g.at[:, G_HALF:], sems.at[1]),
        ]
        for copy in copies:
            copy.start()
        for copy in copies:
            copy.wait()

    @pl.when(core == 0)
    def _():
        go(own, other)

    @pl.when(core != 0)
    def _():
        go(other, own)


def fetch_ada(core, own, other, g, sems):
    def go(high):
        copy = pltpu.make_async_copy(high.at[:, G_ADA - G_HALF : G_BIAS - G_HALF], g, sems.at[0])
        copy.start()
        copy.wait()

    @pl.when(core == 0)
    def _():
        go(other)

    @pl.when(core != 0)
    def _():
        go(own)


def pack_out(pack, keep, send, sems):
    copies = [pltpu.make_async_copy(pack.at[i], ref, sems.at[i]) for i, ref in enumerate((keep, send))]
    for copy in copies:
        copy.start()
    for copy in copies:
        copy.wait()


def putter(core, pack):
    def put(half, rows, cols, value):
        slot = core if half == 0 else 1 - core
        pack[slot, rows, cols] = value

    return put


def front_kernel(core, own, other, x, cond, *refs):
    n_keep, n_w = len(KEEP), len(WEIGHTS)
    y = refs[0]
    k = named(KEEP, refs[1 : 1 + n_keep])
    w = named(WEIGHTS, refs[1 + n_keep : 1 + n_keep + n_w])
    mod, g, sel, selt, sems = refs[1 + n_keep + n_w :]
    build_selectors(sel, selt)
    fetch_halves(core[0], own, other, g, sems)
    ada = unpack(g, selt, w)
    modulate(cond, g, selt, ada, mod)
    forward(x, w, mod, k, y)


def turn_kernel(core, whole, x, cond, grad, y, dx, dc, keep, send, *refs):
    n_keep, n_w, n_t = len(KEEP), len(WEIGHTS), len(TEMPS)
    k = named(KEEP, refs[:n_keep])
    w = named(WEIGHTS, refs[n_keep : n_keep + n_w])
    t = named(TEMPS, refs[n_keep + n_w : n_keep + n_w + n_t])
    mod, g, sel, selt, pack, sems = refs[n_keep + n_w + n_t :]
    copy = pltpu.make_async_copy(whole, g, sems.at[0])
    copy.start()
    build_selectors(sel, selt)
    copy.wait()
    ada = unpack(g, selt, w)
    modulate(cond, g, selt, ada, mod)
    forward(x, w, mod, k, y)
    backward(core[0], grad, x, cond, g, G_ADA, sel, selt, w, mod, k, t, dx, dc, putter(core[0], pack))
    pack_out(pack, keep, send, sems)


def back_kernel(core, own, other, x, cond, grad, *refs):
    n_keep, n_w, n_t = len(KEEP), len(WEIGHTS), len(TEMPS)
    k = named(KEEP, refs[:n_keep])
    w = named(WEIGHTS, refs[n_keep : n_keep + n_w])
    mod, dx, dc, keep, send = refs[n_keep + n_w : n_keep + n_w + 5]
    refs = refs[n_keep + n_w + 5 :]
    t = named(TEMPS, refs[:n_t])
    g, sel, selt, pack, sems = refs[n_t:]
    build_selectors(sel, selt)
    fetch_ada(core[0], own, other, g, sems)
    backward(core[0], grad, x, cond, g, 0, sel, selt, w, mod, k, t, dx, dc, putter(core[0], pack))
    pack_out(pack, keep, send, sems)


VM = pl.BlockSpec(memory_space=pltpu.VMEM)
ANY = pl.BlockSpec(memory_space=pl.ANY)
SM = pl.BlockSpec(memory_space=pltpu.SMEM)
PARAMS = pltpu.CompilerParams(vmem_limit_bytes=60 * 1024 * 1024)
G_BUF = pltpu.VMEM((EXP, G_END), B)
ADA_BUF = pltpu.VMEM((EXP, G_BIAS - G_ADA), B)
SEL_BUFS = [pltpu.VMEM((4, EXP, D), B), pltpu.VMEM((4, D, EXP), B)]
SEMS = pltpu.SemaphoreType.DMA((2,))
ROWS_OUT = jax.ShapeDtypeStruct((ROWS, D), B)
COND_OUT = jax.ShapeDtypeStruct((8, D), F)
HALF_OUT = jax.ShapeDtypeStruct((EXP, P_HALF), B)
PACK_BUF = pltpu.VMEM((2, EXP, P_HALF), B)


def cost(units):
    return pl.CostEstimate(flops=units * 2_000_000_000, bytes_accessed=units * 10_000_000, transcendentals=units * 2_000_000)


def front(core, own, other, x, cond):
    outs = [ROWS_OUT] + shapes(KEEP) + shapes(WEIGHTS) + shapes(MOD)
    return pl.pallas_call(
        front_kernel,
        out_shape=outs,
        in_specs=[SM, ANY, ANY, VM, VM],
        out_specs=[VM] * len(outs),
        scratch_shapes=[G_BUF, *SEL_BUFS, SEMS],
        compiler_params=PARAMS,
        cost_estimate=cost(1),
        name="front",
    )(core, own, other, x, cond)


def turn(core, whole, x, cond, grad):
    return pl.pallas_call(
        turn_kernel,
        out_shape=[ROWS_OUT, ROWS_OUT, COND_OUT, HALF_OUT, HALF_OUT],
        in_specs=[SM, ANY, VM, VM, VM],
        out_specs=[VM] * 3 + [ANY] * 2,
        scratch_shapes=buffers(KEEP) + buffers(WEIGHTS) + buffers(TEMPS) + buffers(MOD) + [G_BUF, *SEL_BUFS, PACK_BUF, SEMS],
        compiler_params=PARAMS,
        cost_estimate=cost(3),
        name="turn",
    )(core, whole, x, cond, grad)


def back(core, own, other, x, cond, grad, kept):
    return pl.pallas_call(
        back_kernel,
        out_shape=[ROWS_OUT, COND_OUT, HALF_OUT, HALF_OUT],
        in_specs=[SM, ANY, ANY, VM, VM, VM] + [VM] * len(kept),
        out_specs=[VM] * 2 + [ANY] * 2,
        scratch_shapes=buffers(TEMPS) + [ADA_BUF, *SEL_BUFS, PACK_BUF, SEMS],
        compiler_params=PARAMS,
        cost_estimate=cost(2),
        name="back",
    )(core, own, other, x, cond, grad, *kept)


def line_up(w_qkv, b_qv, w_proj, b_proj, w_fc1, b_fc1, w_fc2, b_fc2, w_ada, b_ada):
    def pieces(rows):
        rows = jnp.concatenate(rows, axis=0)
        rows = jnp.pad(rows, ((0, -rows.shape[0] % 8), (0, 0)))
        return [rows[i : i + 8] for i in range(0, rows.shape[0], 8)]

    main = jnp.concatenate([w_qkv, w_proj, w_fc1], axis=1)
    bias = jnp.concatenate([b_qv, b_proj, b_fc1, b_fc2, b_ada])
    bias = jnp.pad(bias, (0, 1024 - bias.shape[0])).reshape(8, 128)
    return jnp.concatenate(
        pieces([main[:, i * QUARTER : (i + 1) * QUARTER] for i in range(4)])
        + pieces([w_fc2])
        + pieces([w_ada[:, i * 256 : (i + 1) * 256] for i in range(9)])
        + [bias],
        axis=1,
    )


def swap(x):
    return lax.ppermute(x, "pipe", [(0, 1), (1, 0)])


def to_all(block):
    copies = jnp.broadcast_to(block[None], (CHIPS, *block.shape))
    return lax.all_to_all(copies, "shard", 0, 0, tiled=True).reshape(EXP, block.shape[1])


def scatter(block):
    return lax.all_to_all(block.reshape(CHIPS, 8, P_HALF), "shard", 0, 0, tiled=True)


def shards(latents, conditions, cotangent, w_qkv, b_qv, w_proj, b_proj, w_fc1, b_fc1, w_fc2, b_fc2, w_ada, b_ada):
    p = lax.axis_index("pipe")
    j = lax.axis_index("shard")
    first = p == 0
    core = p.reshape(1).astype(jnp.int32)
    block = line_up(w_qkv[0], b_qv[0], w_proj[0], b_proj[0], w_fc1[0], b_fc1[0], w_fc2[0], b_fc2[0], w_ada[0], b_ada[0])
    block_other = swap(block)
    block1 = jnp.where(first, block_other, block)
    own1 = lax.all_gather(block1, "shard", tiled=True)
    half0 = jnp.where(first, block[:, :G_HALF], block_other[:, G_HALF:])
    own0 = to_all(half0)
    other0 = swap(own0)
    x = lax.dynamic_index_in_dim(latents, p, 0, keepdims=False).reshape(ROWS, D)
    cot = lax.dynamic_index_in_dim(cotangent, p, 0, keepdims=False).reshape(ROWS, D)
    cond = lax.dynamic_index_in_dim(conditions, p, 0, keepdims=False).astype(F)
    cond = jnp.concatenate([cond, jnp.zeros((6, D), F)], axis=0)

    h, *kept = front(core, own0, other0, x, cond)
    y, dx1, dc1, keep1, send1 = turn(core, own1, h, cond, cot)
    parts1 = scatter(keep1 + swap(send1))
    dx0, dc0, keep0, send0 = back(core, own0, other0, x, cond, dx1, kept)
    parts1, send0 = lax.optimization_barrier((parts1, send0))
    parts0 = scatter(keep0 + swap(send0))

    def pair(for_first, for_second):
        keep = jnp.where(first, for_first, for_second)
        came = swap(jnp.where(first, for_second, for_first))
        both = jnp.where(first, jnp.stack([keep, came]), jnp.stack([came, keep]))
        return both.reshape(1, 2, 2, SEQ, D)

    section_outputs = pair(h, y)
    input_grads = pair(dx0, dx1)
    dc = (dc0 + dc1)[:2]
    dc_other = swap(dc)
    cond_grad = jnp.where(first, jnp.stack([dc, dc_other]), jnp.stack([dc_other, dc]))

    def reduced(parts):
        lot = jnp.sum(parts.astype(F), axis=0)
        flat = parts.reshape(EXP, P_HALF)
        ada = lax.dot_general(
            flat[:, P_COND : P_COND + 16], flat[:, P_MOD:P_DB1], (((0,), (0,)), ((), ())), preferred_element_type=F
        )
        return jnp.concatenate([lot, ada[:8], ada[8:]], axis=1)

    lot0 = reduced(parts0)
    lot1 = reduced(parts1)
    kept_half = jnp.where(first, lot0, lot1)
    came_half = swap(jnp.where(first, lot1, lot0))
    low = jnp.where(first, kept_half, came_half)
    high = jnp.where(first, came_half, kept_half)

    rows = jnp.concatenate([low[:, a * QUARTER : (a + 1) * QUARTER] for a in range(3)], axis=0)
    quarters = [rows[6 * q : 6 * q + 6] for q in range(4)]
    db = jnp.concatenate([low[:, P_DB0 : P_DB0 + 128], low[:, P_DB0 + 128 : P_HALF], high[:, P_DB1:P_COND]], axis=0).reshape(-1)
    sums = high[:, P_MOD:P_DB1]
    db_ada = jnp.concatenate([sums[:4].sum(axis=0), sums[4:].sum(axis=0)])

    def slice_of(line, at, width):
        return lax.dynamic_slice(line, (at + width * j,), (width,))

    outs = (
        jnp.concatenate([quarters[0], quarters[1][:, :384]], axis=1),
        slice_of(db, 0, 12),
        quarters[1][:, 384:],
        slice_of(db, 768, 6),
        jnp.concatenate([quarters[2], quarters[3]], axis=1),
        slice_of(db, 1152, 24),
        jnp.concatenate([high[:, a * D : (a + 1) * D] for a in range(3)], axis=0),
        slice_of(db, 2688, 6),
        jnp.concatenate([high[:6, P_HALF : P_HALF + 1152], high[:6, P_HALF + 1152 :]], axis=1),
        slice_of(db_ada, 0, 36),
    )
    return (section_outputs, input_grads, cond_grad) + tuple(o[None] for o in outs)


def solution(mesh):
    rows = P(None, "shard", None, None)
    wide = P("pipe", "shard", None)
    thin = P("pipe", "shard")
    both = P("pipe", None, "shard", None, None)
    pairs = (wide, thin) * 5
    return jax.shard_map(
        shards,
        mesh=mesh,
        in_specs=(rows, P(None, "shard", None), rows) + pairs,
        out_specs=(both, both, P(None, "shard", None)) + pairs,
        check_vma=False,
    )
```

time: 316 us -> 281 us (0.89)
  waiting for transfers between devices: 129 us -> 58 us
  blocking collectives: 0 us -> 48 us
  starting transfers between devices: 38 us -> 24.8 us
    all_to_all x3 -> x2, waiting for transfers between devices: 90.3 us -> 29.4 us  [scatter(): lax.all_to_all(block.reshape(CHIPS, 8, P_HALF), 'shard', 0, 0, tiled=True)]
    all_to_all x0 -> x1, blocking collectives: none -> 48 us  [to_all(): lax.all_to_all(copies, 'shard', 0, 0, tiled=True)]
    all_to_all x3 -> x2, starting transfers between devices: 26.7 us -> 13.2 us  [scatter(): lax.all_to_all(block.reshape(CHIPS, 8, P_HALF), 'shard', 0, 0, tiled=True)]
    ppermute x9 -> x8, waiting for transfers between devices: 22.4 us -> 12.1 us  [swap(): return lax.ppermute(x, 'pipe', [(0, 1), (1, 0)])]
    broadcast_in_dim x3 -> x7, local copies, waits for them, and re-layouts: 0.01 us -> 4.29 us  [shards(): o[None]]
    dynamic_update_slice x5 -> x0, local copies, waits for them, and re-layouts: 3.95 us -> none  [the longest x1 0.81 us: line_up(): line = lax.dynamic_update_slice(line, b_qv, (at_qv,))]
    concatenate x1 -> x4, local copies, waits for them, and re-layouts: 0.01 us -> 3.86 us  [the longest x1 3.43 us: line_up(): bias = jnp.concatenate([b_qv, b_proj, b_fc1, b_fc2, b_ada])]
    reshape x2 -> x3, other arithmetic: 8.33 us -> 7.12 us  [the longest x2 7.11 us: scatter(): block.reshape(CHIPS, 8, P_HALF)]
  transfers between devices with their start and end apart: 13 -> 11, of which waited for: 9 -> 7; matrix products, arithmetic and copies ran while one was open for 4% -> 7% of each run, Pallas kernels for 17% -> 19%
where the time goes in v3:
time: 281 us; the launch traced here: 280 us
  Pallas kernels  95.3 us (34%)
  waiting for transfers between devices  58 us (21%)
  blocking collectives  48 us (17%)
  starting transfers between devices  24.8 us (9%)
  other arithmetic  23 us (8%)
  local copies, waits for them, and re-layouts  14.6 us (5%)
  between operations  14.3 us (5%)
    all_to_all x1, blocking collectives, to_all(): lax.all_to_all(copies, 'shard', 0, 0, tiled=True)  48 us
    pallas_call x1, Pallas kernels, turn(): pl.pallas_call(turn_kernel, out_shape=[ROWS_OUT, ROWS_OUT, COND_OUT, HALF...  41.5 us
    pallas_call x1, Pallas kernels, back(): pl.pallas_call(back_kernel, out_shape=[ROWS_OUT, COND_OUT, HALF_OUT, HALF...  30.3 us
    all_to_all x2, waiting for transfers between devices, scatter(): lax.all_to_all(block.reshape(CHIPS, 8, P_HALF), 'shard', 0, 0, tiled=True)  29.4 us
    pallas_call x1, Pallas kernels, front(): pl.pallas_call(front_kernel, out_shape=outs, in_specs=[SM, ANY, ANY, VM,...  23.5 us
    all_gather x1, waiting for transfers between devices, shards(): own1 = lax.all_gather(block1, 'shard', tiled=True)  16.6 us
    all_to_all x2, starting transfers between devices, scatter(): lax.all_to_all(block.reshape(CHIPS, 8, P_HALF), 'shard', 0, 0, tiled=True)  13.2 us
    ppermute x8, waiting for transfers between devices, swap(): return lax.ppermute(x, 'pipe', [(0, 1), (1, 0)])  12.1 us
  transfers between devices with their start and end apart: 11, of which 7 were waited for; matrix products, arithmetic and copies ran while one was open for 7% of the time, Pallas kernels for 19%

profile of v3, /device:TPU:1, one launch (start us, length us, event | category | flops | bytes accessed | tf_op | source)
XLA Modules:
  0.0 279.9 jit_solution(10186468786014184364)
XLA Ops:
  11.6 3.4 %concatenate.119 = bf16[84]{0:T(256)(128)(2,1)S(1)} concatenate(bf16[12]{0:T(256)(128)(2,1)} %bitcast.66, bf16[6]{0:T(256)(128)(2,1)} %bitcast.67, bf16[24]{0:T(256)(128)(2,1)} %bitcast.68, bf16[6]{0:T(256)(128)(2,1)} %bitcast.69, bf16[36]{0:T(256)(128)(2,1)} %bitcast.70), dimensions={0} | concatenate | bytes 336 | tf_op jit(solution)/shard_map/concatenate | solution.py:628
  19.0 48.0 %all_to_all.15 = bf16[64,8,2688]{2,1,0:T(8,128)(2,1)S(1)} all-to-all(bf16[64,8,2688]{2,1,0:T(8,128)(2,1)S(1)} %broadcast_in_dim.37), channel_id=1, replica_groups=mesh['pipe'=2,'shard'=64] {'shard'}, dimensions={0} | all-to-all | bytes 5505024 | tf_op jit(solution)/shard_map/all_to_all | solution.py:645
  67.0 2.0 collective-permute-start.1
  70.4 1.8 constant_dynamic-slice_fusion
  73.9 23.5 %front.1 = (bf16[512,384]{1,0:T(8,128)(2,1)}, bf16[512,384]{1,0:T(8,128)(2,1)}, bf16[512,1152]{1,0:T(8,128)(2,1)}, f32[6,8,256]{2,1,0:T(8,128)}, bf16[512,384]{1...) custom-call(s32[1]{0:T(128)} %bitcast.core, ...), custom_call_target="tpu_custom_call" | custom-call | flops 2000000000 | bytes 10000000 | tf_op jit(solution)/shard_map/front/pallas_call | solution.py:583
  97.4 16.6 %all-gather.2.cloned.1.call-done.whole = bf16[512,5376]{1,0:T(8,128)(2,1)} async-done(((bf16[8,5376]{1,0:T(8,128)(2,1)}), bf16[512,5376]{1,0:T(8,128)(2,1)}) %all-gather.2.cloned.1.call-update) | async-done | bytes 5505040 | tf_op jit(solution)/shard_map/all_gather | solution.py:660
  113.9 41.5 %turn.1 = (bf16[512,384]{1,0:T(8,128)(2,1)}, bf16[512,384]{1,0:T(8,128)(2,1)}, f32[8,384]{1,0:T(8,128)}, bf16[512,2560]{1,0:T(8,128)(2,1)}, bf16[512,2560]{1,0:T(8,128)(2,1)}) custom-call(s32[1]{0:T(128)} %bitcast.core, bf16[512,5376]{1,0:T(8,128)(2,1)} %all-gather.2.cloned.1.call-done.whole, bf16[512,384]{1,0:T(8,128)(2,1)} %get-tuple-element.40.x, ...), custom_call_target="tpu_custom_call" | custom-call | flops 6000000000 | bytes 30000000 | tf_op jit(solution)/shard_map/turn/pallas_call | solution.py:596
  155.4 2.0 collective-permute-start.5
  157.4 4.7 %collective-permute-done.5 = bf16[512,2560]{1,0:T(8,128)(2,1)S(1)} collective-permute-done((bf16[512,2560]{1,0:T(8,128)(2,1)}, bf16[512,2560]{1,0:T(8,128)(2,1)S(1)}, u32[]{:S(2)}, u32[]{:S(2)}) %collective-permute-start.5) | collective-permute-done | bytes 2621472 | tf_op jit(solution)/shard_map/ppermute | solution.py:640
  162.1 3.6 %add_bitcast_fusion.1 = bf16[64,8,2560]{2,1,0:T(8,128)(2,1)} fusion(bf16[512,2560]{1,0:T(8,128)(2,1)} %get-tuple-element.62, bf16[512,2560]{1,0:T(8,128)(2,1)S(1)} %collective-permute-done.5), kind=kLoop, calls=%fused_computation.3 | loop fusion | flops 1310720 | bytes 7864320 | tf_op jit(solution)/shard_map/reshape | solution.py:649
  165.7 6.9 %all-to-all-start.1 = ((bf16[64,8,2560]{2,1,0:T(8,128)(2,1)}), bf16[64,8,2560]{2,1,0:T(8,128)(2,1)S(1)}, u32[]{:S(2)}, u32[]{:S(2)}) async-start(bf16[64,8,2560]{2,1,0:T(8,128)(2,1)} %add_bitcast_fusion.1), calls=%async_computation.1 | async-start | bytes 5242880 | tf_op jit(solution)/shard_map/all_to_all | solution.py:649
  172.6 30.3 %back.1 = (bf16[512,384]{1,0:T(8,128)(2,1)}, f32[8,384]{1,0:T(8,128)}, bf16[512,2560]{1,0:T(8,128)(2,1)}, bf16[512,2560]{1,0:T(8,128)(2,1)}) custom-call(s32[1]{0:T(128)} %bitcast.core, bf16[512,2688]{1,0:T(8,128)(2,1)} %bitcast.54, bf16[512,2688]{1,0:T(8,128)(2,1)} %collective-permute-done.1.other, bf16[512,384]{1,0:T(8,128)(2,1)} %bitcast.58, ...), custom_call_target="tpu_custom_call" | custom-call | flops 4000000000 | bytes 20000000 | tf_op jit(solution)/shard_map/back/pallas_call | solution.py:609
  203.0 3.2 %all-to-all-done.1 = bf16[64,8,2560]{2,1,0:T(8,128)(2,1)S(1)} async-done(((bf16[64,8,2560]{2,1,0:T(8,128)(2,1)}), bf16[64,8,2560]{2,1,0:T(8,128)(2,1)S(1)}, u32[]{:S(2)}, u32[]{:S(2)}) %all-to-all-start.1) | async-done | bytes 2621472 | tf_op jit(solution)/shard_map/all_to_all | solution.py:649
  206.2 2.4 collective-permute-start.6
  208.6 4.7 %collective-permute-done.6 = bf16[512,2560]{1,0:T(8,128)(2,1)S(1)} collective-permute-done((bf16[512,2560]{1,0:T(8,128)(2,1)}, bf16[512,2560]{1,0:T(8,128)(2,1)S(1)}, u32[]{:S(2)}, u32[]{:S(2)}) %collective-permute-start.6) | collective-permute-done | bytes 2621472 | tf_op jit(solution)/shard_map/ppermute | solution.py:640
  213.4 3.6 %add_bitcast_fusion = bf16[64,8,2560]{2,1,0:T(8,128)(2,1)} fusion(bf16[512,2560]{1,0:T(8,128)(2,1)} %get-tuple-element.61, bf16[512,2560]{1,0:T(8,128)(2,1)S(1)} %collective-permute-done.6), kind=kLoop, calls=%fused_computation.2 | loop fusion | flops 1310720 | bytes 7864320 | tf_op jit(solution)/shard_map/reshape | solution.py:649
  216.9 6.3 %all-to-all-start.2 = ((bf16[64,8,2560]{2,1,0:T(8,128)(2,1)}), bf16[64,8,2560]{2,1,0:T(8,128)(2,1)}, u32[]{:S(2)}, u32[]{:S(2)}) async-start(bf16[64,8,2560]{2,1,0:T(8,128)(2,1)} %add_bitcast_fusion), calls=%async_computation.2 | async-start | bytes 5242880 | tf_op jit(solution)/shard_map/all_to_all | solution.py:649
  224.7 2.1 broadcast_select_fusion.1
  226.7 2.1 broadcast_select_fusion.3
  230.6 26.1 %all-to-all-done.2 = bf16[64,8,2560]{2,1,0:T(8,128)(2,1)} async-done(((bf16[64,8,2560]{2,1,0:T(8,128)(2,1)}), bf16[64,8,2560]{2,1,0:T(8,128)(2,1)}, u32[]{:S(2)}, u32[]{:S(2)}) %all-to-all-start.2) | async-done | bytes 2621472 | tf_op jit(solution)/shard_map/all_to_all | solution.py:649
  258.4 2.2 convert_reduce_fusion.1
  260.6 2.5 collective-permute-start.7
  263.1 2.1 maximum_select_fusion.1
  265.2 2.1 maximum_select_fusion
  (75 shorter events, 21.8 us)
Async XLA Ops:
  7.2 62.5 %copy-start = (bf16[2,2,256,384]{3,2,1,0:T(8,128)(2,1)S(1)}, bf16[2,2,256,384]{3,2,1,0:T(8,128)(2,1)}, u32[]{:S(2)}) copy-start(bf16[2,2,256,384]{3,2,1,0:T(8,128)(2,1)} %param.13) | copy-start | bytes 2359300
  7.2 106.7 %all-gather.2.cloned.1.call-start = ((), (), s32[]{:S(2)}) async-start(), calls=%async_computation.3 | async-start | bytes 5591040 | tf_op jit(solution)/shard_map/all_gather | solution.py:660
  15.0 2.4 collective-permute-start
  19.0 50.0 %copy-start.4 = (bf16[2,2,384]{2,1,0:T(2,128)(2,1)S(1)}, bf16[2,2,384]{2,1,0:T(2,128)(2,1)}, u32[]{:S(2)}) copy-start(bf16[2,2,384]{2,1,0:T(2,128)(2,1)} %param.14) | copy-start | bytes 9220
  67.0 6.9 %copy-start.1 = (bf16[64,8,2688]{2,1,0:T(8,128)(2,1)}, bf16[64,8,2688]{2,1,0:T(8,128)(2,1)S(1)}, u32[]{:S(2)}) copy-start(bf16[64,8,2688]{2,1,0:T(8,128)(2,1)S(1)} %all_to_all.15) | copy-start | bytes 8257540
  67.0 6.9 %collective-permute-start.1 = (bf16[512,2688]{1,0:T(8,128)(2,1)S(1)}, bf16[512,2688]{1,0:T(8,128)(2,1)}, u32[]{:S(2)}, u32[]{:S(2)}) collective-permute-start(bf16[512,2688]{1,0:T(8,128)(2,1)S(1)} %bitcast.52), channel_id=1, source_target_pairs={{0,64},{64,0},{1,65},{65,1},{2,66},{66,2},{3,67},{67,3},{4,68},{68... | collective-permute-start | bytes 8257544 | tf_op jit(solution)/shard_map/ppermute | solution.py:640
  155.4 6.7 %collective-permute-start.5 = (bf16[512,2560]{1,0:T(8,128)(2,1)}, bf16[512,2560]{1,0:T(8,128)(2,1)S(1)}, u32[]{:S(2)}, u32[]{:S(2)}) collective-permute-start(bf16[512,2560]{1,0:T(8,128)(2,1)} %get-tuple-element.63), channel_id=1, source_target_pairs={{0,64},{64,0},{1,65},{65,1},{2,66},{66,2},{3,67},{67,3},{4,68},{68... | collective-permute-start | bytes 7864328 | tf_op jit(solution)/shard_map/ppermute | solution.py:640
  165.7 40.5 %all-to-all-start.1 = ((bf16[64,8,2560]{2,1,0:T(8,128)(2,1)}), bf16[64,8,2560]{2,1,0:T(8,128)(2,1)S(1)}, u32[]{:S(2)}, u32[]{:S(2)}) async-start(bf16[64,8,2560]{2,1,0:T(8,128)(2,1)} %add_bitcast_fusion.1), calls=%async_computation.1 | async-start | bytes 5242880 | tf_op jit(solution)/shard_map/all_to_all | solution.py:649
  206.2 7.2 %collective-permute-start.6 = (bf16[512,2560]{1,0:T(8,128)(2,1)}, bf16[512,2560]{1,0:T(8,128)(2,1)S(1)}, u32[]{:S(2)}, u32[]{:S(2)}) collective-permute-start(bf16[512,2560]{1,0:T(8,128)(2,1)} %get-tuple-element.65), channel_id=1, source_target_pairs={{0,64},{64,0},{1,65},{65,1},{2,66},{66,2},{3,67},{67,3},{4,68},{68... | collective-permute-start | bytes 7864328 | tf_op jit(solution)/shard_map/ppermute | solution.py:640
  216.9 39.8 %all-to-all-start.2 = ((bf16[64,8,2560]{2,1,0:T(8,128)(2,1)}), bf16[64,8,2560]{2,1,0:T(8,128)(2,1)}, u32[]{:S(2)}, u32[]{:S(2)}) async-start(bf16[64,8,2560]{2,1,0:T(8,128)(2,1)} %add_bitcast_fusion), calls=%async_computation.2 | async-start | bytes 5242880 | tf_op jit(solution)/shard_map/all_to_all | solution.py:649
  224.0 5.3 %collective-permute-start.4 = (f32[2,384]{1,0:T(2,128)S(1)}, f32[2,384]{1,0:T(2,128)S(1)}, u32[]{:S(2)}, u32[]{:S(2)}) collective-permute-start(f32[2,384]{1,0:T(2,128)S(1)} %slice_add_fusion), channel_id=1, source_target_pairs={{0,64},{64,0},{1,65},{65,1},{2,66},{66,2},{3,67},{67,3},{4,68},{68... | collective-permute-start | bytes 9224 | tf_op jit(solution)/shard_map/ppermute | solution.py:640
  226.7 36.3 %collective-permute-start.3 = (bf16[512,384]{1,0:T(8,128)(2,1)}, bf16[512,384]{1,0:T(8,128)(2,1)}, u32[]{:S(2)}, u32[]{:S(2)}) collective-permute-start(bf16[512,384]{1,0:T(8,128)(2,1)} %get-tuple-element.76), channel_id=1, source_target_pairs={{0,64},{64,0},{1,65},{65,1},{2,66},{66,2},{3,67},{67,3},{4,68},{68... | collective-permute-start | bytes 1179656 | tf_op jit(solution)/shard_map/ppermute | solution.py:640
  228.8 36.4 %collective-permute-start.2 = (bf16[512,384]{1,0:T(8,128)(2,1)}, bf16[512,384]{1,0:T(8,128)(2,1)}, u32[]{:S(2)}, u32[]{:S(2)}) collective-permute-start(bf16[512,384]{1,0:T(8,128)(2,1)} %get-tuple-element.78), channel_id=1, source_target_pairs={{0,64},{64,0},{1,65},{65,1},{2,66},{66,2},{3,67},{67,3},{4,68},{68... | collective-permute-start | bytes 1179656 | tf_op jit(solution)/shard_map/ppermute | solution.py:640
  230.6 32.5 %copy-start.2 = (bf16[512,384]{1,0:T(8,128)(2,1)S(1)}, bf16[512,384]{1,0:T(8,128)(2,1)}, u32[]{:S(2)}) copy-start(bf16[512,384]{1,0:T(8,128)(2,1)} %get-tuple-element.75) | copy-start | bytes 1179652
  258.4 6.8 %copy-start.3 = (bf16[512,384]{1,0:T(8,128)(2,1)S(1)}, bf16[512,384]{1,0:T(8,128)(2,1)}, u32[]{:S(2)}) copy-start(bf16[512,384]{1,0:T(8,128)(2,1)} %get-tuple-element.77) | copy-start | bytes 1179652
  260.6 6.8 %collective-permute-start.7 = (f32[8,4864]{1,0:T(8,128)S(1)}, f32[8,4864]{1,0:T(8,128)S(1)}, u32[]{:S(2)}, u32[]{:S(2)}) collective-permute-start(f32[8,4864]{1,0:T(8,128)S(1)} %fusion.6), channel_id=1, source_target_pairs={{0,64},{64,0},{1,65},{65,1},{2,66},{66,2},{3,67},{67,3},{4,68},{68... | collective-permute-start | bytes 466952 | tf_op jit(solution)/shard_map/ppermute | solution.py:640
Sparse Core Ops, SparseCore 0:
  18.2 95.6 all-gather.1

commit v4 on v3

--- a/solution.py
+++ b/solution.py
@@ -34,6 +34,7 @@
 K0 = 0.7978845608028654
 K1 = 0.044715
 
+UNROLL = 6
 NN = (1, 0)
 NT = (1, 1)
 TN = (0, 0)
@@ -148,17 +149,17 @@
 
 
 def cond_back(dm, g, g_at, selt):
-    r8 = tile_row((1, EXP), 1)
-    sums = [jnp.zeros((8, EXP), F)] * 4
+    r8 = tile_row((EXP, 1), 0)
+    sums = [jnp.zeros((EXP, 8), F)] * 4
     for n, (i, a, more) in enumerate(ada_groups()):
         at = g_at + a * 256
         piece = dm[:, n * 256 : (n + 1) * 256]
-        sums[i] = sums[i] + jnp.where(r8 >= SHIFTS[i], dot(piece, g[:, at : at + 256], NT), 0.0)
+        sums[i] = sums[i] + jnp.where(r8 >= SHIFTS[i], dot(g[:, at : at + 256], piece, NT), 0.0)
         if more:
-            sums[i] = sums[i] + jnp.where(r8 < SHIFTS[i], dot(piece, g[:, at + 256 : at + 512], NT), 0.0)
+            sums[i] = sums[i] + jnp.where(r8 < SHIFTS[i], dot(g[:, at + 256 : at + 512], piece, NT), 0.0)
     total = jnp.zeros((8, D), F)
     for i in range(4):
-        rest = sums[i]
+        rest = sums[i].T
         for _ in range(3):
             level = rest.astype(B)
             rest = rest - level.astype(F)
@@ -166,7 +167,7 @@
     return total
 
 
-def forward(x, w, mod, k, y):
+def forward(x, w, mod, k, y, save=lambda *names: None):
     main, bias, fc2 = w["main"], w["bias"], w["fc2"]
 
     def ln_in(i, _):
@@ -176,7 +177,7 @@
         k["ain"][rows, :] = (n * (1.0 + mod[lat, D : 2 * D]) + mod[lat, :D]).astype(B)
         return 0
 
-    lax.fori_loop(0, 4, ln_in, 0)
+    lax.fori_loop(0, 4, ln_in, 0, unroll=True)
 
     for c in range(3):
         cs = slice(c * D, (c + 1) * D)
@@ -189,34 +190,33 @@
         at = (i % 3) * 128
         q = k["qkv"][rows, pl.ds(pl.multiple_of(at, 128), 128)]
         key = k["qkv"][rows, pl.ds(pl.multiple_of(D + at, 128), 128)]
-        v = k["qkv"][rows, pl.ds(pl.multiple_of(2 * D + at, 128), 128)]
-        total = None
+        vt = k["qkv"][rows, pl.ds(pl.multiple_of(2 * D + at, 128), 128)].T
+        heads = []
         for h, m in enumerate((low, high)):
-            s = dot(key, q * m, NT) * 0.125
+            s = dot(key, q * (m * 0.125), NT)
             top = jnp.max(s, axis=0, keepdims=True)
             e = jnp.exp(s - top)
             t = jnp.sum(e, axis=0, keepdims=True)
             p = (e * (1.0 / t)).astype(B)
             k["lse"][i, h : h + 1, :] = top + jnp.log(t)
-            part = dot(p, v * m, TN)
-            total = part if total is None else total + part
-        k["att"][rows, pl.ds(pl.multiple_of(at, 128), 128)] = total.astype(B)
-        return 0
-
-    lax.fori_loop(0, 6, attend, 0)
+            heads.append(dot(vt[h * HEAD : (h + 1) * HEAD], p))
+        k["att"][rows, pl.ds(pl.multiple_of(at, 128), 128)] = jnp.concatenate(heads, axis=0).T.astype(B)
+        return 0
+
+    lax.fori_loop(0, 6, attend, 0, unroll=UNROLL)
+    save("ain", "qkv", "lse", "att")
+    k["o"][...] = dot(k["att"][...], main[:, C_PROJ:C_FC1]) + bias[:, C_PROJ:C_FC1]
 
     def mid(i, _):
         rows = pl.ds(pl.multiple_of(i * 128, 128), 128)
         lat = pl.ds(i // 2, 1)
-        o = dot(k["att"][rows, :], main[:, C_PROJ:C_FC1]) + bias[:, C_PROJ:C_FC1]
-        x1 = x[rows, :].astype(F) + mod[lat, 2 * D : 3 * D] * o
-        k["o"][rows, :] = o
+        x1 = x[rows, :].astype(F) + mod[lat, 2 * D : 3 * D] * k["o"][rows, :]
         k["x1"][rows, :] = x1
         n, _ = stats(x1)
         k["min"][rows, :] = (n * (1.0 + mod[lat, 4 * D : 5 * D]) + mod[lat, 3 * D : 4 * D]).astype(B)
         return 0
 
-    lax.fori_loop(0, 4, mid, 0)
+    lax.fori_loop(0, 4, mid, 0, unroll=True)
 
     def mlp(i, _):
         at = pl.multiple_of(i * 256, 256)
@@ -230,17 +230,19 @@
         k["slope"][:, cs] = half + (0.5 * z) * (1.0 - t * t) * (K0 + 3.0 * K0 * K1 * zz)
         return 0
 
-    lax.fori_loop(0, 6, mlp, 0)
+    lax.fori_loop(0, 6, mlp, 0, unroll=True)
+
+    save("o", "x1", "min", "slope", "act")
+    k["f"][...] = dot(k["act"][...], fc2[...]) + w["bias2"][...]
 
     def out(i, _):
         rows = pl.ds(pl.multiple_of(i * 128, 128), 128)
         lat = pl.ds(i // 2, 1)
-        f = dot(k["act"][rows, :], fc2[...]) + w["bias2"][...]
-        k["f"][rows, :] = f
-        y[rows, :] = (k["x1"][rows, :] + mod[lat, 5 * D : 6 * D] * f).astype(B)
-        return 0
-
-    lax.fori_loop(0, 4, out, 0)
+        y[rows, :] = (k["x1"][rows, :] + mod[lat, 5 * D : 6 * D] * k["f"][rows, :]).astype(B)
+        return 0
+
+    save("f")
+    lax.fori_loop(0, 4, out, 0, unroll=True)
 
 
 def token_sum(v):
@@ -251,7 +253,7 @@
     return dot(sel[i], v, NT).astype(B)
 
 
-def backward(core, grad, x, cond, g, g_at, sel, selt, w, mod, k, t, dx, dc, put):
+def backward(core, grad, x, cond, g, g_at, sel, selt, w, mod, k, t, dx, dc, put, ship, finish):
     main, fc2 = w["main"], w["fc2"]
     dmod = t["dmod"]
     dmod[...] = jnp.zeros_like(dmod)
@@ -277,7 +279,7 @@
         add_db(2688, token_sum(df.astype(F)))
         return 0
 
-    lax.fori_loop(0, 4, start, 0)
+    lax.fori_loop(0, 4, start, 0, unroll=True)
 
     def dmlp(i, _):
         cs = pl.ds(pl.multiple_of(i * 256, 256), 256)
@@ -288,7 +290,7 @@
         t["db"][:, ds] = token_sum(dz.astype(F))
         return 0
 
-    lax.fori_loop(0, 6, dmlp, 0)
+    lax.fori_loop(0, 6, dmlp, 0, unroll=True)
 
     t["wide2"][...] = spread(sel, 2, k["min"][...])
     t["wide"][...] = spread(sel, 3, k["min"][...])
@@ -308,10 +310,12 @@
                 part[:, 8 * a : 8 * a + 8, :].reshape(128, D).astype(B),
             )
 
+    t["dn"][...] = dot(t["dz"][...], main[:, C_FC1:C_MAIN], NT)
+
     def dmid(i, _):
         rows = pl.ds(pl.multiple_of(i * 128, 128), 128)
         lat = pl.ds(i // 2, 1)
-        dmin = dot(t["dz"][rows, :], main[:, C_FC1:C_MAIN], NT)
+        dmin = t["dn"][rows, :]
         n, inv = stats(k["x1"][rows, :])
         add_mod(lat, 4, token_sum(dmin * n))
         add_mod(lat, 3, token_sum(dmin))
@@ -321,10 +325,10 @@
         add_mod(lat, 2, token_sum(d1 * k["o"][rows, :]))
         t["df"][rows, :] = do
         add_db(768, token_sum(do.astype(F)))
-        t["datt"][rows, :] = dot(do, main[:, C_PROJ:C_FC1], NT).astype(B)
-        return 0
-
-    lax.fori_loop(0, 4, dmid, 0)
+        return 0
+
+    lax.fori_loop(0, 4, dmid, 0, unroll=True)
+    t["datt"][...] = dot(t["df"][...], main[:, C_PROJ:C_FC1], NT).astype(B)
 
     t["wide2"][...] = spread(sel, 1, k["att"][...])
     d1 = dot(t["wide2"][...], t["df"][...])
@@ -343,26 +347,27 @@
         key = k["qkv"][rows, ks]
         v = k["qkv"][rows, vs]
         da = t["datt"][rows, qs]
-        dq = dk = dv = None
+        kt = key.T
+        dk = dv = None
+        dqs = []
         for h, m in enumerate((low, high)):
-            qm = q * m
+            qm = q * (m * 0.125)
             dam = da * m
-            s = dot(key, qm, NT) * 0.125
+            s = dot(key, qm, NT)
             p = jnp.exp(s - k["lse"][i, h : h + 1, :])
             dp = dot(v, dam, NT)
             ds = (p * (dp - jnp.sum(p * dp, axis=0, keepdims=True))).astype(B)
             v1 = dot(p.astype(B), dam)
             k1 = dot(ds, qm)
-            q1 = dot(ds, key * m, TN)
+            dqs.append(dot(kt[h * HEAD : (h + 1) * HEAD], ds))
             dv = v1 if dv is None else dv + v1
             dk = k1 if dk is None else dk + k1
-            dq = q1 if dq is None else dq + q1
-        t["dqkv"][rows, qs] = (dq * 0.125).astype(B)
-        t["dqkv"][rows, ks] = (dk * 0.125).astype(B)
+        t["dqkv"][rows, qs] = (jnp.concatenate(dqs, axis=0).T * 0.125).astype(B)
+        t["dqkv"][rows, ks] = dk.astype(B)
         t["dqkv"][rows, vs] = dv.astype(B)
         return 0
 
-    lax.fori_loop(0, 6, dattend, 0)
+    lax.fori_loop(0, 6, dattend, 0, unroll=UNROLL)
 
     t["wide"][...] = spread(sel, 0, k["ain"][...])
     t["wide2"][...] = spread(sel, 1, k["ain"][...])
@@ -372,6 +377,8 @@
     put(0, slice(0, EXP), slice(QUARTER, QUARTER + 384), jnp.where(r8 < 4, d1, t["part"][:, :384]).astype(B))
     d0 = dot(t["wide"][...], t["dqkv"][:, 384:QUARTER])
     put(0, slice(0, EXP), slice(384, QUARTER), jnp.where(r8 < 6, d0, t["part2"][...]).astype(B))
+    ship(0, 0, P_DB0)
+    ship(1, 0, P_MOD)
 
     def bias_sums(i, _):
         rows = pl.ds(pl.multiple_of(i * 128, 128), 128)
@@ -379,12 +386,14 @@
         add_db(D, token_sum(t["dqkv"][rows, 2 * D :].astype(F)))
         return 0
 
-    lax.fori_loop(0, 4, bias_sums, 0)
+    lax.fori_loop(0, 4, bias_sums, 0, unroll=True)
+
+    t["dn"][...] = dot(t["dqkv"][...], main[:, C_QKV:C_PROJ], NT)
 
     def dlast(i, _):
         rows = pl.ds(pl.multiple_of(i * 128, 128), 128)
         lat = pl.ds(i // 2, 1)
-        dain = dot(t["dqkv"][rows, :], main[:, C_QKV:C_PROJ], NT)
+        dain = t["dn"][rows, :]
         n, inv = stats(x[rows, :].astype(F))
         add_mod(lat, 1, token_sum(dain * n))
         add_mod(lat, 0, token_sum(dain))
@@ -392,7 +401,7 @@
         dx[rows, :] = (t["dx1"][rows, :] + back).astype(B)
         return 0
 
-    lax.fori_loop(0, 4, dlast, 0)
+    lax.fori_loop(0, 4, dlast, 0, unroll=True)
 
     c = cond[...]
     sig = jax.nn.sigmoid(c)
@@ -422,6 +431,9 @@
     pick = ((feature - 6 * group_of(feature, 6)) == (lane & 7)) & (lane < 16)
     found = dot(both, pick.astype(F).astype(B))
     put(1, slice(0, EXP), slice(P_COND, P_HALF), jnp.where((r8 >> 2) == (lane >> 3), found, 0.0).astype(B))
+    ship(0, P_DB0, P_HALF)
+    ship(1, P_MOD, P_HALF)
+    finish()
 
 
 KEEP = (
@@ -447,6 +459,7 @@
     ("dz", (ROWS, FF), B),
     ("wide", (EXP, ROWS), B),
     ("dx1", (ROWS, D), F),
+    ("dn", (ROWS, D), F),
     ("datt", (ROWS, D), B),
     ("dqkv", (ROWS, 3 * D), B),
 )
@@ -500,12 +513,40 @@
         go(own)
 
 
-def pack_out(pack, keep, send, sems):
-    copies = [pltpu.make_async_copy(pack.at[i], ref, sems.at[i]) for i, ref in enumerate((keep, send))]
-    for copy in copies:
-        copy.start()
-    for copy in copies:
-        copy.wait()
+def sender(core, pack, keep, send, sems):
+    started = []
+
+    def start(half, first, last):
+        n = len(started)
+        cols = slice(first, last)
+
+        def copy(slot, ref):
+            return pltpu.make_async_copy(pack.at[slot, :, cols], ref.at[:, cols], sems.at[n])
+
+        mine = copy(0, keep)
+        theirs = copy(1, send)
+        started.append((half, mine, theirs))
+
+        @pl.when(core == half)
+        def _():
+            mine.start()
+
+        @pl.when(core != half)
+        def _():
+            theirs.start()
+
+    def finish():
+        for half, mine, theirs in started:
+
+            @pl.when(core == half)
+            def _(mine=mine):
+                mine.wait()
+
+            @pl.when(core != half)
+            def _(theirs=theirs):
+                theirs.wait()
+
+    return start, finish
 
 
 def putter(core, pack):
@@ -516,34 +557,43 @@
     return put
 
 
-def front_kernel(core, own, other, x, cond, *refs):
-    n_keep, n_w = len(KEEP), len(WEIGHTS)
-    y = refs[0]
-    k = named(KEEP, refs[1 : 1 + n_keep])
-    w = named(WEIGHTS, refs[1 + n_keep : 1 + n_keep + n_w])
-    mod, g, sel, selt, sems = refs[1 + n_keep + n_w :]
+def front_kernel(core, own, other, x, cond, y, *refs):
+    saved = KEEP + WEIGHTS + MOD
+    n = len(saved)
+    out = named(saved, refs[:n])
+    buf = named(saved, refs[n : 2 * n])
+    g, sel, selt, sems, save_sems = refs[2 * n :]
+    copies = []
+
+    def save(*names):
+        for name in names:
+            copy = pltpu.make_async_copy(buf[name], out[name], save_sems.at[len(copies)])
+            copy.start()
+            copies.append(copy)
+
+    build_selectors(sel, selt)
+    fetch_halves(core[0], own, other, g, sems)
+    ada = unpack(g, selt, buf)
+    save("main", "bias", "bias2", "fc2")
+    modulate(cond, g, selt, ada, buf["mod"])
+    save("mod")
+    forward(x, buf, buf["mod"], buf, y, save)
+    for copy in copies:
+        copy.wait()
+
+
+def turn_kernel(core, own, other, x, cond, grad, y, dx, dc, keep, send, *refs):
+    n_keep, n_w, n_t = len(KEEP), len(WEIGHTS), len(TEMPS)
+    k = named(KEEP, refs[:n_keep])
+    w = named(WEIGHTS, refs[n_keep : n_keep + n_w])
+    t = named(TEMPS, refs[n_keep + n_w : n_keep + n_w + n_t])
+    mod, g, sel, selt, pack, sems = refs[n_keep + n_w + n_t :]
     build_selectors(sel, selt)
     fetch_halves(core[0], own, other, g, sems)
     ada = unpack(g, selt, w)
     modulate(cond, g, selt, ada, mod)
     forward(x, w, mod, k, y)
-
-
-def turn_kernel(core, whole, x, cond, grad, y, dx, dc, keep, send, *refs):
-    n_keep, n_w, n_t = len(KEEP), len(WEIGHTS), len(TEMPS)
-    k = named(KEEP, refs[:n_keep])
-    w = named(WEIGHTS, refs[n_keep : n_keep + n_w])
-    t = named(TEMPS, refs[n_keep + n_w : n_keep + n_w + n_t])
-    mod, g, sel, selt, pack, sems = refs[n_keep + n_w + n_t :]
-    copy = pltpu.make_async_copy(whole, g, sems.at[0])
-    copy.start()
-    build_selectors(sel, selt)
-    copy.wait()
-    ada = unpack(g, selt, w)
-    modulate(cond, g, selt, ada, mod)
-    forward(x, w, mod, k, y)
-    backward(core[0], grad, x, cond, g, G_ADA, sel, selt, w, mod, k, t, dx, dc, putter(core[0], pack))
-    pack_out(pack, keep, send, sems)
+    backward(core[0], grad, x, cond, g, G_ADA, sel, selt, w, mod, k, t, dx, dc, putter(core[0], pack), *sender(core[0], pack, keep, send, sems))
 
 
 def back_kernel(core, own, other, x, cond, grad, *refs):
@@ -556,8 +606,7 @@
     g, sel, selt, pack, sems = refs[n_t:]
     build_selectors(sel, selt)
     fetch_ada(core[0], own, other, g, sems)
-    backward(core[0], grad, x, cond, g, 0, sel, selt, w, mod, k, t, dx, dc, putter(core[0], pack))
-    pack_out(pack, keep, send, sems)
+    backward(core[0], grad, x, cond, g, 0, sel, selt, w, mod, k, t, dx, dc, putter(core[0], pack), *sender(core[0], pack, keep, send, sems))
 
 
 VM = pl.BlockSpec(memory_space=pltpu.VMEM)
@@ -567,7 +616,7 @@
 G_BUF = pltpu.VMEM((EXP, G_END), B)
 ADA_BUF = pltpu.VMEM((EXP, G_BIAS - G_ADA), B)
 SEL_BUFS = [pltpu.VMEM((4, EXP, D), B), pltpu.VMEM((4, D, EXP), B)]
-SEMS = pltpu.SemaphoreType.DMA((2,))
+SEMS = pltpu.SemaphoreType.DMA((5,))
 ROWS_OUT = jax.ShapeDtypeStruct((ROWS, D), B)
 COND_OUT = jax.ShapeDtypeStruct((8, D), F)
 HALF_OUT = jax.ShapeDtypeStruct((EXP, P_HALF), B)
@@ -584,25 +633,26 @@
         front_kernel,
         out_shape=outs,
         in_specs=[SM, ANY, ANY, VM, VM],
-        out_specs=[VM] * len(outs),
-        scratch_shapes=[G_BUF, *SEL_BUFS, SEMS],
+        out_specs=[VM] + [ANY] * (len(outs) - 1),
+        scratch_shapes=buffers(KEEP + WEIGHTS + MOD)
+        + [G_BUF, *SEL_BUFS, SEMS, pltpu.SemaphoreType.DMA((len(outs) - 1,))],
         compiler_params=PARAMS,
         cost_estimate=cost(1),
         name="front",
     )(core, own, other, x, cond)
 
 
-def turn(core, whole, x, cond, grad):
+def turn(core, own, other, x, cond, grad):
     return pl.pallas_call(
         turn_kernel,
         out_shape=[ROWS_OUT, ROWS_OUT, COND_OUT, HALF_OUT, HALF_OUT],
-        in_specs=[SM, ANY, VM, VM, VM],
+        in_specs=[SM, ANY, ANY, VM, VM, VM],
         out_specs=[VM] * 3 + [ANY] * 2,
         scratch_shapes=buffers(KEEP) + buffers(WEIGHTS) + buffers(TEMPS) + buffers(MOD) + [G_BUF, *SEL_BUFS, PACK_BUF, SEMS],
         compiler_params=PARAMS,
         cost_estimate=cost(3),
         name="turn",
-    )(core, whole, x, cond, grad)
+    )(core, own, other, x, cond, grad)
 
 
 def back(core, own, other, x, cond, grad, kept):
@@ -618,31 +668,47 @@
     )(core, own, other, x, cond, grad, *kept)
 
 
+def line_up_kernel(w_qkv, w_proj, w_fc1, w_fc2, w_ada, bias, out, main, ada):
+    def rows(ref, first, last):
+        return ref[:, first:last].astype(F)
+
+    main[0:6, :] = rows(w_qkv, 0, QUARTER)
+    main[6:12, :384] = rows(w_qkv, QUARTER, C_PROJ)
+    main[6:12, 384:] = rows(w_proj, 0, D)
+    main[12:18, :] = rows(w_fc1, 0, QUARTER)
+    main[18:24, :] = rows(w_fc1, QUARTER, FF)
+    ada[48:56, :] = jnp.zeros((8, 256), F)
+    for i in range(9):
+        ada[6 * i : 6 * i + 6, :] = rows(w_ada, 256 * i, 256 * i + 256)
+    for a in range(3):
+        out[:, a * QUARTER : (a + 1) * QUARTER] = main[8 * a : 8 * a + 8, :].astype(B)
+        out[:, G_FC2 + a * D : G_FC2 + (a + 1) * D] = w_fc2[8 * a : 8 * a + 8, :]
+    for a in range(7):
+        out[:, G_ADA + a * 256 : G_ADA + (a + 1) * 256] = ada[8 * a : 8 * a + 8, :].astype(B)
+    first = lax.broadcasted_iota(jnp.int32, (8, 1), 0) == 0
+    out[:, G_BIAS:G_END] = jnp.where(first, bias[...].astype(F), 0.0).astype(B)
+
+
 def line_up(w_qkv, b_qv, w_proj, b_proj, w_fc1, b_fc1, w_fc2, b_fc2, w_ada, b_ada):
-    def pieces(rows):
-        rows = jnp.concatenate(rows, axis=0)
-        rows = jnp.pad(rows, ((0, -rows.shape[0] % 8), (0, 0)))
-        return [rows[i : i + 8] for i in range(0, rows.shape[0], 8)]
-
-    main = jnp.concatenate([w_qkv, w_proj, w_fc1], axis=1)
-    bias = jnp.concatenate([b_qv, b_proj, b_fc1, b_fc2, b_ada])
-    bias = jnp.pad(bias, (0, 1024 - bias.shape[0])).reshape(8, 128)
-    return jnp.concatenate(
-        pieces([main[:, i * QUARTER : (i + 1) * QUARTER] for i in range(4)])
-        + pieces([w_fc2])
-        + pieces([w_ada[:, i * 256 : (i + 1) * 256] for i in range(9)])
-        + [bias],
-        axis=1,
-    )
+    bias = jnp.concatenate([b_qv, b_proj, b_fc1, b_fc2, b_ada, jnp.zeros((44,), B)]).reshape(1, 128)
+    return pl.pallas_call(
+        line_up_kernel,
+        out_shape=jax.ShapeDtypeStruct((8, G_END), B),
+        in_specs=[VM] * 6,
+        out_specs=VM,
+        scratch_shapes=[pltpu.VMEM((24, QUARTER), F), pltpu.VMEM((56, 256), F)],
+        name="line_up",
+    )(w_qkv, w_proj, w_fc1, w_fc2, w_ada, bias)
 
 
 def swap(x):
     return lax.ppermute(x, "pipe", [(0, 1), (1, 0)])
 
 
-def to_all(block):
-    copies = jnp.broadcast_to(block[None], (CHIPS, *block.shape))
-    return lax.all_to_all(copies, "shard", 0, 0, tiled=True).reshape(EXP, block.shape[1])
+def to_all(blocks):
+    copies = jnp.broadcast_to(blocks[None], (CHIPS, *blocks.shape))
+    came = lax.all_to_all(copies, "shard", 0, 0, tiled=True)
+    return [came[:, i].reshape(EXP, blocks.shape[2]) for i in range(2)]
 
 
 def scatter(block):
@@ -656,18 +722,18 @@
     core = p.reshape(1).astype(jnp.int32)
     block = line_up(w_qkv[0], b_qv[0], w_proj[0], b_proj[0], w_fc1[0], b_fc1[0], w_fc2[0], b_fc2[0], w_ada[0], b_ada[0])
     block_other = swap(block)
-    block1 = jnp.where(first, block_other, block)
-    own1 = lax.all_gather(block1, "shard", tiled=True)
-    half0 = jnp.where(first, block[:, :G_HALF], block_other[:, G_HALF:])
-    own0 = to_all(half0)
+    low = jnp.where(first, block[:, :G_HALF], block_other[:, G_HALF:])
+    high = jnp.where(first, block_other[:, :G_HALF], block[:, G_HALF:])
+    own0, own1 = to_all(jnp.stack([low, high]))
     other0 = swap(own0)
+    other1 = swap(own1)
     x = lax.dynamic_index_in_dim(latents, p, 0, keepdims=False).reshape(ROWS, D)
     cot = lax.dynamic_index_in_dim(cotangent, p, 0, keepdims=False).reshape(ROWS, D)
     cond = lax.dynamic_index_in_dim(conditions, p, 0, keepdims=False).astype(F)
     cond = jnp.concatenate([cond, jnp.zeros((6, D), F)], axis=0)
 
     h, *kept = front(core, own0, other0, x, cond)
-    y, dx1, dc1, keep1, send1 = turn(core, own1, h, cond, cot)
+    y, dx1, dc1, keep1, send1 = turn(core, own1, other1, h, cond, cot)
     parts1 = scatter(keep1 + swap(send1))
     dx0, dc0, keep0, send0 = back(core, own0, other0, x, cond, dx1, kept)
     parts1, send0 = lax.optimization_barrier((parts1, send0))

time: 281 us -> 270 us (0.961); the launches traced: 280 us -> 265 us
  blocking collectives: 48 us -> 76.1 us
  Pallas kernels: 95.3 us -> 76.5 us
  between operations: 14.3 us -> 1.13 us
  waiting for transfers between devices: 58 us -> 53.3 us
  starting transfers between devices: 24.8 us -> 21.6 us
    all_to_all x1, blocking collectives: 48 us -> 76.1 us  [to_all(): came = lax.all_to_all(copies, 'shard', 0, 0, tiled=True)]
    all_gather x1 -> x0, waiting for transfers between devices: 16.6 us -> none  [shards(): own1 = lax.all_gather(block1, 'shard', tiled=True)]
    pallas_call x1, Pallas kernels: 41.5 us -> 32.6 us  [turn(): pl.pallas_call(turn_kernel, out_shape=[ROWS_OUT, ROWS_OUT, COND_OUT, HALF...]
    all_to_all x2, waiting for transfers between devices: 29.4 us -> 36.1 us  [scatter(): lax.all_to_all(block.reshape(CHIPS, 8, P_HALF), 'shard', 0, 0, tiled=True)]
    pallas_call x1, Pallas kernels: 30.3 us -> 24 us  [back(): pl.pallas_call(back_kernel, out_shape=[ROWS_OUT, COND_OUT, HALF_OUT, HALF...]
    ppermute x8 -> x9, waiting for transfers between devices: 12.1 us -> 17.1 us  [swap(): return lax.ppermute(x, 'pipe', [(0, 1), (1, 0)])]
    pallas_call x1, Pallas kernels: 23.5 us -> 18.5 us  [front(): pl.pallas_call(front_kernel, out_shape=outs, in_specs=[SM, ANY, ANY, VM,...]
    ppermute x8 -> x9, starting transfers between devices: 11.5 us -> 9.53 us  [swap(): return lax.ppermute(x, 'pipe', [(0, 1), (1, 0)])]
  transfers between devices with their start and end apart: 11 -> 11, of which waited for: 7 -> 6; matrix products, arithmetic and copies ran while one was open for 7% -> 6% of each run, Pallas kernels for 19% -> 16%
where the time goes in v4:
time: 270 us; the launch traced here: 265 us
  Pallas kernels  76.5 us (28%)
  blocking collectives  76.1 us (28%)
  waiting for transfers between devices  53.3 us (20%)
  other arithmetic  21.8 us (8%)
  starting transfers between devices  21.6 us (8%)
  local copies, waits for them, and re-layouts  12.6 us (5%)
    all_to_all x1, blocking collectives, to_all(): came = lax.all_to_all(copies, 'shard', 0, 0, tiled=True)  76.1 us
    all_to_all x2, waiting for transfers between devices, scatter(): lax.all_to_all(block.reshape(CHIPS, 8, P_HALF), 'shard', 0, 0, tiled=True)  36.1 us
    pallas_call x1, Pallas kernels, turn(): pl.pallas_call(turn_kernel, out_shape=[ROWS_OUT, ROWS_OUT, COND_OUT, HALF...  32.6 us
    pallas_call x1, Pallas kernels, back(): pl.pallas_call(back_kernel, out_shape=[ROWS_OUT, COND_OUT, HALF_OUT, HALF...  24 us
    pallas_call x1, Pallas kernels, front(): pl.pallas_call(front_kernel, out_shape=outs, in_specs=[SM, ANY, ANY, VM,...  18.5 us
    ppermute x9, waiting for transfers between devices, swap(): return lax.ppermute(x, 'pipe', [(0, 1), (1, 0)])  17.1 us
    all_to_all x2, starting transfers between devices, scatter(): lax.all_to_all(block.reshape(CHIPS, 8, P_HALF), 'shard', 0, 0, tiled=True)  12.1 us
    ppermute x9, starting transfers between devices, swap(): return lax.ppermute(x, 'pipe', [(0, 1), (1, 0)])  9.53 us
  transfers between devices with their start and end apart: 11, of which 6 were waited for; matrix products, arithmetic and copies ran while one was open for 6% of the time, Pallas kernels for 16%

profile of v4, /device:TPU:1, one launch (start us, length us, event | category | flops | bytes accessed | tf_op | source)
XLA Modules:
  0.0 265.0 jit_solution(9819657706523364267)
XLA Ops:
  0.7 3.9 %concatenate.67 = bf16[128]{0:T(256)(128)(2,1)} concatenate(bf16[12]{0:T(256)(128)(2,1)} %bitcast.64, bf16[6]{0:T(256)(128)(2,1)} %bitcast.65, bf16[24]{0:T(256)(128)(2,1)} %bitcast.66, bf16[6]{0:T(256)(128)(2,1)} %bitcast.67, bf16[36]{0:T(256)(128)(2,1)} %bitcast.68, bf16[44]{0:T(256)(128)(2,1)S(1)} %broadcast_in_dim.40), dimensions={0} | concatenate | bytes 512 | tf_op jit(solution)/shard_map/concatenate | solution.py:693
  9.9 76.1 %all_to_all.15 = bf16[64,2,8,2688]{3,2,1,0:T(8,128)(2,1)S(1)} all-to-all(bf16[64,2,8,2688]{3,2,1,0:T(8,128)(2,1)S(1)} %broadcast_in_dim.41), channel_id=1, replica_groups=mesh['pipe'=2,'shard'=64] {'shard'}, dimensions={0} | all-to-all | bytes 11010048 | tf_op jit(solution)/shard_map/all_to_all | solution.py:710
  86.0 1.9 slice_bitcast_fusion.1
  88.0 2.2 collective-permute-start.1
  90.8 2.0 constant_dynamic-slice_fusion
  92.8 6.1 %collective-permute-done.1.other = bf16[512,2688]{1,0:T(8,128)(2,1)} collective-permute-done((bf16[512,2688]{1,0:T(8,128)(2,1)S(1)}, bf16[512,2688]{1,0:T(8,128)(2,1)}, u32[]{:S(2)}, u32[]{:S(2)}) %collective-permute-start.1) | collective-permute-done | bytes 2752544 | tf_op jit(solution)/shard_map/ppermute | solution.py:705
  99.0 18.5 %front.1 = (bf16[512,384]{1,0:T(8,128)(2,1)}, bf16[512,384]{1,0:T(8,128)(2,1)}, bf16[512,1152]{1,0:T(8,128)(2,1)}, f32[6,8,256]{2,1,0:T(8,128)}, bf16[512,384]{1...) custom-call(s32[1]{0:T(128)} %bitcast.core, ...), custom_call_target="tpu_custom_call" | custom-call | flops 2000000000 | bytes 10000000 | tf_op jit(solution)/shard_map/front/pallas_call | solution.py:632
  117.4 32.6 %turn.1 = (bf16[512,384]{1,0:T(8,128)(2,1)}, bf16[512,384]{1,0:T(8,128)(2,1)}, f32[8,384]{1,0:T(8,128)}, bf16[512,2560]{1,0:T(8,128)(2,1)}, bf16[512,2560]{1,0:T(8,128)(2,1)}) custom-call(s32[1]{0:T(128)} %bitcast.core, bf16[512,2688]{1,0:T(8,128)(2,1)} %get-tuple-element.70.own, bf16[512,2688]{1,0:T(8,128)(2,1)} %collective-permute-done.2.other, ...), custom_call_target="tpu_custom_call" | custom-call | flops 6000000000 | bytes 30000000 | tf_op jit(solution)/shard_map/turn/pallas_call | solution.py:646
  150.1 5.1 %collective-permute-done.6 = bf16[512,2560]{1,0:T(8,128)(2,1)S(1)} collective-permute-done((bf16[512,2560]{1,0:T(8,128)(2,1)}, bf16[512,2560]{1,0:T(8,128)(2,1)S(1)}, u32[]{:S(2)}, u32[]{:S(2)}) %collective-permute-start.6) | collective-permute-done | bytes 2621472 | tf_op jit(solution)/shard_map/ppermute | solution.py:705
  155.2 3.6 %add_bitcast_fusion.1 = bf16[64,8,2560]{2,1,0:T(8,128)(2,1)} fusion(bf16[512,2560]{1,0:T(8,128)(2,1)} %get-tuple-element.62, bf16[512,2560]{1,0:T(8,128)(2,1)S(1)} %collective-permute-done.6), kind=kLoop, calls=%fused_computation.5 | loop fusion | flops 1310720 | bytes 7864320 | tf_op jit(solution)/shard_map/reshape | solution.py:715
  158.8 5.4 %all-to-all-start.1 = ((bf16[64,8,2560]{2,1,0:T(8,128)(2,1)}), bf16[64,8,2560]{2,1,0:T(8,128)(2,1)S(1)}, u32[]{:S(2)}, u32[]{:S(2)}) async-start(bf16[64,8,2560]{2,1,0:T(8,128)(2,1)} %add_bitcast_fusion.1), calls=%async_computation.1 | async-start | bytes 5242880 | tf_op jit(solution)/shard_map/all_to_all | solution.py:715
  164.2 24.0 %back.1 = (bf16[512,384]{1,0:T(8,128)(2,1)}, f32[8,384]{1,0:T(8,128)}, bf16[512,2560]{1,0:T(8,128)(2,1)}, bf16[512,2560]{1,0:T(8,128)(2,1)}) custom-call(s32[1]{0:T(128)} %bitcast.core, bf16[512,2688]{1,0:T(8,128)(2,1)} %copy-done.2, bf16[512,2688]{1,0:T(8,128)(2,1)} %collective-permute-done.1.other, bf16[512,384]{1,0:T(8,128)(2,1)} %bitcast.54, ...), custom_call_target="tpu_custom_call" | custom-call | flops 4000000000 | bytes 20000000 | tf_op jit(solution)/shard_map/back/pallas_call | solution.py:659
  188.2 9.7 %all-to-all-done.1 = bf16[64,8,2560]{2,1,0:T(8,128)(2,1)S(1)} async-done(((bf16[64,8,2560]{2,1,0:T(8,128)(2,1)}), bf16[64,8,2560]{2,1,0:T(8,128)(2,1)S(1)}, u32[]{:S(2)}, u32[]{:S(2)}) %all-to-all-start.1) | async-done | bytes 2621472 | tf_op jit(solution)/shard_map/all_to_all | solution.py:715
  197.8 2.1 collective-permute-start.7
  200.0 4.7 %collective-permute-done.7 = bf16[512,2560]{1,0:T(8,128)(2,1)S(1)} collective-permute-done((bf16[512,2560]{1,0:T(8,128)(2,1)}, bf16[512,2560]{1,0:T(8,128)(2,1)S(1)}, u32[]{:S(2)}, u32[]{:S(2)}) %collective-permute-start.7) | collective-permute-done | bytes 2621472 | tf_op jit(solution)/shard_map/ppermute | solution.py:705
  204.7 3.5 %add_bitcast_fusion = bf16[64,8,2560]{2,1,0:T(8,128)(2,1)} fusion(bf16[512,2560]{1,0:T(8,128)(2,1)} %get-tuple-element.61, bf16[512,2560]{1,0:T(8,128)(2,1)S(1)} %collective-permute-done.7), kind=kLoop, calls=%fused_computation.4 | loop fusion | flops 1310720 | bytes 7864320 | tf_op jit(solution)/shard_map/reshape | solution.py:715
  208.2 6.8 %all-to-all-start.2 = ((bf16[64,8,2560]{2,1,0:T(8,128)(2,1)}), bf16[64,8,2560]{2,1,0:T(8,128)(2,1)}, u32[]{:S(2)}, u32[]{:S(2)}) async-start(bf16[64,8,2560]{2,1,0:T(8,128)(2,1)} %add_bitcast_fusion), calls=%async_computation.2 | async-start | bytes 5242880 | tf_op jit(solution)/shard_map/all_to_all | solution.py:715
  216.4 1.9 broadcast_select_fusion.1
  218.2 1.9 broadcast_select_fusion.3
  222.0 26.5 %all-to-all-done.2 = bf16[64,8,2560]{2,1,0:T(8,128)(2,1)} async-done(((bf16[64,8,2560]{2,1,0:T(8,128)(2,1)}), bf16[64,8,2560]{2,1,0:T(8,128)(2,1)}, u32[]{:S(2)}, u32[]{:S(2)}) %all-to-all-start.2) | async-done | bytes 2621472 | tf_op jit(solution)/shard_map/all_to_all | solution.py:715
  250.1 2.1 convert_reduce_fusion.1
  252.3 2.5 collective-permute-start.8
  254.7 2.2 maximum_select_fusion.1
  256.9 2.2 maximum_select_fusion
  (58 shorter events, 16.5 us)
Async XLA Ops:
  0.6 89.6 %copy-start = (bf16[2,2,384]{2,1,0:T(2,128)(2,1)S(1)}, bf16[2,2,384]{2,1,0:T(2,128)(2,1)}, u32[]{:S(2)}) copy-start(bf16[2,2,384]{2,1,0:T(2,128)(2,1)} %param.14) | copy-start | bytes 9220
  6.1 2.6 collective-permute-start
  86.0 4.8 %copy-start.4 = (bf16[2,2,256,384]{3,2,1,0:T(8,128)(2,1)S(1)}, bf16[2,2,256,384]{3,2,1,0:T(8,128)(2,1)}, u32[]{:S(2)}) copy-start(bf16[2,2,256,384]{3,2,1,0:T(8,128)(2,1)} %param.15) | copy-start | bytes 2359300
  88.0 11.0 %copy-start.2 = (bf16[512,2688]{1,0:T(8,128)(2,1)}, bf16[512,2688]{1,0:T(8,128)(2,1)S(1)}, u32[]{:S(2)}) copy-start(bf16[512,2688]{1,0:T(8,128)(2,1)S(1)} %get-tuple-element.69.own) | copy-start | bytes 8257540
  88.0 11.0 %collective-permute-start.1 = (bf16[512,2688]{1,0:T(8,128)(2,1)S(1)}, bf16[512,2688]{1,0:T(8,128)(2,1)}, u32[]{:S(2)}, u32[]{:S(2)}) collective-permute-start(bf16[512,2688]{1,0:T(8,128)(2,1)S(1)} %get-tuple-element.69.own), channel_id=1, source_target_pairs={{0,64},{64,0},{1,65},{65,1},{2,66},{66,2},{3,67},{67,3},{4,68},{68... | collective-permute-start | bytes 8257544 | tf_op jit(solution)/shard_map/ppermute | solution.py:705
  90.2 27.2 %collective-permute-start.2 = (bf16[512,2688]{1,0:T(8,128)(2,1)}, bf16[512,2688]{1,0:T(8,128)(2,1)}, u32[]{:S(2)}, u32[]{:S(2)}) collective-permute-start(bf16[512,2688]{1,0:T(8,128)(2,1)} %get-tuple-element.70.own), channel_id=1, source_target_pairs={{0,64},{64,0},{1,65},{65,1},{2,66},{66,2},{3,67},{67,3},{4,68},{68... | collective-permute-start | bytes 8257544 | tf_op jit(solution)/shard_map/ppermute | solution.py:705
  150.0 5.2 %collective-permute-start.6 = (bf16[512,2560]{1,0:T(8,128)(2,1)}, bf16[512,2560]{1,0:T(8,128)(2,1)S(1)}, u32[]{:S(2)}, u32[]{:S(2)}) collective-permute-start(bf16[512,2560]{1,0:T(8,128)(2,1)} %get-tuple-element.63), channel_id=1, source_target_pairs={{0,64},{64,0},{1,65},{65,1},{2,66},{66,2},{3,67},{67,3},{4,68},{68... | collective-permute-start | bytes 7864328 | tf_op jit(solution)/shard_map/ppermute | solution.py:705
  158.8 39.0 %all-to-all-start.1 = ((bf16[64,8,2560]{2,1,0:T(8,128)(2,1)}), bf16[64,8,2560]{2,1,0:T(8,128)(2,1)S(1)}, u32[]{:S(2)}, u32[]{:S(2)}) async-start(bf16[64,8,2560]{2,1,0:T(8,128)(2,1)} %add_bitcast_fusion.1), calls=%async_computation.1 | async-start | bytes 5242880 | tf_op jit(solution)/shard_map/all_to_all | solution.py:715
  197.8 6.9 %collective-permute-start.7 = (bf16[512,2560]{1,0:T(8,128)(2,1)}, bf16[512,2560]{1,0:T(8,128)(2,1)S(1)}, u32[]{:S(2)}, u32[]{:S(2)}) collective-permute-start(bf16[512,2560]{1,0:T(8,128)(2,1)} %get-tuple-element.65), channel_id=1, source_target_pairs={{0,64},{64,0},{1,65},{65,1},{2,66},{66,2},{3,67},{67,3},{4,68},{68... | collective-permute-start | bytes 7864328 | tf_op jit(solution)/shard_map/ppermute | solution.py:705
  208.2 8.2 %copy-start.3 = (bf16[512,384]{1,0:T(8,128)(2,1)S(1)}, bf16[512,384]{1,0:T(8,128)(2,1)}, u32[]{:S(2)}) copy-start(bf16[512,384]{1,0:T(8,128)(2,1)} %get-tuple-element.42.grad) | copy-start | bytes 1179652
  208.2 40.2 %all-to-all-start.2 = ((bf16[64,8,2560]{2,1,0:T(8,128)(2,1)}), bf16[64,8,2560]{2,1,0:T(8,128)(2,1)}, u32[]{:S(2)}, u32[]{:S(2)}) async-start(bf16[64,8,2560]{2,1,0:T(8,128)(2,1)} %add_bitcast_fusion), calls=%async_computation.2 | async-start | bytes 5242880 | tf_op jit(solution)/shard_map/all_to_all | solution.py:715
  215.7 5.0 %collective-permute-start.5 = (f32[2,384]{1,0:T(2,128)S(1)}, f32[2,384]{1,0:T(2,128)S(1)}, u32[]{:S(2)}, u32[]{:S(2)}) collective-permute-start(f32[2,384]{1,0:T(2,128)S(1)} %slice_add_fusion), channel_id=1, source_target_pairs={{0,64},{64,0},{1,65},{65,1},{2,66},{66,2},{3,67},{67,3},{4,68},{68... | collective-permute-start | bytes 9224 | tf_op jit(solution)/shard_map/ppermute | solution.py:705
  218.2 36.5 %collective-permute-start.4 = (bf16[512,384]{1,0:T(8,128)(2,1)}, bf16[512,384]{1,0:T(8,128)(2,1)}, u32[]{:S(2)}, u32[]{:S(2)}) collective-permute-start(bf16[512,384]{1,0:T(8,128)(2,1)} %get-tuple-element.72), channel_id=1, source_target_pairs={{0,64},{64,0},{1,65},{65,1},{2,66},{66,2},{3,67},{67,3},{4,68},{68... | collective-permute-start | bytes 1179656 | tf_op jit(solution)/shard_map/ppermute | solution.py:705
  220.2 36.7 %collective-permute-start.3 = (bf16[512,384]{1,0:T(8,128)(2,1)}, bf16[512,384]{1,0:T(8,128)(2,1)}, u32[]{:S(2)}, u32[]{:S(2)}) collective-permute-start(bf16[512,384]{1,0:T(8,128)(2,1)} %get-tuple-element.74), channel_id=1, source_target_pairs={{0,64},{64,0},{1,65},{65,1},{2,66},{66,2},{3,67},{67,3},{4,68},{68... | collective-permute-start | bytes 1179656 | tf_op jit(solution)/shard_map/ppermute | solution.py:705
  252.2 12.5 %copy-start.1 = (bf16[2,2,384]{2,1,0:T(2,128)(2,1)S(1)}, bf16[2,2,384]{2,1,0:T(2,128)(2,1)}, u32[]{:S(2)}) copy-start(bf16[2,2,384]{2,1,0:T(2,128)(2,1)} %param.14) | copy-start | bytes 9220
  252.3 6.8 %collective-permute-start.8 = (f32[8,4864]{1,0:T(8,128)S(1)}, f32[8,4864]{1,0:T(8,128)S(1)}, u32[]{:S(2)}, u32[]{:S(2)}) collective-permute-start(f32[8,4864]{1,0:T(8,128)S(1)} %fusion.6), channel_id=1, source_target_pairs={{0,64},{64,0},{1,65},{65,1},{2,66},{66,2},{3,67},{67,3},{4,68},{68... | collective-permute-start | bytes 466952 | tf_op jit(solution)/shard_map/ppermute | solution.py:705

commit v5 on v4

--- a/solution.py
+++ b/solution.py
@@ -668,7 +668,7 @@
     )(core, own, other, x, cond, grad, *kept)
 
 
-def line_up_kernel(w_qkv, w_proj, w_fc1, w_fc2, w_ada, bias, out, main, ada):
+def line_up_kernel(w_qkv, w_proj, w_fc1, w_fc2, w_ada, b_qv, b_proj, b_fc1, b_fc2, b_ada, out, main, ada, bias):
     def rows(ref, first, last):
         return ref[:, first:last].astype(F)
 
@@ -685,30 +685,31 @@
         out[:, G_FC2 + a * D : G_FC2 + (a + 1) * D] = w_fc2[8 * a : 8 * a + 8, :]
     for a in range(7):
         out[:, G_ADA + a * 256 : G_ADA + (a + 1) * 256] = ada[8 * a : 8 * a + 8, :].astype(B)
-    first = lax.broadcasted_iota(jnp.int32, (8, 1), 0) == 0
-    out[:, G_BIAS:G_END] = jnp.where(first, bias[...].astype(F), 0.0).astype(B)
+    bias[...] = jnp.zeros((8, 128), F)
+    for ref, (lane, width) in zip((b_qv, b_proj, b_fc1, b_fc2, b_ada), BIASES):
+        bias[0:1, lane : lane + width] = ref[...].astype(F)
+    out[:, G_BIAS:G_END] = bias[...].astype(B)
 
 
 def line_up(w_qkv, b_qv, w_proj, b_proj, w_fc1, b_fc1, w_fc2, b_fc2, w_ada, b_ada):
-    bias = jnp.concatenate([b_qv, b_proj, b_fc1, b_fc2, b_ada, jnp.zeros((44,), B)]).reshape(1, 128)
+    biases = [b.reshape(1, -1) for b in (b_qv, b_proj, b_fc1, b_fc2, b_ada)]
     return pl.pallas_call(
         line_up_kernel,
         out_shape=jax.ShapeDtypeStruct((8, G_END), B),
-        in_specs=[VM] * 6,
+        in_specs=[VM] * 10,
         out_specs=VM,
-        scratch_shapes=[pltpu.VMEM((24, QUARTER), F), pltpu.VMEM((56, 256), F)],
+        scratch_shapes=[pltpu.VMEM((24, QUARTER), F), pltpu.VMEM((56, 256), F), pltpu.VMEM((8, 128), F)],
         name="line_up",
-    )(w_qkv, w_proj, w_fc1, w_fc2, w_ada, bias)
+    )(w_qkv, w_proj, w_fc1, w_fc2, w_ada, *biases)
 
 
 def swap(x):
     return lax.ppermute(x, "pipe", [(0, 1), (1, 0)])
 
 
-def to_all(blocks):
-    copies = jnp.broadcast_to(blocks[None], (CHIPS, *blocks.shape))
-    came = lax.all_to_all(copies, "shard", 0, 0, tiled=True)
-    return [came[:, i].reshape(EXP, blocks.shape[2]) for i in range(2)]
+def to_all(block):
+    copies = jnp.broadcast_to(block[None], (CHIPS, *block.shape))
+    return lax.all_to_all(copies, "shard", 0, 0, tiled=True).reshape(EXP, block.shape[1])
 
 
 def scatter(block):
@@ -724,15 +725,18 @@
     block_other = swap(block)
     low = jnp.where(first, block[:, :G_HALF], block_other[:, G_HALF:])
     high = jnp.where(first, block_other[:, :G_HALF], block[:, G_HALF:])
-    own0, own1 = to_all(jnp.stack([low, high]))
+    own0 = to_all(low)
     other0 = swap(own0)
-    other1 = swap(own1)
+    high, own0 = lax.optimization_barrier((high, own0))
+    own1 = to_all(high)
     x = lax.dynamic_index_in_dim(latents, p, 0, keepdims=False).reshape(ROWS, D)
     cot = lax.dynamic_index_in_dim(cotangent, p, 0, keepdims=False).reshape(ROWS, D)
     cond = lax.dynamic_index_in_dim(conditions, p, 0, keepdims=False).astype(F)
     cond = jnp.concatenate([cond, jnp.zeros((6, D), F)], axis=0)
 
     h, *kept = front(core, own0, other0, x, cond)
+    h, own1 = lax.optimization_barrier((h, own1))
+    other1 = swap(own1)
     y, dx1, dc1, keep1, send1 = turn(core, own1, other1, h, cond, cot)
     parts1 = scatter(keep1 + swap(send1))
     dx0, dc0, keep0, send0 = back(core, own0, other0, x, cond, dx1, kept)
@@ -750,6 +754,10 @@
     dc = (dc0 + dc1)[:2]
     dc_other = swap(dc)
     cond_grad = jnp.where(first, jnp.stack([dc, dc_other]), jnp.stack([dc_other, dc]))
+
+    parts0, section_outputs, input_grads, cond_grad = lax.optimization_barrier(
+        (parts0, section_outputs, input_grads, cond_grad)
+    )
 
     def reduced(parts):
         lot = jnp.sum(parts.astype(F), axis=0)

time: 270 us -> 254 us (0.941)
  blocking collectives: 76.1 us -> 47.1 us
  waiting for transfers between devices: 53.3 us -> 66.2 us
  starting transfers between devices: 21.6 us -> 31.5 us
  local copies, waits for them, and re-layouts: 12.6 us -> 7.98 us
  other arithmetic: 21.8 us -> 18.1 us
    all_to_all x1, blocking collectives: 76.1 us -> 47.1 us  [to_all(): lax.all_to_all(copies, 'shard', 0, 0, tiled=True)]
    all_to_all x0 -> x1, waiting for transfers between devices: none -> 15.4 us  [to_all(): lax.all_to_all(copies, 'shard', 0, 0, tiled=True)]
    all_to_all x0 -> x1, starting transfers between devices: none -> 6.22 us  [to_all(): lax.all_to_all(copies, 'shard', 0, 0, tiled=True)]
    concatenate x1 -> x0, local copies, waits for them, and re-layouts: 3.94 us -> none  [line_up(): jnp.concatenate([b_qv, b_proj, b_fc1, b_fc2, b_ada, jnp.zeros((44,), B)])]
  transfers between devices with their start and end apart: 11 -> 12, of which waited for: 6 -> 9; matrix products, arithmetic and copies ran while one was open for 6% -> 4% of each run, Pallas kernels for 16% -> 17%
where the time goes in v5:
time: 254 us; the launch traced here: 250 us
  Pallas kernels  76 us (30%)
  waiting for transfers between devices  66.2 us (26%)
  blocking collectives  47.1 us (19%)
  starting transfers between devices  31.5 us (12%)
  other arithmetic  18.1 us (7%)
  local copies, waits for them, and re-layouts  7.98 us (3%)
  matrix products  2.55 us (1%)
    all_to_all x1, blocking collectives, to_all(): lax.all_to_all(copies, 'shard', 0, 0, tiled=True)  47.1 us
    all_to_all x2, waiting for transfers between devices, scatter(): lax.all_to_all(block.reshape(CHIPS, 8, P_HALF), 'shard', 0, 0, tiled=True)  33.8 us
    pallas_call x1, Pallas kernels, turn(): pl.pallas_call(turn_kernel, out_shape=[ROWS_OUT, ROWS_OUT, COND_OUT, HALF...  32.2 us
    pallas_call x1, Pallas kernels, back(): pl.pallas_call(back_kernel, out_shape=[ROWS_OUT, COND_OUT, HALF_OUT, HALF...  23.9 us
    pallas_call x1, Pallas kernels, front(): pl.pallas_call(front_kernel, out_shape=outs, in_specs=[SM, ANY, ANY, VM,...  18.3 us
    ppermute x9, waiting for transfers between devices, swap(): return lax.ppermute(x, 'pipe', [(0, 1), (1, 0)])  17.1 us
    all_to_all x1, waiting for transfers between devices, to_all(): lax.all_to_all(copies, 'shard', 0, 0, tiled=True)  15.4 us
    all_to_all x2, starting transfers between devices, scatter(): lax.all_to_all(block.reshape(CHIPS, 8, P_HALF), 'shard', 0, 0, tiled=True)  13.5 us
  transfers between devices with their start and end apart: 12, of which 9 were waited for; matrix products, arithmetic and copies ran while one was open for 4% of the time, Pallas kernels for 17%

profile of v5, /device:TPU:1, one launch (start us, length us, event | category | flops | bytes accessed | tf_op | source)
XLA Modules:
  0.0 250.4 jit_solution(7055857557785543720)
XLA Ops:
  0.7 1.7 line_up.1
  2.3 1.4 collective-permute-start
  5.9 47.1 %all_to_all.20 = bf16[64,8,2688]{2,1,0:T(8,128)(2,1)S(1)} all-to-all(bf16[64,8,2688]{2,1,0:T(8,128)(2,1)S(1)} %broadcast_in_dim.43), channel_id=1, replica_groups=mesh['pipe'=2,'shard'=64] {'shard'}, dimensions={0} | all-to-all | bytes 5505024 | tf_op jit(solution)/shard_map/all_to_all | solution.py:712
  53.0 2.0 collective-permute-start.1
  55.0 1.8 broadcast_in_dim.44
  56.8 6.2 %all-to-all-start.1 = ((bf16[64,8,2688]{2,1,0:T(8,128)(2,1)}), bf16[64,8,2688]{2,1,0:T(8,128)(2,1)}, u32[]{:S(2)}, u32[]{:S(2)}) async-start(bf16[64,8,2688]{2,1,0:T(8,128)(2,1)} %broadcast_in_dim.44), calls=%async_computation.1 | async-start | bytes 5505024 | tf_op jit(solution)/shard_map/all_to_all | solution.py:712
  64.5 18.3 %front.1 = (bf16[512,384]{1,0:T(8,128)(2,1)}, bf16[512,384]{1,0:T(8,128)(2,1)}, bf16[512,1152]{1,0:T(8,128)(2,1)}, f32[6,8,256]{2,1,0:T(8,128)}, bf16[512,384]{1...) custom-call(s32[1]{0:T(128)} %bitcast.core, ...), custom_call_target="tpu_custom_call" | custom-call | flops 2000000000 | bytes 10000000 | tf_op jit(solution)/shard_map/front/pallas_call | solution.py:632
  82.7 15.4 %all-to-all-done.1 = bf16[64,8,2688]{2,1,0:T(8,128)(2,1)} async-done(((bf16[64,8,2688]{2,1,0:T(8,128)(2,1)}), bf16[64,8,2688]{2,1,0:T(8,128)(2,1)}, u32[]{:S(2)}, u32[]{:S(2)}) %all-to-all-start.1) | async-done | bytes 2752544 | tf_op jit(solution)/shard_map/all_to_all | solution.py:712
  98.1 2.2 collective-permute-start.2
  101.1 4.2 %collective-permute-done.2.other = bf16[512,2688]{1,0:T(8,128)(2,1)} collective-permute-done((bf16[512,2688]{1,0:T(8,128)(2,1)}, bf16[512,2688]{1,0:T(8,128)(2,1)}, u32[]{:S(2)}, u32[]{:S(2)}) %collective-permute-start.2) | collective-permute-done | bytes 2752544 | tf_op jit(solution)/shard_map/ppermute | solution.py:707
  105.4 32.2 %turn.1 = (bf16[512,384]{1,0:T(8,128)(2,1)}, bf16[512,384]{1,0:T(8,128)(2,1)}, f32[8,384]{1,0:T(8,128)}, bf16[512,2560]{1,0:T(8,128)(2,1)}, bf16[512,2560]{1,0:T(8,128)(2,1)}) custom-call(s32[1]{0:T(128)} %bitcast.core, bf16[512,2688]{1,0:T(8,128)(2,1)} %bitcast.9.own, bf16[512,2688]{1,0:T(8,128)(2,1)} %collective-permute-done.2.other, ...), custom_call_target="tpu_custom_call" | custom-call | flops 6000000000 | bytes 30000000 | tf_op jit(solution)/shard_map/turn/pallas_call | solution.py:646
  137.7 5.1 %collective-permute-done.3 = bf16[512,2560]{1,0:T(8,128)(2,1)S(1)} collective-permute-done((bf16[512,2560]{1,0:T(8,128)(2,1)}, bf16[512,2560]{1,0:T(8,128)(2,1)S(1)}, u32[]{:S(2)}, u32[]{:S(2)}) %collective-permute-start.3) | collective-permute-done | bytes 2621472 | tf_op jit(solution)/shard_map/ppermute | solution.py:707
  142.8 3.6 %add_bitcast_fusion.1 = bf16[64,8,2560]{2,1,0:T(8,128)(2,1)} fusion(bf16[512,2560]{1,0:T(8,128)(2,1)} %get-tuple-element.70, bf16[512,2560]{1,0:T(8,128)(2,1)S(1)} %collective-permute-done.3), kind=kLoop, calls=%fused_computation.3 | loop fusion | flops 1310720 | bytes 7864320 | tf_op jit(solution)/shard_map/reshape | solution.py:716
  146.4 6.9 %all-to-all-start.2 = ((bf16[64,8,2560]{2,1,0:T(8,128)(2,1)}), bf16[64,8,2560]{2,1,0:T(8,128)(2,1)S(1)}, u32[]{:S(2)}, u32[]{:S(2)}) async-start(bf16[64,8,2560]{2,1,0:T(8,128)(2,1)} %add_bitcast_fusion.1), calls=%async_computation.2 | async-start | bytes 5242880 | tf_op jit(solution)/shard_map/all_to_all | solution.py:716
  153.3 23.9 %back.1 = (bf16[512,384]{1,0:T(8,128)(2,1)}, f32[8,384]{1,0:T(8,128)}, bf16[512,2560]{1,0:T(8,128)(2,1)}, bf16[512,2560]{1,0:T(8,128)(2,1)}) custom-call(s32[1]{0:T(128)} %bitcast.core, bf16[512,2688]{1,0:T(8,128)(2,1)} %bitcast.41, bf16[512,2688]{1,0:T(8,128)(2,1)} %collective-permute-done.1.other, bf16[512,384]{1,0:T(8,128)(2,1)} %bitcast.45, ...), custom_call_target="tpu_custom_call" | custom-call | flops 4000000000 | bytes 20000000 | tf_op jit(solution)/shard_map/back/pallas_call | solution.py:659
  177.2 9.5 %all-to-all-done.2 = bf16[64,8,2560]{2,1,0:T(8,128)(2,1)S(1)} async-done(((bf16[64,8,2560]{2,1,0:T(8,128)(2,1)}), bf16[64,8,2560]{2,1,0:T(8,128)(2,1)S(1)}, u32[]{:S(2)}, u32[]{:S(2)}) %all-to-all-start.2) | async-done | bytes 2621472 | tf_op jit(solution)/shard_map/all_to_all | solution.py:716
  186.7 2.1 collective-permute-start.4
  188.9 4.7 %collective-permute-done.4 = bf16[512,2560]{1,0:T(8,128)(2,1)S(1)} collective-permute-done((bf16[512,2560]{1,0:T(8,128)(2,1)}, bf16[512,2560]{1,0:T(8,128)(2,1)S(1)}, u32[]{:S(2)}, u32[]{:S(2)}) %collective-permute-start.4) | collective-permute-done | bytes 2621472 | tf_op jit(solution)/shard_map/ppermute | solution.py:707
  193.6 3.5 %add_bitcast_fusion = bf16[64,8,2560]{2,1,0:T(8,128)(2,1)} fusion(bf16[512,2560]{1,0:T(8,128)(2,1)} %get-tuple-element.69, bf16[512,2560]{1,0:T(8,128)(2,1)S(1)} %collective-permute-done.4), kind=kLoop, calls=%fused_computation.2 | loop fusion | flops 1310720 | bytes 7864320 | tf_op jit(solution)/shard_map/reshape | solution.py:716
  197.1 6.6 %all-to-all-start.3 = ((bf16[64,8,2560]{2,1,0:T(8,128)(2,1)}), bf16[64,8,2560]{2,1,0:T(8,128)(2,1)}, u32[]{:S(2)}, u32[]{:S(2)}) async-start(bf16[64,8,2560]{2,1,0:T(8,128)(2,1)} %add_bitcast_fusion), calls=%async_computation.3 | async-start | bytes 5242880 | tf_op jit(solution)/shard_map/all_to_all | solution.py:716
  213.0 24.3 %all-to-all-done.3 = bf16[64,8,2560]{2,1,0:T(8,128)(2,1)} async-done(((bf16[64,8,2560]{2,1,0:T(8,128)(2,1)}), bf16[64,8,2560]{2,1,0:T(8,128)(2,1)}, u32[]{:S(2)}, u32[]{:S(2)}) %all-to-all-start.3) | async-done | bytes 2621472 | tf_op jit(solution)/shard_map/all_to_all | solution.py:716
  237.2 2.1 convert_reduce_fusion.1
  239.4 1.6 fusion.2
  241.1 2.5 collective-permute-start.8
  (57 shorter events, 20.4 us)
Async XLA Ops:
  0.6 63.0 %copy-start = (bf16[2,2,256,384]{3,2,1,0:T(8,128)(2,1)S(1)}, bf16[2,2,256,384]{3,2,1,0:T(8,128)(2,1)}, u32[]{:S(2)}) copy-start(bf16[2,2,256,384]{3,2,1,0:T(8,128)(2,1)} %param.13) | copy-start | bytes 2359300
  2.3 2.6 %collective-permute-start = (bf16[8,5376]{1,0:T(8,128)(2,1)}, bf16[8,5376]{1,0:T(8,128)(2,1)S(1)}, u32[]{:S(2)}, u32[]{:S(2)}) collective-permute-start(bf16[8,5376]{1,0:T(8,128)(2,1)} %line_up.1), channel_id=1, source_target_pairs={{0,64},{64,0},{1,65},{65,1},{2,66},{66,2},{3,67},{67,3},{4,68},{68... | collective-permute-start | bytes 258056 | tf_op jit(solution)/shard_map/ppermute | solution.py:707
  53.0 3.8 %copy-start.1 = (bf16[64,8,2688]{2,1,0:T(8,128)(2,1)}, bf16[64,8,2688]{2,1,0:T(8,128)(2,1)S(1)}, u32[]{:S(2)}) copy-start(bf16[64,8,2688]{2,1,0:T(8,128)(2,1)S(1)} %all_to_all.20) | copy-start | bytes 8257540
  53.0 11.5 %collective-permute-start.1 = (bf16[512,2688]{1,0:T(8,128)(2,1)S(1)}, bf16[512,2688]{1,0:T(8,128)(2,1)}, u32[]{:S(2)}, u32[]{:S(2)}) collective-permute-start(bf16[512,2688]{1,0:T(8,128)(2,1)S(1)} %bitcast.39), channel_id=1, source_target_pairs={{0,64},{64,0},{1,65},{65,1},{2,66},{66,2},{3,67},{67,3},{4,68},{68... | collective-permute-start | bytes 8257544 | tf_op jit(solution)/shard_map/ppermute | solution.py:707
  56.8 6.2 %copy-start.4 = (bf16[2,2,384]{2,1,0:T(2,128)(2,1)S(1)}, bf16[2,2,384]{2,1,0:T(2,128)(2,1)}, u32[]{:S(2)}) copy-start(bf16[2,2,384]{2,1,0:T(2,128)(2,1)} %param.14) | copy-start | bytes 9220
  56.8 41.3 %all-to-all-start.1 = ((bf16[64,8,2688]{2,1,0:T(8,128)(2,1)}), bf16[64,8,2688]{2,1,0:T(8,128)(2,1)}, u32[]{:S(2)}, u32[]{:S(2)}) async-start(bf16[64,8,2688]{2,1,0:T(8,128)(2,1)} %broadcast_in_dim.44), calls=%async_computation.1 | async-start | bytes 5505024 | tf_op jit(solution)/shard_map/all_to_all | solution.py:712
  64.5 35.9 %copy-start.3 = (bf16[2,2,256,384]{3,2,1,0:T(8,128)(2,1)S(1)}, bf16[2,2,256,384]{3,2,1,0:T(8,128)(2,1)}, u32[]{:S(2)}) copy-start(bf16[2,2,256,384]{3,2,1,0:T(8,128)(2,1)} %param.15) | copy-start | bytes 2359300
  98.1 7.3 %collective-permute-start.2 = (bf16[512,2688]{1,0:T(8,128)(2,1)}, bf16[512,2688]{1,0:T(8,128)(2,1)}, u32[]{:S(2)}, u32[]{:S(2)}) collective-permute-start(bf16[512,2688]{1,0:T(8,128)(2,1)} %bitcast.9.own), channel_id=1, source_target_pairs={{0,64},{64,0},{1,65},{65,1},{2,66},{66,2},{3,67},{67,3},{4,68},{68... | collective-permute-start | bytes 8257544 | tf_op jit(solution)/shard_map/ppermute | solution.py:707
  137.6 5.2 %collective-permute-start.3 = (bf16[512,2560]{1,0:T(8,128)(2,1)}, bf16[512,2560]{1,0:T(8,128)(2,1)S(1)}, u32[]{:S(2)}, u32[]{:S(2)}) collective-permute-start(bf16[512,2560]{1,0:T(8,128)(2,1)} %get-tuple-element.71), channel_id=1, source_target_pairs={{0,64},{64,0},{1,65},{65,1},{2,66},{66,2},{3,67},{67,3},{4,68},{68... | collective-permute-start | bytes 7864328 | tf_op jit(solution)/shard_map/ppermute | solution.py:707
  146.4 40.4 %all-to-all-start.2 = ((bf16[64,8,2560]{2,1,0:T(8,128)(2,1)}), bf16[64,8,2560]{2,1,0:T(8,128)(2,1)S(1)}, u32[]{:S(2)}, u32[]{:S(2)}) async-start(bf16[64,8,2560]{2,1,0:T(8,128)(2,1)} %add_bitcast_fusion.1), calls=%async_computation.2 | async-start | bytes 5242880 | tf_op jit(solution)/shard_map/all_to_all | solution.py:716
  186.7 6.9 %collective-permute-start.4 = (bf16[512,2560]{1,0:T(8,128)(2,1)}, bf16[512,2560]{1,0:T(8,128)(2,1)S(1)}, u32[]{:S(2)}, u32[]{:S(2)}) collective-permute-start(bf16[512,2560]{1,0:T(8,128)(2,1)} %get-tuple-element.73), channel_id=1, source_target_pairs={{0,64},{64,0},{1,65},{65,1},{2,66},{66,2},{3,67},{67,3},{4,68},{68... | collective-permute-start | bytes 7864328 | tf_op jit(solution)/shard_map/ppermute | solution.py:707
  197.1 40.1 %all-to-all-start.3 = ((bf16[64,8,2560]{2,1,0:T(8,128)(2,1)}), bf16[64,8,2560]{2,1,0:T(8,128)(2,1)}, u32[]{:S(2)}, u32[]{:S(2)}) async-start(bf16[64,8,2560]{2,1,0:T(8,128)(2,1)} %add_bitcast_fusion), calls=%async_computation.3 | async-start | bytes 5242880 | tf_op jit(solution)/shard_map/all_to_all | solution.py:716
  205.0 4.7 %collective-permute-start.6 = (bf16[512,384]{1,0:T(8,128)(2,1)S(1)}, bf16[512,384]{1,0:T(8,128)(2,1)S(1)}, u32[]{:S(2)}, u32[]{:S(2)}) collective-permute-start(bf16[512,384]{1,0:T(8,128)(2,1)S(1)} %get-tuple-element.86), channel_id=1, source_target_pairs={{0,64},{64,0},{1,65},{65,1},{2,66},{66,2},{3,67},{67,3},{4,68},{68... | collective-permute-start | bytes 1179656 | tf_op jit(solution)/shard_map/ppermute | solution.py:707
  206.9 3.8 %collective-permute-start.5 = (bf16[512,384]{1,0:T(8,128)(2,1)S(1)}, bf16[512,384]{1,0:T(8,128)(2,1)S(1)}, u32[]{:S(2)}, u32[]{:S(2)}) collective-permute-start(bf16[512,384]{1,0:T(8,128)(2,1)S(1)} %get-tuple-element.88), channel_id=1, source_target_pairs={{0,64},{64,0},{1,65},{65,1},{2,66},{66,2},{3,67},{67,3},{4,68},{68... | collective-permute-start | bytes 1179656 | tf_op jit(solution)/shard_map/ppermute | solution.py:707
  207.7 1.3 collective-permute-start.7
  213.0 28.0 %copy-start.2 = (f32[16,1152]{1,0:T(8,128)S(1)}, f32[16,1152]{1,0:T(8,128)}, u32[]{:S(2)}) copy-start(f32[16,1152]{1,0:T(8,128)} %fusion) | copy-start | bytes 221188
  241.1 3.5 %collective-permute-start.8 = (f32[8,4864]{1,0:T(8,128)S(1)}, f32[8,4864]{1,0:T(8,128)S(1)}, u32[]{:S(2)}, u32[]{:S(2)}) collective-permute-start(f32[8,4864]{1,0:T(8,128)S(1)} %fusion.6), channel_id=1, source_target_pairs={{0,64},{64,0},{1,65},{65,1},{2,66},{66,2},{3,67},{67,3},{4,68},{68... | collective-permute-start | bytes 466952 | tf_op jit(solution)/shard_map/ppermute | solution.py:707
